TPU v7x, 32 devices: a whole 2x2x4 slice. The times are simulated.
32 devices in a mesh: narrow: 2 (over y), wide: 16 (over z, x, core).
Axes of the slice: x: 2, y: 2, z: 4, core: 2. Of those that a mesh axis runs over, the one named last changes fastest.
Arguments:
- hidden: bfloat16 [2, 48, 208, 1152], P('narrow', 'wide'), may hold values from -6 to 6
- cotangent: bfloat16 [2, 48, 208, 1152], P('narrow', 'wide'), may hold values from -6 to 6
- text: bfloat16 [2, 128, 4096], P('narrow'), may hold values from -6 to 6
- timesteps: int32 [2], P('narrow'), may hold values from 0 to 999
- seg_ids: int32 [2, 48], P('narrow'), may hold values from 0 to 5, never falling along the last dimension, each value on 1 to 16 neighbouring positions
- text_len: int32 [2], P('narrow'), may hold values from 32 to 128, as said below
- ada_weight: bfloat16 [1152, 10368], P('wide'), may hold values from -0.1875 to 0.1875
- text_weight: bfloat16 [4096, 1152], P('wide'), may hold values from -0.09375 to 0.09375
- kv_weight: bfloat16 [1152, 2304], P('wide'), may hold values from -0.1875 to 0.1875
- qkv_weight: bfloat16 [1152, 3456], P('wide'), may hold values from -0.1875 to 0.1875
- out_weight: bfloat16 [1152, 1152], P('wide'), may hold values from -1.5 to 1.5
- cross_q_weight: bfloat16 [1152, 1152], P('wide'), may hold values from -0.1875 to 0.1875
- cross_out_weight: bfloat16 [1152, 1152], P('wide'), may hold values from -1 to 1
- temp_qkv_weight: bfloat16 [1152, 3456], P('wide'), may hold values from -0.1875 to 0.1875
- temp_out_weight: bfloat16 [1152, 1152], P('wide'), may hold values from -0.25 to 0.25
- up_weight: bfloat16 [1152, 4608], P('wide'), may hold values from -0.1875 to 0.1875
- down_weight: bfloat16 [4608, 1152], P('wide'), may hold values from -0.09375 to 0.09375
- cross_gain: float32 [1152], replicated, may hold values from 0.25 to 1.75
Outputs:
- block_out: bfloat16 [2, 48, 208, 1152], P('narrow', 'wide')
- grad_hidden: bfloat16 [2, 48, 208, 1152], P('narrow', 'wide')
- grad_ada: float32 [1152, 10368], P('wide')
- grad_text: float32 [4096, 1152], P('wide')
- grad_kv: float32 [1152, 2304], P('wide')
- grad_qkv: float32 [1152, 3456], P('wide')
- grad_out: float32 [1152, 1152], P('wide')
- grad_cross_q: float32 [1152, 1152], P('wide')
- grad_cross_out: float32 [1152, 1152], P('wide')
- grad_temp_qkv: float32 [1152, 3456], P('wide')
- grad_temp_out: float32 [1152, 1152], P('wide')
- grad_up: float32 [1152, 4608], P('wide')
- grad_down: float32 [4608, 1152], P('wide')
- grad_gain: float32 [1152], replicated
Inputs may be any that keep to these rules, and one draw needn't show every extreme that they name: `seg_ids`: clip numbers never fall along the frames of a bucket; a clip spans 1 to 16 frames, and some clip spans exactly 16. `text_len`: in every draw some bucket uses all 128 text tokens.
All inputs are finite; a program needn't handle non-finite values.
Results may differ from a plain program's by a relative error of at most 0.024.
Values may be sent and summed in bfloat16 or wider, within the bound.
A program may use at most 384 MiB of HBM per device.

v0:
```python
import math

import jax
import jax.numpy as jnp
from jax import lax
from jax.sharding import PartitionSpec as P

HEADS = 16


def shortened(x):

    def short(part):
        return part.astype(jnp.bfloat16) if part.dtype == jnp.float32 else part

    return jax.tree.map(short, x)


def with_halo(block, sides, width):
    for axis, dim in sides:
        count = lax.axis_size(axis)
        forward = [(i, i + 1) for i in range(count - 1)]
        backward = [(target, source) for source, target in forward]
        low = lax.ppermute(
            lax.slice_in_dim(block, block.shape[dim] - width, None, axis=dim), axis, forward
        )
        high = lax.ppermute(lax.slice_in_dim(block, 0, width, axis=dim), axis, backward)
        block = jnp.concatenate([low, block, high], axis=dim)
    return block


def layer_norm(values):
    centred = values - jnp.mean(values, -1, keepdims=True)
    variance = jnp.mean(centred * centred, -1, keepdims=True)
    return centred * lax.rsqrt(variance + 1e-06)


def modulate(values, shift_vec, scale_vec):
    return layer_norm(values) * (1.0 + scale_vec) + shift_vec


def scaled_norm(values, gain_vec):
    return layer_norm(values) * gain_vec


def time_embed(steps, model_width):
    half_width = model_width // 2
    freqs = jnp.exp(-math.log(10000.0) * jnp.arange(half_width, dtype=jnp.float32) / half_width)
    angles = steps.astype(jnp.float32)[:, None] * freqs[None, :]
    return jnp.concatenate([jnp.cos(angles), jnp.sin(angles)], -1)


def project(operand, weights):
    return jnp.dot(operand, weights, preferred_element_type=jnp.float32)


def project_back(gradient, weights):
    return lax.dot_general(
        gradient, weights, (((1,), (1,)), ((), ())), preferred_element_type=jnp.float32
    )


def project_rows(operand, gradient):
    return lax.dot_general(
        operand, gradient, (((0,), (0,)), ((), ())), preferred_element_type=jnp.float32
    )


def fetch_rows(shards):
    return jax.tree.map(
        lambda part, own: part.astype(own.dtype),
        lax.all_gather(shortened(shards), "wide", axis=0, tiled=True),
        shards,
    )


def back_weights(shards):
    return jax.tree.map(
        lambda part, own: part.astype(own.dtype),
        lax.all_gather(shortened(shards), "wide", axis=0, tiled=True),
        shards,
    )


def grad_rows(operand, gradient):
    return lax.psum_scatter(
        project_rows(operand, gradient), "wide", scatter_dimension=0, tiled=True
    )


def body(
    hidden,
    cotangent,
    text,
    timesteps,
    seg_ids,
    text_len,
    ada_weight,
    text_weight,
    kv_weight,
    qkv_weight,
    out_weight,
    cross_q_weight,
    cross_out_weight,
    temp_qkv_weight,
    temp_out_weight,
    up_weight,
    down_weight,
    cross_gain,
):
    frames = hidden.shape[1]
    patches = hidden.shape[2]
    model_width = hidden.shape[3]
    head_count = HEADS
    head_size = model_width // head_count
    row_count = frames * patches
    text_count = text.shape[1]
    position = lax.axis_index("wide")
    rows_model = ada_weight.shape[0]
    rows_text = text_weight.shape[0]
    score_scale = head_size ** (-0.5)
    signal = jax.nn.silu(time_embed(timesteps, model_width)[0]).astype(jnp.bfloat16)
    signal_rows = lax.dynamic_slice_in_dim(signal, position * rows_model, rows_model)
    mod_part = jnp.dot(signal_rows, ada_weight, preferred_element_type=jnp.float32)
    prompt = text[0]
    prompt_rows = lax.dynamic_slice_in_dim(prompt, position * rows_text, rows_text, 1)
    text_part = project(prompt_rows, text_weight)
    modulation, text_sum = lax.psum((mod_part, text_part), "wide")
    modulation = modulation.reshape(9, model_width)
    shift_a, scale_a, gate_a = (modulation[0], modulation[1], modulation[2])
    shift_t, scale_t, gate_t = (modulation[3], modulation[4], modulation[5])
    shift_m, scale_m, gate_m = (modulation[6], modulation[7], modulation[8])
    prompt_low = text_sum.astype(jnp.bfloat16)
    prompt_cols = lax.dynamic_slice_in_dim(prompt_low, position * rows_model, rows_model, 1)
    kv_part = project(prompt_cols, kv_weight)
    text_kv = lax.psum(kv_part, "wide").astype(jnp.bfloat16)
    keys_c = text_kv[:, :model_width].reshape(text_count, head_count, head_size)
    values_c = text_kv[:, model_width:].reshape(text_count, head_count, head_size)
    valid = jnp.arange(text_count) < text_len[0]
    start = hidden[0].reshape(row_count, model_width).astype(jnp.float32)
    full_qkv, full_out = fetch_rows((qkv_weight, out_weight))
    normed_a = modulate(start, shift_a, scale_a).astype(jnp.bfloat16)
    qkv_a = (
        project(normed_a, full_qkv)
        .astype(jnp.bfloat16)
        .reshape(frames, patches, 3, head_count, head_size)
    )
    query_a, keys_a, values_a = (qkv_a[:, :, 0], qkv_a[:, :, 1], qkv_a[:, :, 2])
    scores_a = (
        jnp.einsum("fphd,fqhd->fhpq", query_a, keys_a, preferred_element_type=jnp.float32)
        * score_scale
    )
    total_a = jax.nn.logsumexp(scores_a, axis=-1, keepdims=True)
    probs_a = jnp.exp(scores_a - total_a).astype(jnp.bfloat16)
    attn_a = jnp.einsum("fhpq,fqhd->fphd", probs_a, values_a, preferred_element_type=jnp.float32)
    attn_a = attn_a.astype(jnp.bfloat16).reshape(row_count, model_width)
    branch_a = project(attn_a, full_out)
    first = start + gate_a * branch_a
    full_cross_q, full_cross_out = fetch_rows((cross_q_weight, cross_out_weight))
    normed_c = scaled_norm(first, cross_gain).astype(jnp.bfloat16)
    query_c = (
        project(normed_c, full_cross_q)
        .astype(jnp.bfloat16)
        .reshape(row_count, head_count, head_size)
    )
    scores_c = (
        jnp.einsum("nhd,lhd->hnl", query_c, keys_c, preferred_element_type=jnp.float32)
        * score_scale
    )
    scores_c = jnp.where(valid, scores_c, -1e30)
    total_c = jax.nn.logsumexp(scores_c, axis=-1, keepdims=True)
    probs_c = jnp.exp(scores_c - total_c).astype(jnp.bfloat16)
    attn_c = jnp.einsum("hnl,lhd->nhd", probs_c, values_c, preferred_element_type=jnp.float32)
    attn_c = attn_c.astype(jnp.bfloat16).reshape(row_count, model_width)
    branch_c = project(attn_c, full_cross_out)
    second = first + branch_c
    full_temp_qkv, full_temp_out = fetch_rows((temp_qkv_weight, temp_out_weight))
    normed_t = modulate(second, shift_t, scale_t).astype(jnp.bfloat16)
    qkv_t = (
        project(normed_t, full_temp_qkv)
        .astype(jnp.bfloat16)
        .reshape(frames, patches, 3 * model_width)
    )
    query_t = qkv_t[:, :, :model_width].reshape(frames, patches, head_count, head_size)
    nearby = with_halo(qkv_t[:, :, model_width:], (("wide", 0),), 2)
    clip_pad = jnp.pad(seg_ids[0], 2, constant_values=-1)
    clip_local = lax.dynamic_slice_in_dim(clip_pad, position * frames, frames + 4)
    own_clip = clip_local[2 : frames + 2]
    allowed = jnp.stack(
        [clip_local[offset : offset + frames] == own_clip for offset in range(5)], -1
    )

    def window_keys(offset):
        return nearby[offset : offset + frames, :, :model_width].reshape(
            frames, patches, head_count, head_size
        )

    def window_values(offset):
        return nearby[offset : offset + frames, :, model_width:].reshape(
            frames, patches, head_count, head_size
        )

    def temporal_probs():
        score_list = [
            jnp.einsum(
                "fphd,fphd->fph", query_t, window_keys(offset), preferred_element_type=jnp.float32
            )
            * score_scale
            for offset in range(5)
        ]
        scores_t = jnp.where(allowed[:, None, None, :], jnp.stack(score_list, -1), -1e30)
        return jax.nn.softmax(scores_t, -1)

    probs_t = temporal_probs()
    probs_low_t = probs_t.astype(jnp.bfloat16)
    attn_t = jnp.zeros((frames, patches, head_count, head_size), jnp.float32)
    for offset in range(5):
        attn_t = attn_t + jnp.einsum(
            "fph,fphd->fphd",
            probs_low_t[..., offset],
            window_values(offset),
            preferred_element_type=jnp.float32,
        )
    attn_t = attn_t.astype(jnp.bfloat16).reshape(row_count, model_width)
    branch_t = project(attn_t, full_temp_out)
    third = second + gate_t * branch_t
    (full_up,) = fetch_rows((up_weight,))
    normed_m = modulate(third, shift_m, scale_m).astype(jnp.bfloat16)
    hidden_m = project(normed_m, full_up)
    act = jax.nn.gelu(hidden_m, approximate=True).astype(jnp.bfloat16)
    (full_down,) = fetch_rows((down_weight,))
    branch_m = project(act, full_down)
    result = third + gate_m * branch_m
    block_out = result.astype(jnp.bfloat16).reshape(1, frames, patches, model_width)
    gradient = cotangent[0].reshape(row_count, model_width).astype(jnp.float32)
    d_gate_m = jnp.sum(gradient * branch_m, 0)
    d_branch_m = (gate_m * gradient).astype(jnp.bfloat16)
    (back_down,) = back_weights((down_weight,))
    grad_down = grad_rows(act, d_branch_m)
    d_act = project_back(d_branch_m, back_down)
    unused_gelu, gelu_back = jax.vjp(lambda values: jax.nn.gelu(values, approximate=True), hidden_m)
    d_hidden_m = gelu_back(d_act)[0].astype(jnp.bfloat16)
    (back_up,) = back_weights((up_weight,))
    grad_up = grad_rows(normed_m, d_hidden_m)
    d_normed_m = project_back(d_hidden_m, back_up)
    unused_mlp, mlp_back = jax.vjp(modulate, third, shift_m, scale_m)
    d_third, d_shift_m, d_scale_m = mlp_back(d_normed_m)
    gradient = gradient + d_third
    d_gate_t = jnp.sum(gradient * branch_t, 0)
    d_branch_t = (gate_t * gradient).astype(jnp.bfloat16)
    back_temp_qkv, back_temp_out = back_weights((temp_qkv_weight, temp_out_weight))
    grad_temp_out = grad_rows(attn_t, d_branch_t)
    d_attn_t = (
        project_back(d_branch_t, back_temp_out)
        .astype(jnp.bfloat16)
        .reshape(frames, patches, head_count, head_size)
    )
    d_prob_list = [
        jnp.einsum(
            "fphd,fphd->fph", d_attn_t, window_values(offset), preferred_element_type=jnp.float32
        )
        for offset in range(5)
    ]
    d_probs_t = jnp.stack(d_prob_list, -1)
    inner_t = jnp.sum(probs_t * d_probs_t, -1, keepdims=True)
    d_scores_t = probs_t * (d_probs_t - inner_t) * score_scale
    d_query_t = jnp.zeros((frames, patches, head_count, head_size), jnp.float32)
    d_nearby = jnp.zeros((frames + 4, patches, 2 * model_width), jnp.float32)
    for offset in range(5):
        d_query_t = d_query_t + d_scores_t[..., offset, None] * window_keys(offset)
        d_keys_w = (d_scores_t[..., offset, None] * query_t).reshape(frames, patches, model_width)
        d_values_w = (
            probs_low_t[..., offset, None].astype(jnp.float32) * d_attn_t.astype(jnp.float32)
        ).reshape(frames, patches, model_width)
        piece = jnp.concatenate([d_keys_w, d_values_w], -1)
        d_nearby = d_nearby + jnp.pad(piece, ((offset, 4 - offset), (0, 0), (0, 0)))
    edge_grads = jnp.concatenate([d_nearby[:2], d_nearby[frames + 2 :]], 0)
    arrived = with_halo(edge_grads.astype(jnp.bfloat16), (("wide", 0),), 2).astype(edge_grads.dtype)
    d_kv_t = d_nearby[2 : frames + 2]
    d_kv_t = d_kv_t + jnp.pad(arrived[:2], ((0, frames - 2), (0, 0), (0, 0)))
    d_kv_t = d_kv_t + jnp.pad(arrived[6:], ((frames - 2, 0), (0, 0), (0, 0)))
    d_qkv_t = jnp.concatenate([d_query_t.reshape(frames, patches, model_width), d_kv_t], -1)
    d_qkv_t = d_qkv_t.reshape(row_count, 3 * model_width).astype(jnp.bfloat16)
    grad_temp_qkv = grad_rows(normed_t, d_qkv_t)
    d_normed_t = project_back(d_qkv_t, back_temp_qkv)
    unused_temp, temp_back = jax.vjp(modulate, second, shift_t, scale_t)
    d_second, d_shift_t, d_scale_t = temp_back(d_normed_t)
    gradient = gradient + d_second
    d_branch_c = gradient.astype(jnp.bfloat16)
    back_cross_q, back_cross_out = back_weights((cross_q_weight, cross_out_weight))
    grad_cross_out = grad_rows(attn_c, d_branch_c)
    d_attn_c = (
        project_back(d_branch_c, back_cross_out)
        .astype(jnp.bfloat16)
        .reshape(row_count, head_count, head_size)
    )
    probs_full_c = jnp.exp(scores_c - total_c)
    d_probs_c = jnp.einsum("nhd,lhd->hnl", d_attn_c, values_c, preferred_element_type=jnp.float32)
    inner_c = jnp.sum(probs_full_c * d_probs_c, -1, keepdims=True)
    d_scores_c = (probs_full_c * (d_probs_c - inner_c)).astype(jnp.bfloat16)
    d_query_c = (
        jnp.einsum("hnl,lhd->nhd", d_scores_c, keys_c, preferred_element_type=jnp.float32)
        * score_scale
    )
    d_query_c = d_query_c.reshape(row_count, model_width).astype(jnp.bfloat16)
    d_keys_c = (
        jnp.einsum("hnl,nhd->lhd", d_scores_c, query_c, preferred_element_type=jnp.float32)
        * score_scale
    )
    d_values_c = jnp.einsum("hnl,nhd->lhd", probs_c, d_attn_c, preferred_element_type=jnp.float32)
    d_kv_part = jnp.concatenate(
        [d_keys_c.reshape(text_count, model_width), d_values_c.reshape(text_count, model_width)], -1
    )
    grad_cross_q = grad_rows(normed_c, d_query_c)
    d_normed_c = project_back(d_query_c, back_cross_q)
    unused_cross, cross_back = jax.vjp(scaled_norm, first, cross_gain)
    d_first, d_gain_part = cross_back(d_normed_c)
    gradient = gradient + d_first
    d_gate_a = jnp.sum(gradient * branch_a, 0)
    d_branch_a = (gate_a * gradient).astype(jnp.bfloat16)
    back_qkv, back_out = back_weights((qkv_weight, out_weight))
    grad_out = grad_rows(attn_a, d_branch_a)
    d_attn_a = (
        project_back(d_branch_a, back_out)
        .astype(jnp.bfloat16)
        .reshape(frames, patches, head_count, head_size)
    )
    probs_full_a = jnp.exp(scores_a - total_a)
    d_probs_a = jnp.einsum(
        "fphd,fqhd->fhpq", d_attn_a, values_a, preferred_element_type=jnp.float32
    )
    inner_a = jnp.sum(probs_full_a * d_probs_a, -1, keepdims=True)
    d_scores_a = (probs_full_a * (d_probs_a - inner_a)).astype(jnp.bfloat16)
    d_query_a = (
        jnp.einsum("fhpq,fqhd->fphd", d_scores_a, keys_a, preferred_element_type=jnp.float32)
        * score_scale
    )
    d_keys_a = (
        jnp.einsum("fhpq,fphd->fqhd", d_scores_a, query_a, preferred_element_type=jnp.float32)
        * score_scale
    )
    d_values_a = jnp.einsum(
        "fhpq,fphd->fqhd", probs_a, d_attn_a, preferred_element_type=jnp.float32
    )
    d_qkv_a = (
        jnp.stack([d_query_a, d_keys_a, d_values_a], 2)
        .reshape(row_count, 3 * model_width)
        .astype(jnp.bfloat16)
    )
    grad_qkv = grad_rows(normed_a, d_qkv_a)
    d_normed_a = project_back(d_qkv_a, back_qkv)
    unused_spatial, spatial_back = jax.vjp(modulate, start, shift_a, scale_a)
    d_start, d_shift_a, d_scale_a = spatial_back(d_normed_a)
    grad_hidden = (gradient + d_start).astype(jnp.bfloat16).reshape(1, frames, patches, model_width)
    d_modulation = jnp.concatenate(
        [
            d_shift_a,
            d_scale_a,
            d_gate_a,
            d_shift_t,
            d_scale_t,
            d_gate_t,
            d_shift_m,
            d_scale_m,
            d_gate_m,
        ]
    )
    d_modulation, d_gain_wide, d_text_kv = lax.psum((d_modulation, d_gain_part, d_kv_part), "wide")
    d_text_kv_low = d_text_kv.astype(jnp.bfloat16)
    grad_kv_part = project_rows(prompt_cols, d_text_kv_low)
    d_prompt_cols = project_back(d_text_kv_low, kv_weight).astype(jnp.bfloat16)
    d_prompt = lax.all_gather(d_prompt_cols, "wide", axis=1, tiled=True)
    grad_text_part = project_rows(prompt_rows, d_prompt)
    grad_ada_part = signal_rows.astype(jnp.float32)[:, None] * d_modulation[None, :]
    (
        grad_ada,
        grad_text,
        grad_kv,
        grad_qkv,
        grad_out,
        grad_cross_q,
        grad_cross_out,
        grad_temp_qkv,
        grad_temp_out,
        grad_up,
        grad_down,
        grad_gain,
    ) = (
        lax.psum(grad_ada_part.astype(jnp.bfloat16), "narrow").astype(jnp.float32),
        lax.psum(grad_text_part.astype(jnp.bfloat16), "narrow").astype(jnp.float32),
        lax.psum(grad_kv_part.astype(jnp.bfloat16), "narrow").astype(jnp.float32),
        lax.psum(grad_qkv.astype(jnp.bfloat16), "narrow").astype(jnp.float32),
        lax.psum(grad_out.astype(jnp.bfloat16), "narrow").astype(jnp.float32),
        lax.psum(grad_cross_q.astype(jnp.bfloat16), "narrow").astype(jnp.float32),
        lax.psum(grad_cross_out.astype(jnp.bfloat16), "narrow").astype(jnp.float32),
        lax.psum(grad_temp_qkv.astype(jnp.bfloat16), "narrow").astype(jnp.float32),
        lax.psum(grad_temp_out.astype(jnp.bfloat16), "narrow").astype(jnp.float32),
        lax.psum(grad_up.astype(jnp.bfloat16), "narrow").astype(jnp.float32),
        lax.psum(grad_down.astype(jnp.bfloat16), "narrow").astype(jnp.float32),
        lax.psum(d_gain_wide.astype(jnp.bfloat16), "narrow").astype(jnp.float32),
    )
    return (
        block_out,
        grad_hidden,
        grad_ada,
        grad_text,
        grad_kv,
        grad_qkv,
        grad_out,
        grad_cross_q,
        grad_cross_out,
        grad_temp_qkv,
        grad_temp_out,
        grad_up,
        grad_down,
        grad_gain,
    )


def solution(mesh):
    return jax.shard_map(
        body,
        mesh=mesh,
        in_specs=(
            P("narrow", "wide", None, None),
            P("narrow", "wide", None, None),
            P("narrow", None, None),
            P("narrow"),
            P("narrow", None),
            P("narrow"),
            P("wide", None),
            P("wide", None),
            P("wide", None),
            P("wide", None),
            P("wide", None),
            P("wide", None),
            P("wide", None),
            P("wide", None),
            P("wide", None),
            P("wide", None),
            P("wide", None),
            P(),
        ),
        out_specs=(
            P("narrow", "wide", None, None),
            P("narrow", "wide", None, None),
            P("wide", None),
            P("wide", None),
            P("wide", None),
            P("wide", None),
            P("wide", None),
            P("wide", None),
            P("wide", None),
            P("wide", None),
            P("wide", None),
            P("wide", None),
            P("wide", None),
            P(),
        ),
        check_vma=False,
    )
```

profile of v0, /device:TPU:0, one launch (start us, length us, event | category | flops | bytes accessed | tf_op | source)
XLA Modules:
  0.0 1990.2 jit_solution(10481011241025722994)
XLA Ops:
  17.7 78.1 %all-reduce.22 = bf16[128,1152]{0,1:T(8,128)(2,1)} all-reduce(f32[128,1152]{0,1:T(8,128)S(1)} %fusion.78), channel_id=1, replica_groups=mesh['narrow'=2,'wide'=16] {'wide'}, use_global_device_ids=true, to_apply=%region_5.6 | all-reduce | flops 147456 | bytes 884736 | tf_op jit(solution)/shard_map/psum | solution.py:128
  99.2 79.8 %all-reduce.23 = (f32[10368]{0:T(1024)S(1)}, bf16[128,2304]{1,0:T(8,128)(2,1)S(1)}) all-reduce(f32[10368]{0:T(1024)S(1)} %convolution_reduce_fusion, f32[128,2304]{1,0:T(8,128)} %fusion.90), channel_id=1, replica_groups=mesh['narrow'=2,'wide'=16] {'wide'}, use_global_device_ids=true, to_apply=%region_0.1 | all-reduce | flops 305280 | bytes 1852416 | tf_op jit(solution)/shard_map/psum | solution.py:128
  192.1 16.2 reshape.524
  279.2 26.0 %all-gather.17.cloned.1.call-done = bf16[1152,3456]{1,0:T(8,128)(2,1)} async-done(((bf16[72,3456]{1,0:T(8,128)(2,1)}), bf16[1152,3456]{1,0:T(8,128)(2,1)}) %all-gather.17.cloned.1.call-update) | async-done | bytes 7962640 | tf_op jit(solution)/shard_map/all_gather | solution.py:72
  389.2 66.9 %all-gather.23.cloned.1.call-done = bf16[4608,1152]{1,0:T(8,128)(2,1)} async-done(((bf16[288,1152]{1,0:T(8,128)(2,1)}), bf16[4608,1152]{1,0:T(8,128)(2,1)}) %all-gather.23.cloned.1.call-update) | async-done | bytes 10616848 | tf_op jit(solution)/shard_map/all_gather | solution.py:72
  456.1 13.3 fusion.131
  469.4 75.9 %all-gather.21.cloned.1.call-done = bf16[1152,4608]{1,0:T(8,128)(2,1)} async-done(((bf16[72,4608]{1,0:T(8,128)(2,1)}), bf16[1152,4608]{1,0:T(8,128)(2,1)}) %all-gather.21.cloned.1.call-update) | async-done | bytes 10616848 | tf_op jit(solution)/shard_map/all_gather | solution.py:72
  545.3 23.7 %fusion.13 = (bf16[624,4608]{1,0:T(8,128)(2,1)}, f32[624,4608]{1,0:T(8,128)}) fusion(f32[624,4608]{1,0:T(8,128)} %fusion.131, bf16[1152,4608]{1,0:T(8,128)(2,1)} %all-gather.21.cloned.1.call-done, f32[624,1152]{1,0:T(8,128)} %copy-done.49, f32[1152]{0:T(1024)S(1)} %get-tuple-element.115, f32[1152]{0:T(1024)S(1)} %get-tuple-element.116, ...), kind=kOutput, calls=%fused_computation.28 | convolution fusion | flops 6686005248 | bytes 42260352 | tf_op jit(solution)/shard_map/dot_general | solution.py:54
  569.1 15.7 multiply_reduce_fusion.4
  584.8 21.1 %fusion.40 = (f32[1152]{0:T(1024)}, bf16[624,1152]{1,0:T(8,128)(2,1)}, f32[624]{0:T(1024)S(1)}, f32[624,1152]{1,0:T(8,128)}) fusion(bf16[1,3,208,1152]{3,2,1,0:T(8,128)(2,1)S(1)} %copy-done.57, f32[624,1152]{1,0:T(8,128)S(1)} %copy-done.50, f32[1152]{0:T(1024)S(1)} %get-tuple-element.114, f32[624]{0:T(1024)S(1)} %multiply_multiply_fusion.6, ...), kind=kOutput, calls=%fused_computation.130 | convolution fusion | flops 6660125184 | bytes 33643776 | tf_op jit(solution)/shard_map/dot_general | solution.py:54
  653.6 19.2 fusion.119
  723.6 12.5 multiply_reduce_fusion.6
  787.8 12.5 fusion.41
  829.0 13.2 multiply_convert_fusion.1
  868.0 14.5 convert_element_type.341
  895.8 17.4 fusion.115
  913.9 15.8 fusion.113
  950.7 99.1 %all-reduce.24 = (f32[10368]{0:T(1024)S(1)}, bf16[128,2304]{0,1:T(8,128)(2,1)S(1)}, bf16[1152]{0:T(1024)(128)(2,1)S(1)}) all-reduce(f32[10368]{0:T(1024)S(1)} %constant_dynamic-update-slice_fusion.1, f32[128,2304]{0,1:T(8,128)S(1)} %pad_maximum_fusion.8, f32[1152]{0:T(1024)S(1)} %get-tuple-element.14), channel_id=1, replica_groups=mesh['narrow'=2,'wide'=16] {'wide'}, use_global_device_ids=true, to_apply=%region_37.38 | all-reduce | flops 306432 | bytes 1859328 | tf_op jit(solution)/shard_map/psum | solution.py:368
  1051.0 17.9 all_gather.43
  1081.0 137.9 %reduce-scatter.33.cloned.1.call-done = f32[72,3456]{1,0:T(8,128)} async-done(((f32[1152,3456]{1,0:T(8,128)}), f32[72,3456]{1,0:T(8,128)}) %reduce-scatter.33.cloned.1.call-update) | async-done | bytes 995344
  1220.9 173.0 %reduce-scatter.25.cloned.1.call-done = f32[72,3456]{1,0:T(8,128)} async-done(((f32[1152,3456]{1,0:T(8,128)}), f32[72,3456]{1,0:T(8,128)}) %reduce-scatter.25.cloned.1.call-update) | async-done | bytes 995344
  1395.9 213.8 %reduce-scatter.23.cloned.1.call-done = f32[288,1152]{1,0:T(8,128)} async-done(((f32[4608,1152]{1,0:T(8,128)}), f32[288,1152]{1,0:T(8,128)}) %reduce-scatter.23.cloned.1.call-update) | async-done | bytes 1327120 | tf_op jit(solution)/shard_map/reduce_scatter | solution.py:86
  1611.9 214.2 %reduce-scatter.21.cloned.1.call-done = f32[72,4608]{1,0:T(8,128)} async-done(((f32[1152,4608]{1,0:T(8,128)}), f32[72,4608]{1,0:T(8,128)}) %reduce-scatter.21.cloned.1.call-update) | async-done | bytes 1327120 | tf_op jit(solution)/shard_map/reduce_scatter | solution.py:86
  1844.8 122.4 %all-reduce.21.cloned.1.call-done = (bf16[72,10368]{1,0:T(8,128)(2,1)}, bf16[256,1152]{1,0:T(8,128)(2,1)}, bf16[72,2304]{1,0:T(8,128)(2,1)}, bf16[72,3456]{1,0:T...) async-done(((bf16[72,10368]{1,0:T(8,128)(2,1)}, ...) | async-done | bytes 5400592 | tf_op jit(solution)/shard_map/psum | solution.py:389
  (511 shorter events, 472.6 us)
Async XLA Ops:
  7.2 173.8 %all-gather.9.cloned.1.call-start = ((), (), s32[]{:S(2)}) async-start(), calls=%async_computation.8 | async-start | bytes 8460288 | tf_op jit(solution)/shard_map/all_gather | solution.py:72
  7.9 237.4 %all-gather.11.cloned.1.call-start = ((), (), s32[]{:S(2)}) async-start(), calls=%async_computation.9 | async-start | bytes 2820096 | tf_op jit(solution)/shard_map/all_gather | solution.py:72
  8.7 248.1 %all-gather.13.cloned.1.call-start = ((), (), s32[]{:S(2)}) async-start(), calls=%async_computation.10 | async-start | bytes 2820096 | tf_op jit(solution)/shard_map/all_gather | solution.py:72
  9.4 262.2 %all-gather.15.cloned.1.call-start = ((), (), s32[]{:S(2)}) async-start(), calls=%async_computation.11 | async-start | bytes 2820096 | tf_op jit(solution)/shard_map/all_gather | solution.py:72
  10.0 295.2 %all-gather.17.cloned.1.call-start = ((), (), s32[]{:S(2)}) async-start(), calls=%async_computation.12 | async-start | bytes 8460288 | tf_op jit(solution)/shard_map/all_gather | solution.py:72
  10.6 369.5 %all-gather.19.cloned.1.call-start = ((), (), s32[]{:S(2)}) async-start(), calls=%async_computation.13 | async-start | bytes 2820096 | tf_op jit(solution)/shard_map/all_gather | solution.py:72
  11.2 445.0 %all-gather.23.cloned.1.call-start = ((), (), s32[]{:S(2)}) async-start(), calls=%async_computation.15 | async-start | bytes 11280384 | tf_op jit(solution)/shard_map/all_gather | solution.py:72
  11.9 533.4 %all-gather.21.cloned.1.call-start = ((), (), s32[]{:S(2)}) async-start(), calls=%async_computation.14 | async-start | bytes 11280384 | tf_op jit(solution)/shard_map/all_gather | solution.py:72
  12.7 1061.6 %reduce-scatter.35.cloned.1.call-start = ((), (), s32[]{:S(2)}) async-start(), calls=%async_computation.23 | async-start | bytes 5640192
  14.9 253.7 %copy-start.119 = (pred[128]{0:T(512)(128)(4,1)}, pred[128]{0:T(512)(128)(4,1)S(1)}, u32[]{:S(2)}) copy-start(pred[128]{0:T(512)(128)(4,1)S(1)} %iota_compare_fusion.8) | copy-start | bytes 388
  179.1 366.2 %copy-start.91 = (f32[1152]{0:T(1024)}, f32[1152]{0:T(1024)S(1)}, u32[]{:S(2)}) copy-start(f32[1152]{0:T(1024)S(1)} %get-tuple-element.115) | copy-start | bytes 13828
  179.1 405.7 %copy-start.93 = (f32[1152]{0:T(1024)}, f32[1152]{0:T(1024)S(1)}, u32[]{:S(2)}) copy-start(f32[1152]{0:T(1024)S(1)} %get-tuple-element.116) | copy-start | bytes 13828
  318.7 29.3 %collective-permute-start.1 = (bf16[2,208,2304]{2,1,0:T(8,128)(2,1)}, bf16[2,208,2304]{2,1,0:T(8,128)(2,1)}, u32[]{:S(2)}, u32[]{:S(2)}) collective-permute-start(bf16[2,208,2304]{2,1,0:T(8,128)(2,1)} %get-tuple-element.81), channel_id=1, source_target_pairs={{1,0},{2,1},{3,2},{4,3},{5,4},{6,5},{7,6},{8,7},{9,8},{10,9},{11,1... | collective-permute-start | bytes 5750792 | tf_op jit(solution)/shard_map/ppermute | solution.py:27
  320.0 32.0 %collective-permute-start = (bf16[2,208,2304]{2,1,0:T(8,128)(2,1)}, bf16[2,208,2304]{2,1,0:T(8,128)(2,1)}, u32[]{:S(2)}, u32[]{:S(2)}) collective-permute-start(bf16[2,208,2304]{2,1,0:T(8,128)(2,1)} %get-tuple-element.82), channel_id=1, source_target_pairs={{0,1},{1,2},{2,3},{3,4},{4,5},{5,6},{6,7},{7,8},{8,9},{9,10},{10,1... | collective-permute-start | bytes 5750792 | tf_op jit(solution)/shard_map/ppermute | solution.py:24
  679.3 19.2 collective-permute-start.3
  684.9 18.3 collective-permute-start.2
  696.1 379.9 %reduce-scatter.29.cloned.1.call-start = ((), (), s32[]{:S(2)}) async-start(), calls=%async_computation.20 | async-start | bytes 5640192
  762.9 314.7 %reduce-scatter.31.cloned.1.call-start = ((), (), s32[]{:S(2)}) async-start(), calls=%async_computation.21 | async-start | bytes 5640192
  770.8 308.5 %reduce-scatter.27.cloned.1.call-start = ((), (), s32[]{:S(2)}) async-start(), calls=%async_computation.19 | async-start | bytes 5640192
  786.4 432.4 %reduce-scatter.33.cloned.1.call-start = ((), (), s32[]{:S(2)}) async-start(), calls=%async_computation.22 | async-start | bytes 16920576
  800.3 593.6 %reduce-scatter.25.cloned.1.call-start = ((), (), s32[]{:S(2)}) async-start(), calls=%async_computation.18 | async-start | bytes 16920576
  894.5 715.2 %reduce-scatter.23.cloned.1.call-start = ((), (), s32[]{:S(2)}) async-start(), calls=%async_computation.17 | async-start | bytes 22560768 | tf_op jit(solution)/shard_map/reduce_scatter | solution.py:86
  913.3 912.8 %reduce-scatter.21.cloned.1.call-start = ((), (), s32[]{:S(2)}) async-start(), calls=%async_computation.16 | async-start | bytes 22560768 | tf_op jit(solution)/shard_map/reduce_scatter | solution.py:86
  929.7 1037.5 %all-reduce.21.cloned.1.call-start = ((), (), s32[]{:S(2)}) async-start(), calls=%async_computation.24 | async-start | bytes 10801152 | tf_op jit(solution)/shard_map/psum | solution.py:389
  (136 other events, 1906.9 us)
Sparse Core Ops, SparseCore 0:
  10.2 82.2 all-gather.8
  94.6 46.9 all-gather.10
  143.8 43.7 all-gather.12
  189.6 42.6 all-gather.14
  234.3 70.8 all-gather.16
  307.2 59.4 all-gather.18
  369.1 87.0 all-gather.22
  458.4 86.8 all-gather.20
  696.2 78.5 reduce-scatter.34
  778.7 87.0 reduce-scatter.28
  869.8 78.7 reduce-scatter.30
  952.5 91.0 reduce-scatter.26
  1047.7 171.1 reduce-scatter.32
  1222.8 170.9 reduce-scatter.24
  1397.9 211.7 reduce-scatter.22
  1614.2 211.8 reduce-scatter.20
  1830.6 136.5 all-reduce.20
where the time goes:
time: 2000 us; the launch traced here: 1990 us
  waiting for transfers between devices  1040 us (52%)
  matrix products  298 us (15%)
  blocking collectives  280 us (14%)
  local copies, waits for them, and re-layouts  195 us (10%)
  other arithmetic  152 us (8%)
    reduce_scatter x2, waiting for transfers between devices, grad_rows(): lax.psum_scatter(project_rows(operand, gradient), 'wide', scatter_dimensi...  428 us
    unnamed x23, waiting for transfers between devices  316 us
    all_gather x8, waiting for transfers between devices, fetch_rows(): lax.all_gather(shortened(shards), 'wide', axis=0, tiled=True)  169 us
    psum x2, blocking collectives, body(): modulation, text_sum = lax.psum((mod_part, text_part), 'wide')  158 us
    psum x1, waiting for transfers between devices, body(): lax.psum(grad_ada_part.astype(jnp.bfloat16), 'narrow').astype(jnp.float32)  122 us
    psum x1, blocking collectives, body(): lax.psum((d_modulation, d_gain_part, d_kv_part), 'wide')  99.1 us
    dot_general x10, matrix products, project(): return jnp.dot(operand, weights, preferred_element_type=jnp.float32)  94.6 us
    dot_general x10, matrix products, project_rows(): lax.dot_general(operand, gradient, (((0,), (0,)), ((), ())), preferred_el...  84.7 us
  transfers between devices with their start and end apart: 21, of which 8 were waited for; matrix products, arithmetic and copies ran while one was open for 23% of the time, Pallas kernels for 0%

commit v1 on v0

--- a/solution.py
+++ b/solution.py
@@ -1,19 +1,518 @@
+import functools
 import math
 
 import jax
 import jax.numpy as jnp
 from jax import lax
+from jax.experimental import pallas as pl
+from jax.experimental.pallas import tpu as pltpu
 from jax.sharding import PartitionSpec as P
 
 HEADS = 16
-
-
-def shortened(x):
-
-    def short(part):
-        return part.astype(jnp.bfloat16) if part.dtype == jnp.float32 else part
-
-    return jax.tree.map(short, x)
+MESH = pl.DeviceIdType.MESH
+DMA = pltpu.SemaphoreType.DMA
+LIMIT = 60 * 2**20
+
+
+class Place:
+    def __init__(self, wide):
+        self.wide = wide
+        self.chips = wide // 2
+        self.plane = lax.axis_index("narrow")
+        self.index = lax.axis_index("wide")
+        self.core = lax.rem(self.index, 2)
+        chip = lax.div(self.index, 2)
+        odd = lax.rem(chip, 2)
+        half = lax.div(chip, 2)
+        self.pos = (1 - odd) * half + odd * (self.chips - 1 - half)
+
+    def chip(self, step):
+        n = self.chips
+        q = lax.rem(self.pos + (step % n), n)
+        high = lax.div(q, n // 2)
+        return (1 - high) * (2 * q) + high * (2 * (n - q) - 1)
+
+    def member(self, step, core=None):
+        return 2 * self.chip(step) + (self.core if core is None else core)
+
+    def near(self):
+        return ((self.plane, self.member(1)), (self.plane, self.member(-1)),
+                (1 - self.plane, self.index), (self.plane, self.index + 1 - 2 * self.core))
+
+def greet(devices):
+    barrier = pltpu.get_barrier_semaphore()
+    for device in devices:
+        pl.semaphore_signal(barrier, inc=1, device_id=device, device_id_type=MESH)
+    pl.semaphore_wait(barrier, len(devices))
+
+def remote(src, dst, send, recv, device):
+    return pltpu.make_async_remote_copy(src_ref=src, dst_ref=dst, send_sem=send, recv_sem=recv,
+                                        device_id=device, device_id_type=MESH)
+
+def lanes(start, size):
+    return pl.ds(pl.multiple_of(start, 128), size)
+
+def gather_scratch(wide, count):
+    chips = wide // 2; reach = chips // 2
+    return [DMA((count, 2, reach, 2)), DMA((count, 2, reach, 2)), DMA((count, chips - 1)), DMA((count, chips - 1)),
+            DMA((count, chips)), DMA((count, chips)), DMA((count,))]
+
+def gather_steps(place, own, full, sems):
+    ring_s, ring_r, side_s, side_r, twin_s, twin_r, loc = sems
+    count = len(own)
+    chips = place.chips
+    reach = chips // 2
+    right, left, across, twin = place.near()
+    y = place.plane
+    sends = []
+    def go(c):
+        c.start(); sends.append(c)
+    def cols(i, part):
+        width = own[i].shape[-1]; a = width // 3
+        if part == 0: return lanes(y * (width - a), a)
+        if part == 1: return lanes(a, width - 2 * a)
+        return lanes((1 - y) * (width - a), a)
+    def ring(i, d, s, part, j, src=None):
+        sl = cols(i, part)
+        source = full[i].at[j, :, sl] if src is None else src.at[:, sl]
+        return remote(source, full[i].at[j, :, sl], ring_s.at[i, d, s-1, part], ring_r.at[i, d, s-1, part], (right, left)[d])
+    def side(i, slot, j, part):
+        sl = cols(i, part)
+        return remote(full[i].at[j, :, sl], full[i].at[j, :, sl], side_s.at[i, slot], side_r.at[i, slot], across)
+    def core_copy(i, slot, j, src=None):
+        return remote(full[i].at[j] if src is None else src, full[i].at[j], twin_s.at[i, slot], twin_r.at[i, slot], twin)
+    me = place.index
+    for part in (0, 1):
+        for i in range(count):
+            for d in (0, 1):
+                go(ring(i, d, 1, part, me, own[i]))
+    local = []
+    for i in range(count):
+        c = pltpu.make_async_copy(own[i], full[i].at[me], loc.at[i]); c.start(); local.append(c)
+        go(core_copy(i, chips - 1, me, own[i]))
+    yield
+    def shards(s):
+        if s == reach: return [(2 * s - 2, place.member(s))]
+        return [(2 * s - 2, place.member(-s)), (2 * s - 1, place.member(s))]
+    def finish(s, i):
+        for slot, j in shards(s):
+            side(i, slot, j, 2).wait_recv()
+            go(core_copy(i, slot, j))
+    for s in range(1, reach + 1):
+        for part in (0, 1):
+            for i in range(count):
+                for d in (0, 1):
+                    if s == reach and part != d: continue
+                    j = place.member(-s if d == 0 else s)
+                    ring(i, d, s, part, j).wait_recv()
+                    if s + 1 < reach or (s + 1 == reach and part == d):
+                        go(ring(i, d, s + 1, part, j))
+                    if part == 0:
+                        go(side(i, 2 * s - 2 + (0 if s == reach else d), j, 0))
+            yield
+        if s > 1:
+            for i in range(count): finish(s - 1, i)
+    for i in range(count): finish(reach, i)
+    yield
+    other = 1 - place.core
+    for s in range(1, reach + 1):
+        for i in range(count):
+            for (slot, _), step in zip(shards(s), (-s, s)):
+                core_copy(i, slot, place.member(step, other)).wait_recv()
+    for i in range(count):
+        core_copy(i, chips - 1, place.member(0, other)).wait_recv()
+    for c in local: c.wait()
+    for c in sends: c.wait_send()
+
+def gather_kernel(wide, count, *refs):
+    own, full = refs[:count], refs[count:2*count]
+    place = Place(wide)
+    greet(place.near())
+    for _ in gather_steps(place, own, full, refs[2*count:]): pass
+
+ANY = pl.BlockSpec(memory_space=pl.ANY)
+VM = pl.BlockSpec(memory_space=pltpu.VMEM)
+
+def gather(wide, arrays, collective_id):
+    count = len(arrays)
+    return pl.pallas_call(
+        functools.partial(gather_kernel, wide, count),
+        out_shape=[jax.ShapeDtypeStruct((wide,) + a.shape, a.dtype) for a in arrays],
+        in_specs=[ANY] * count,
+        out_specs=[ANY] * count,
+        scratch_shapes=gather_scratch(wide, count),
+        compiler_params=pltpu.CompilerParams(collective_id=collective_id, has_side_effects=True),
+        name="gather_rows",
+    )(*arrays)
+
+def scatter_scratch(wide, shapes):
+    chips = wide // 2; reach = chips // 2; count = len(shapes)
+    bufs = []
+    for rows, width in shapes:
+        bufs += [pltpu.VMEM((chips, rows, width), jnp.bfloat16),
+                 pltpu.VMEM((chips, rows, width), jnp.bfloat16),
+                 pltpu.VMEM((chips, rows, 2 * (width // 9)), jnp.bfloat16),
+                 pltpu.VMEM((2, reach, rows, width - 2 * (width // 9)), jnp.bfloat16),
+                 pltpu.VMEM((rows, width), jnp.bfloat16)]
+    sems = [DMA((count, chips)), DMA((count, chips)), DMA((count, chips)), DMA((count, chips)), DMA((count, chips)),
+            DMA((count, 2, reach)), DMA((count, 2, reach)), DMA((count,)), DMA((count,))]
+    return bufs + sems
+
+def scatter_steps(place, parts, outs, bufs, sems):
+    load, twin_s, twin_r, side_s, side_r, ring_s, ring_r, last_s, last_r = sems
+    count = len(parts)
+    chips = place.chips
+    reach = chips // 2
+    right, left, across, twin = place.near()
+    y = place.plane
+    other = 1 - place.core
+    sends = []
+    def go(c):
+        c.start(); sends.append(c)
+    own = [bufs[5*i] for i in range(count)]; tw = [bufs[5*i+1] for i in range(count)]
+    sd = [bufs[5*i+2] for i in range(count)]; rg = [bufs[5*i+3] for i in range(count)]; lt = [bufs[5*i+4] for i in range(count)]
+    steps = [reach] + [x for s in range(reach - 1, 0, -1) for x in (s, -s)] + [0]
+    slot_of = {s: k for k, s in enumerate(steps)}
+    slot_of[-reach] = slot_of[reach]
+    w = [o.shape[-1] // 9 for o in own]
+    def ringcols(i, d, s):
+        base = y * 2 * w[i]
+        if s > 1: return base, 7 * w[i]
+        k = 4 if (d + i) % 2 == 0 else 3
+        return (base, 4 * w[i]) if k == 4 else (base + 4 * w[i], 3 * w[i])
+    def twin_copy(i, k):
+        return remote(parts[i].at[place.member(steps[k], other)], tw[i].at[k], twin_s.at[i, k], twin_r.at[i, k], twin)
+    def load_copy(i, k):
+        return pltpu.make_async_copy(parts[i].at[place.member(steps[k])], own[i].at[k], load.at[i, k])
+    def side(i, k):
+        return remote(own[i].at[k, :, lanes((1 - y) * 7 * w[i], 2 * w[i])], sd[i].at[k], side_s.at[i, k], side_r.at[i, k], across)
+    def ring(i, d, s):
+        start, size = ringcols(i, d, s)
+        k = slot_of[(reach + 1 - s) if d == 0 else -(reach + 1 - s)]
+        return remote(own[i].at[k, :, lanes(start, size)], rg[i].at[d, s-1, :, lanes(start - y * 2 * w[i], size)],
+                      ring_s.at[i, d, s-1], ring_r.at[i, d, s-1], (right, left)[d])
+    def last(i):
+        sl = lanes(y * 2 * w[i], 7 * w[i])
+        return remote(own[i].at[slot_of[0], :, sl], lt[i].at[:, sl], last_s.at[i], last_r.at[i], across)
+    def add(i, dst_k, start, src, src_start, pieces):
+        def one(t, _):
+            to = lanes(start + t * w[i], w[i])
+            value = own[i][dst_k, :, to].astype(jnp.float32)
+            value += src[:, lanes(src_start + t * w[i], w[i])].astype(jnp.float32)
+            own[i][dst_k, :, to] = value.astype(jnp.bfloat16)
+            return 0
+        lax.fori_loop(0, pieces, one, 0)
+    for k in range(chips):
+        for i in range(count):
+            go(twin_copy(i, k)); load_copy(i, k).start()
+    yield
+    def pair(k):
+        for i in range(count):
+            load_copy(i, k).wait(); twin_copy(i, k).wait_recv()
+            add(i, k, 0, tw[i].at[k], 0, 9)
+            go(side(i, k))
+    def planes(k):
+        for i in range(count):
+            side(i, k).wait_recv()
+            add(i, k, y * 7 * w[i], sd[i].at[k], 0, 2)
+    def ring_in(i, d, s):
+        ring(i, d, s).wait_recv()
+        start, size = ringcols(i, d, s)
+        t = reach - s
+        add(i, slot_of[t if d == 0 else -t], start, rg[i].at[d, s-1], start - y * 2 * w[i], size // w[i])
+    need = {1: [slot_of[reach]]}
+    for s in range(2, reach + 1):
+        need[s] = [slot_of[reach + 1 - s], slot_of[-(reach + 1 - s)]]
+    pair(0); yield
+    pair(1); pair(2); yield
+    planes(0)
+    for i in range(count):
+        for d in (0, 1): go(ring(i, d, 1))
+    yield
+    done = 3
+    for s in range(2, reach + 1):
+        while done < min(chips, 2 * s + 1):
+            pair(done); done += 1
+        if s == reach:
+            while done < chips:
+                pair(done); done += 1
+        for k in need[s]: planes(k)
+        yield
+        for i in range(count):
+            for d in (0, 1):
+                ring_in(i, d, s - 1)
+                go(ring(i, d, s))
+        yield
+    planes(slot_of[0])
+    for i in range(count):
+        for d in (0, 1): ring_in(i, d, reach)
+        go(last(i))
+    yield
+    for i in range(count):
+        last(i).wait_recv()
+        k = slot_of[0]
+        mine, theirs = y * 7 * w[i], (1 - y) * 7 * w[i]
+        def copy(t, _, i=i, k=k, mine=mine, theirs=theirs):
+            a, b = lanes(mine + t * w[i], w[i]), lanes(theirs + t * w[i], w[i])
+            outs[i][:, a] = own[i][k, :, a]
+            outs[i][:, b] = lt[i][:, b]
+            return 0
+        lax.fori_loop(0, 2, copy, 0)
+        def both(t, _, i=i, k=k):
+            c = lanes((2 + t) * w[i], w[i])
+            outs[i][:, c] = (own[i][k, :, c].astype(jnp.float32) + lt[i][:, c].astype(jnp.float32)).astype(jnp.bfloat16)
+            return 0
+        lax.fori_loop(0, 5, both, 0)
+    for c in sends: c.wait_send()
+
+def scatter_kernel(wide, count, *refs):
+    parts, outs = refs[:count], refs[count:2*count]
+    bufs, sems = refs[2*count:7*count], refs[7*count:]
+    place = Place(wide)
+    greet(place.near())
+    for _ in scatter_steps(place, parts, outs, bufs, sems): pass
+
+def scatter(wide, arrays, collective_id):
+    count = len(arrays)
+    shapes = [a.shape[1:] for a in arrays]
+    return pl.pallas_call(
+        functools.partial(scatter_kernel, wide, count),
+        out_shape=[jax.ShapeDtypeStruct(s, jnp.bfloat16) for s in shapes],
+        in_specs=[ANY] * count,
+        out_specs=[VM] * count,
+        scratch_shapes=scatter_scratch(wide, shapes),
+        compiler_params=pltpu.CompilerParams(collective_id=collective_id, has_side_effects=True, vmem_limit_bytes=LIMIT),
+        name="scatter_rows",
+    )(*arrays)
+
+
+def front_scratch(wide, mod_block, text_block, kv_block):
+    f32, bf16 = jnp.float32, jnp.bfloat16
+    return ([pltpu.VMEM((wide,) + mod_block, f32), pltpu.VMEM((wide,) + text_block, bf16),
+             pltpu.VMEM((wide,) + kv_block, bf16), pltpu.VMEM((wide,) + kv_block, bf16)]
+            + [DMA((wide,))] * 10)
+
+
+def peers(place):
+    n = place.wide
+    return [(t, lax.rem(place.index + t, n)) for t in range(1, n)]
+
+
+def front_steps(place, mod_parts, text_parts, kv_rows, mod_all, kv_all, prompt, scratch):
+    mod_in, text_in, kv_out, kv_in = scratch[:4]
+    ms, mr, ts, tr, gs, gr, ks, kr, hs, hr = scratch[4:]
+    n, me, y = place.wide, place.index, place.plane
+    others = peers(place)
+    sends = []
+
+    def go(copy):
+        copy.start()
+        sends.append(copy)
+
+    def mod_copy(t, j):
+        return remote(mod_parts.at[j], mod_in.at[t], ms.at[t], mr.at[t], (y, j))
+
+    def text_copy(t, j):
+        return remote(text_parts.at[j], text_in.at[t], ts.at[t], tr.at[t], (y, j))
+
+    def mod_back(t, j, i):
+        return remote(mod_all.at[i], mod_all.at[i], gs.at[t], gr.at[t], (y, j))
+
+    def kv_copy(t, j):
+        return remote(kv_out.at[j], kv_in.at[t], ks.at[t], kr.at[t], (y, j))
+
+    def kv_back(t, j, i):
+        return remote(kv_all.at[i], kv_all.at[i], hs.at[t], hr.at[t], (y, j))
+
+    for t, j in others:
+        go(text_copy(t, j))
+        go(mod_copy(t, j))
+    yield
+    total = text_parts[me].astype(jnp.float32)
+    for t, j in others:
+        text_copy(t, j).wait_recv()
+        total += text_in[t].astype(jnp.float32)
+    prompt[...] = total.astype(jnp.bfloat16)
+
+    def block(j, _):
+        kv_out[j] = jnp.dot(prompt[...], kv_rows[j], preferred_element_type=jnp.float32).astype(jnp.bfloat16)
+        return 0
+
+    lax.fori_loop(0, n, block, 0)
+    for t, j in others:
+        go(kv_copy(t, j))
+    total = mod_parts[me]
+    for t, j in others:
+        mod_copy(t, j).wait_recv()
+        total += mod_in[t]
+    mod_all[me] = total
+    for t, j in others:
+        go(mod_back(t, j, me))
+    yield
+    total = kv_out[me].astype(jnp.float32)
+    for t, j in others:
+        kv_copy(t, j).wait_recv()
+        total += kv_in[t].astype(jnp.float32)
+    kv_all[me] = total.astype(jnp.bfloat16)
+    for t, j in others:
+        go(kv_back(t, j, me))
+    yield
+    for t, j in others:
+        i = lax.rem(me + n - t, n)
+        mod_back(t, j, i).wait_recv()
+        kv_back(t, j, i).wait_recv()
+    for copy in sends:
+        copy.wait_send()
+
+
+def start_kernel(wide, count, *refs):
+    mod_parts, text_parts, kv_rows = refs[:3]
+    own, refs = refs[3:3 + count], refs[3 + count:]
+    mod_all, kv_all, prompt = refs[:3]
+    full, refs = refs[3:3 + count], refs[3 + count:]
+    place = Place(wide)
+    right, left, across, twin = place.near()
+    greet([across] + [(place.plane, j) for t, j in peers(place)])
+    small = front_steps(place, mod_parts, text_parts, kv_rows, mod_all, kv_all, prompt, refs[:14])
+    large = gather_steps(place, own, full, refs[14:])
+    next(large)
+    next(small)
+    next(large)
+    next(small)
+    next(large)
+    next(small)
+    for _ in large:
+        pass
+    for _ in small:
+        pass
+
+
+def start(wide, mod_parts, text_parts, kv_rows, arrays, collective_id):
+    count = len(arrays)
+    kv_block = (text_parts.shape[1], kv_rows.shape[2])
+    out = pl.pallas_call(
+        functools.partial(start_kernel, wide, count),
+        out_shape=[
+            jax.ShapeDtypeStruct(mod_parts.shape, mod_parts.dtype),
+            jax.ShapeDtypeStruct((wide,) + kv_block, jnp.bfloat16),
+            jax.ShapeDtypeStruct(text_parts.shape[1:], jnp.bfloat16),
+        ]
+        + [jax.ShapeDtypeStruct((wide,) + a.shape, a.dtype) for a in arrays],
+        in_specs=[VM] * 3 + [ANY] * count,
+        out_specs=[VM] * 3 + [ANY] * count,
+        scratch_shapes=front_scratch(wide, mod_parts.shape[1:], text_parts.shape[1:], kv_block)
+        + gather_scratch(wide, count),
+        compiler_params=pltpu.CompilerParams(
+            collective_id=collective_id, has_side_effects=True, vmem_limit_bytes=LIMIT
+        ),
+        name="start",
+    )(mod_parts, text_parts, kv_rows, *arrays)
+    return out[0], out[1], out[2], out[3:]
+
+
+def everyone(place):
+    n, me, y = place.wide, place.index, place.plane
+    near = [(t, (y, lax.rem(me + t, n))) for t in range(1, n)]
+    return near + [(n + t, (1 - y, lax.rem(me + t, n))) for t in range(n)]
+
+
+def finish_scratch(wide, vec_block, kv_block):
+    f32, bf16 = jnp.float32, jnp.bfloat16
+    return ([pltpu.VMEM((wide,) + vec_block, f32), pltpu.VMEM((wide,) + kv_block, bf16)]
+            + [DMA((wide,))] * 4 + [DMA((2 * wide,))] * 6)
+
+
+def finish_steps(place, vec_parts, kv_parts, kv_rows, vec_all, kv_all, prompt_all, scratch):
+    vec_in, kv_in = scratch[:2]
+    vs, vr, ks, kr, gs, gr, hs, hr, ps, pr = scratch[2:]
+    n, me, y = place.wide, place.index, place.plane
+    others = peers(place)
+    all_others = everyone(place)
+    sends = []
+
+    def go(copy):
+        copy.start()
+        sends.append(copy)
+
+    def vec_copy(t, j):
+        return remote(vec_parts.at[j], vec_in.at[t], vs.at[t], vr.at[t], (y, j))
+
+    def kv_copy(t, j):
+        return remote(kv_parts.at[j], kv_in.at[t], ks.at[t], kr.at[t], (y, j))
+
+    def source(u):
+        return (y if u < n else 1 - y), lax.rem(me + 2 * n - u, n)
+
+    def spread(ref, send, recv, u, device, plane, i):
+        return remote(ref.at[plane, i], ref.at[plane, i], send.at[u], recv.at[u], device)
+
+    for t, j in others:
+        go(kv_copy(t, j))
+        go(vec_copy(t, j))
+    total = kv_parts[me].astype(jnp.float32)
+    for t, j in others:
+        kv_copy(t, j).wait_recv()
+        total += kv_in[t].astype(jnp.float32)
+    kv_all[y, me] = total.astype(jnp.bfloat16)
+    for u, device in all_others:
+        go(spread(kv_all, hs, hr, u, device, y, me))
+    total = vec_parts[me]
+    for t, j in others:
+        vec_copy(t, j).wait_recv()
+        total += vec_in[t]
+    vec_all[y, me] = total
+    for u, device in all_others:
+        go(spread(vec_all, gs, gr, u, device, y, me))
+    yield
+    for u, device in all_others:
+        plane, i = source(u)
+        if u < n:
+            spread(kv_all, hs, hr, u, device, plane, i).wait_recv()
+
+    def block(j, total):
+        return total + lax.dot_general(
+            kv_all[y, j], kv_rows[j], (((1,), (1,)), ((), ())), preferred_element_type=jnp.float32
+        )
+
+    rows = lax.fori_loop(0, n, block, jnp.zeros(prompt_all.shape[2:], jnp.float32))
+    prompt_all[y, me] = rows.astype(jnp.bfloat16)
+    for u, device in all_others:
+        go(spread(prompt_all, ps, pr, u, device, y, me))
+    yield
+    for u, device in all_others:
+        plane, i = source(u)
+        if u >= n:
+            spread(kv_all, hs, hr, u, device, plane, i).wait_recv()
+        spread(vec_all, gs, gr, u, device, plane, i).wait_recv()
+        spread(prompt_all, ps, pr, u, device, plane, i).wait_recv()
+    for copy in sends:
+        copy.wait_send()
+
+
+def finish_kernel(wide, vec_parts, kv_parts, kv_rows, vec_all, kv_all, prompt_all, *scratch):
+    place = Place(wide)
+    greet([device for u, device in everyone(place)])
+    for _ in finish_steps(place, vec_parts, kv_parts, kv_rows, vec_all, kv_all, prompt_all, scratch):
+        pass
+
+
+def finish(wide, vec_parts, kv_parts, kv_rows, collective_id):
+    text_count, rows = kv_parts.shape[1], kv_rows.shape[1]
+    return pl.pallas_call(
+        functools.partial(finish_kernel, wide),
+        out_shape=[
+            jax.ShapeDtypeStruct((2,) + vec_parts.shape, jnp.float32),
+            jax.ShapeDtypeStruct((2,) + kv_parts.shape, jnp.bfloat16),
+            jax.ShapeDtypeStruct((2, wide, text_count, rows), jnp.bfloat16),
+        ],
+        in_specs=[VM] * 3,
+        out_specs=[VM] * 3,
+        scratch_shapes=finish_scratch(wide, vec_parts.shape[1:], kv_parts.shape[1:]),
+        compiler_params=pltpu.CompilerParams(
+            collective_id=collective_id, has_side_effects=True, vmem_limit_bytes=LIMIT
+        ),
+        name="finish",
+    )(vec_parts, kv_parts, kv_rows)
 
 
 def with_halo(block, sides, width):
@@ -66,26 +565,12 @@
     )
 
 
-def fetch_rows(shards):
-    return jax.tree.map(
-        lambda part, own: part.astype(own.dtype),
-        lax.all_gather(shortened(shards), "wide", axis=0, tiled=True),
-        shards,
-    )
-
-
-def back_weights(shards):
-    return jax.tree.map(
-        lambda part, own: part.astype(own.dtype),
-        lax.all_gather(shortened(shards), "wide", axis=0, tiled=True),
-        shards,
-    )
-
-
-def grad_rows(operand, gradient):
-    return lax.psum_scatter(
-        project_rows(operand, gradient), "wide", scatter_dimension=0, tiled=True
-    )
+def whole(value):
+    return value.reshape(-1, value.shape[-1])
+
+
+def part_rows(wide, operand, gradient):
+    return project_rows(operand, gradient).astype(jnp.bfloat16).reshape(wide, -1, gradient.shape[-1])
 
 
 def body(
@@ -119,27 +604,43 @@
     rows_model = ada_weight.shape[0]
     rows_text = text_weight.shape[0]
     score_scale = head_size ** (-0.5)
+    plane = lax.axis_index("narrow")
+    wide = lax.axis_size("wide")
+
+    def swap(value):
+        return lax.ppermute(value, "narrow", [(0, 1), (1, 0)])
+
+    def by_plane(own, other):
+        return jnp.where(plane == 0, jnp.stack([own, other]), jnp.stack([other, own]))
+
+    def blocks(value):
+        return value.reshape(value.shape[0], wide, -1).transpose(1, 0, 2)
+
     signal = jax.nn.silu(time_embed(timesteps, model_width)[0]).astype(jnp.bfloat16)
     signal_rows = lax.dynamic_slice_in_dim(signal, position * rows_model, rows_model)
     mod_part = jnp.dot(signal_rows, ada_weight, preferred_element_type=jnp.float32)
-    prompt = text[0]
-    prompt_rows = lax.dynamic_slice_in_dim(prompt, position * rows_text, rows_text, 1)
+    prompt_rows = lax.dynamic_slice_in_dim(text[0], position * rows_text, rows_text, 1)
     text_part = project(prompt_rows, text_weight)
-    modulation, text_sum = lax.psum((mod_part, text_part), "wide")
+    kv_rows = blocks(kv_weight)
+    modulation, kv_all, prompt_cols, (full_qkv, full_out) = start(
+        wide,
+        mod_part.reshape(wide, 1, -1),
+        blocks(text_part).astype(jnp.bfloat16),
+        kv_rows,
+        (qkv_weight, out_weight),
+        0,
+    )
+    full_qkv, full_out = whole(full_qkv), whole(full_out)
     modulation = modulation.reshape(9, model_width)
     shift_a, scale_a, gate_a = (modulation[0], modulation[1], modulation[2])
     shift_t, scale_t, gate_t = (modulation[3], modulation[4], modulation[5])
     shift_m, scale_m, gate_m = (modulation[6], modulation[7], modulation[8])
-    prompt_low = text_sum.astype(jnp.bfloat16)
-    prompt_cols = lax.dynamic_slice_in_dim(prompt_low, position * rows_model, rows_model, 1)
-    kv_part = project(prompt_cols, kv_weight)
-    text_kv = lax.psum(kv_part, "wide").astype(jnp.bfloat16)
+    text_kv = kv_all.transpose(1, 0, 2).reshape(text_count, 2 * model_width)
     keys_c = text_kv[:, :model_width].reshape(text_count, head_count, head_size)
     values_c = text_kv[:, model_width:].reshape(text_count, head_count, head_size)
     valid = jnp.arange(text_count) < text_len[0]
-    start = hidden[0].reshape(row_count, model_width).astype(jnp.float32)
-    full_qkv, full_out = fetch_rows((qkv_weight, out_weight))
-    normed_a = modulate(start, shift_a, scale_a).astype(jnp.bfloat16)
+    tokens = hidden[0].reshape(row_count, model_width).astype(jnp.float32)
+    normed_a = modulate(tokens, shift_a, scale_a).astype(jnp.bfloat16)
     qkv_a = (
         project(normed_a, full_qkv)
         .astype(jnp.bfloat16)
@@ -155,8 +656,10 @@
     attn_a = jnp.einsum("fhpq,fqhd->fphd", probs_a, values_a, preferred_element_type=jnp.float32)
     attn_a = attn_a.astype(jnp.bfloat16).reshape(row_count, model_width)
     branch_a = project(attn_a, full_out)
-    first = start + gate_a * branch_a
-    full_cross_q, full_cross_out = fetch_rows((cross_q_weight, cross_out_weight))
+    first = tokens + gate_a * branch_a
+    full_cross_q, full_cross_out, full_temp_qkv, full_temp_out = map(
+        whole, gather(wide, (cross_q_weight, cross_out_weight, temp_qkv_weight, temp_out_weight), 1)
+    )
     normed_c = scaled_norm(first, cross_gain).astype(jnp.bfloat16)
     query_c = (
         project(normed_c, full_cross_q)
@@ -174,7 +677,6 @@
     attn_c = attn_c.astype(jnp.bfloat16).reshape(row_count, model_width)
     branch_c = project(attn_c, full_cross_out)
     second = first + branch_c
-    full_temp_qkv, full_temp_out = fetch_rows((temp_qkv_weight, temp_out_weight))
     normed_t = modulate(second, shift_t, scale_t).astype(jnp.bfloat16)
     qkv_t = (
         project(normed_t, full_temp_qkv)
@@ -224,32 +726,32 @@
     attn_t = attn_t.astype(jnp.bfloat16).reshape(row_count, model_width)
     branch_t = project(attn_t, full_temp_out)
     third = second + gate_t * branch_t
-    (full_up,) = fetch_rows((up_weight,))
+    full_up, full_down = map(whole, gather(wide, (up_weight, down_weight), 2))
     normed_m = modulate(third, shift_m, scale_m).astype(jnp.bfloat16)
     hidden_m = project(normed_m, full_up)
     act = jax.nn.gelu(hidden_m, approximate=True).astype(jnp.bfloat16)
-    (full_down,) = fetch_rows((down_weight,))
     branch_m = project(act, full_down)
     result = third + gate_m * branch_m
     block_out = result.astype(jnp.bfloat16).reshape(1, frames, patches, model_width)
     gradient = cotangent[0].reshape(row_count, model_width).astype(jnp.float32)
     d_gate_m = jnp.sum(gradient * branch_m, 0)
     d_branch_m = (gate_m * gradient).astype(jnp.bfloat16)
-    (back_down,) = back_weights((down_weight,))
-    grad_down = grad_rows(act, d_branch_m)
+    back_down = full_down
+    grad_down = part_rows(wide, act, d_branch_m)
     d_act = project_back(d_branch_m, back_down)
     unused_gelu, gelu_back = jax.vjp(lambda values: jax.nn.gelu(values, approximate=True), hidden_m)
     d_hidden_m = gelu_back(d_act)[0].astype(jnp.bfloat16)
-    (back_up,) = back_weights((up_weight,))
-    grad_up = grad_rows(normed_m, d_hidden_m)
+    back_up = full_up
+    grad_up = part_rows(wide, normed_m, d_hidden_m)
+    grad_up, grad_down = scatter(wide, (grad_up, grad_down), 3)
     d_normed_m = project_back(d_hidden_m, back_up)
     unused_mlp, mlp_back = jax.vjp(modulate, third, shift_m, scale_m)
     d_third, d_shift_m, d_scale_m = mlp_back(d_normed_m)
     gradient = gradient + d_third
     d_gate_t = jnp.sum(gradient * branch_t, 0)
     d_branch_t = (gate_t * gradient).astype(jnp.bfloat16)
-    back_temp_qkv, back_temp_out = back_weights((temp_qkv_weight, temp_out_weight))
-    grad_temp_out = grad_rows(attn_t, d_branch_t)
+    back_temp_qkv, back_temp_out = full_temp_qkv, full_temp_out
+    grad_temp_out = part_rows(wide, attn_t, d_branch_t)
     d_attn_t = (
         project_back(d_branch_t, back_temp_out)
         .astype(jnp.bfloat16)
@@ -281,14 +783,14 @@
     d_kv_t = d_kv_t + jnp.pad(arrived[6:], ((frames - 2, 0), (0, 0), (0, 0)))
     d_qkv_t = jnp.concatenate([d_query_t.reshape(frames, patches, model_width), d_kv_t], -1)
     d_qkv_t = d_qkv_t.reshape(row_count, 3 * model_width).astype(jnp.bfloat16)
-    grad_temp_qkv = grad_rows(normed_t, d_qkv_t)
+    grad_temp_qkv = part_rows(wide, normed_t, d_qkv_t)
     d_normed_t = project_back(d_qkv_t, back_temp_qkv)
     unused_temp, temp_back = jax.vjp(modulate, second, shift_t, scale_t)
     d_second, d_shift_t, d_scale_t = temp_back(d_normed_t)
     gradient = gradient + d_second
     d_branch_c = gradient.astype(jnp.bfloat16)
-    back_cross_q, back_cross_out = back_weights((cross_q_weight, cross_out_weight))
-    grad_cross_out = grad_rows(attn_c, d_branch_c)
+    back_cross_q, back_cross_out = full_cross_q, full_cross_out
+    grad_cross_out = part_rows(wide, attn_c, d_branch_c)
     d_attn_c = (
         project_back(d_branch_c, back_cross_out)
         .astype(jnp.bfloat16)
@@ -311,15 +813,18 @@
     d_kv_part = jnp.concatenate(
         [d_keys_c.reshape(text_count, model_width), d_values_c.reshape(text_count, model_width)], -1
     )
-    grad_cross_q = grad_rows(normed_c, d_query_c)
+    grad_cross_q = part_rows(wide, normed_c, d_query_c)
+    grad_cross_q, grad_cross_out, grad_temp_qkv, grad_temp_out = scatter(
+        wide, (grad_cross_q, grad_cross_out, grad_temp_qkv, grad_temp_out), 4
+    )
     d_normed_c = project_back(d_query_c, back_cross_q)
     unused_cross, cross_back = jax.vjp(scaled_norm, first, cross_gain)
     d_first, d_gain_part = cross_back(d_normed_c)
     gradient = gradient + d_first
     d_gate_a = jnp.sum(gradient * branch_a, 0)
     d_branch_a = (gate_a * gradient).astype(jnp.bfloat16)
-    back_qkv, back_out = back_weights((qkv_weight, out_weight))
-    grad_out = grad_rows(attn_a, d_branch_a)
+    back_qkv, back_out = full_qkv, full_out
+    grad_out = part_rows(wide, attn_a, d_branch_a)
     d_attn_a = (
         project_back(d_branch_a, back_out)
         .astype(jnp.bfloat16)
@@ -347,12 +852,13 @@
         .reshape(row_count, 3 * model_width)
         .astype(jnp.bfloat16)
     )
-    grad_qkv = grad_rows(normed_a, d_qkv_a)
+    grad_qkv = part_rows(wide, normed_a, d_qkv_a)
+    grad_qkv, grad_out = scatter(wide, (grad_qkv, grad_out), 5)
     d_normed_a = project_back(d_qkv_a, back_qkv)
-    unused_spatial, spatial_back = jax.vjp(modulate, start, shift_a, scale_a)
+    unused_spatial, spatial_back = jax.vjp(modulate, tokens, shift_a, scale_a)
     d_start, d_shift_a, d_scale_a = spatial_back(d_normed_a)
     grad_hidden = (gradient + d_start).astype(jnp.bfloat16).reshape(1, frames, patches, model_width)
-    d_modulation = jnp.concatenate(
+    vectors = jnp.concatenate(
         [
             d_shift_a,
             d_scale_a,
@@ -363,41 +869,35 @@
             d_shift_m,
             d_scale_m,
             d_gate_m,
+            d_gain_part,
         ]
     )
-    d_modulation, d_gain_wide, d_text_kv = lax.psum((d_modulation, d_gain_part, d_kv_part), "wide")
-    d_text_kv_low = d_text_kv.astype(jnp.bfloat16)
-    grad_kv_part = project_rows(prompt_cols, d_text_kv_low)
-    d_prompt_cols = project_back(d_text_kv_low, kv_weight).astype(jnp.bfloat16)
-    d_prompt = lax.all_gather(d_prompt_cols, "wide", axis=1, tiled=True)
-    grad_text_part = project_rows(prompt_rows, d_prompt)
-    grad_ada_part = signal_rows.astype(jnp.float32)[:, None] * d_modulation[None, :]
-    (
-        grad_ada,
-        grad_text,
-        grad_kv,
-        grad_qkv,
-        grad_out,
-        grad_cross_q,
-        grad_cross_out,
-        grad_temp_qkv,
-        grad_temp_out,
-        grad_up,
-        grad_down,
-        grad_gain,
-    ) = (
-        lax.psum(grad_ada_part.astype(jnp.bfloat16), "narrow").astype(jnp.float32),
-        lax.psum(grad_text_part.astype(jnp.bfloat16), "narrow").astype(jnp.float32),
-        lax.psum(grad_kv_part.astype(jnp.bfloat16), "narrow").astype(jnp.float32),
-        lax.psum(grad_qkv.astype(jnp.bfloat16), "narrow").astype(jnp.float32),
-        lax.psum(grad_out.astype(jnp.bfloat16), "narrow").astype(jnp.float32),
-        lax.psum(grad_cross_q.astype(jnp.bfloat16), "narrow").astype(jnp.float32),
-        lax.psum(grad_cross_out.astype(jnp.bfloat16), "narrow").astype(jnp.float32),
-        lax.psum(grad_temp_qkv.astype(jnp.bfloat16), "narrow").astype(jnp.float32),
-        lax.psum(grad_temp_out.astype(jnp.bfloat16), "narrow").astype(jnp.float32),
-        lax.psum(grad_up.astype(jnp.bfloat16), "narrow").astype(jnp.float32),
-        lax.psum(grad_down.astype(jnp.bfloat16), "narrow").astype(jnp.float32),
-        lax.psum(d_gain_wide.astype(jnp.bfloat16), "narrow").astype(jnp.float32),
+    vec_all, d_kv_all, d_prompt_all = finish(
+        wide, vectors.reshape(wide, 1, -1), blocks(d_kv_part).astype(jnp.bfloat16), kv_rows, 6
+    )
+    vec_all = vec_all.reshape(2, -1)
+    d_modulation, d_gain = vec_all[:, : 9 * model_width], vec_all[:, 9 * model_width :]
+
+    def merged(value):
+        return value.transpose(0, 2, 1, 3).reshape(2 * text_count, -1)
+
+    both_cols = by_plane(prompt_cols, swap(prompt_cols)).reshape(2 * text_count, -1)
+    both_rows = by_plane(prompt_rows, swap(prompt_rows)).reshape(2 * text_count, -1)
+    both_signal = by_plane(signal_rows, swap(signal_rows)).astype(jnp.float32)
+    grad_kv = project_rows(both_cols, merged(d_kv_all))
+    grad_text = project_rows(both_rows, merged(d_prompt_all))
+    grad_ada = (
+        both_signal[0][:, None] * d_modulation[0][None, :]
+        + both_signal[1][:, None] * d_modulation[1][None, :]
+    )
+    grad_gain = d_gain[0] + d_gain[1]
+    grad_qkv, grad_out, grad_cross_q, grad_cross_out = (
+        grad_qkv.astype(jnp.float32), grad_out.astype(jnp.float32),
+        grad_cross_q.astype(jnp.float32), grad_cross_out.astype(jnp.float32),
+    )
+    grad_temp_qkv, grad_temp_out, grad_up, grad_down = (
+        grad_temp_qkv.astype(jnp.float32), grad_temp_out.astype(jnp.float32),
+        grad_up.astype(jnp.float32), grad_down.astype(jnp.float32),
     )
     return (
         block_out,

time: 2000 us -> 1260 us (0.63)
  waiting for transfers between devices: 1040 us -> 0.02 us
  Pallas kernels: 0 us -> 634 us
  blocking collectives: 280 us -> 0 us
  matrix products: 298 us -> 264 us
    pallas_call x0 -> x7, Pallas kernels: none -> 634 us  [the longest x3 268 us: scatter(): pl.pallas_call(functools.partial(scatter_kernel, wide, count), out_shape=...]
    reduce_scatter x2 -> x0, waiting for transfers between devices: 428 us -> none  [grad_rows(): lax.psum_scatter(project_rows(operand, gradient), 'wide', scatter_dimensi...]
    unnamed x23 -> x0, waiting for transfers between devices: 316 us -> none
    psum x4 -> x0, blocking collectives: 262 us -> none  [the longest x2 158 us: body(): modulation, text_sum = lax.psum((mod_part, text_part), 'wide')]
    all_gather x8 -> x0, waiting for transfers between devices: 169 us -> none  [fetch_rows(): lax.all_gather(shortened(shards), 'wide', axis=0, tiled=True)]
    psum x1 -> x0, waiting for transfers between devices: 122 us -> none  [body(): lax.psum(grad_ada_part.astype(jnp.bfloat16), 'narrow').astype(jnp.float32)]
    convert_element_type x24 -> x12, other arithmetic: 39.2 us -> 18.2 us  [the longest x1 2.39 us: body(): grad_up.astype(jnp.float32)]
    dot_general x10 -> x9, matrix products: 94.6 us -> 81.6 us  [project(): return jnp.dot(operand, weights, preferred_element_type=jnp.float32)]
  transfers between devices with their start and end apart: 21 -> 7, of which waited for: 8 -> 0; matrix products, arithmetic and copies ran while one was open for 23% -> 15% of each run, Pallas kernels for 0% -> 30%
where the time goes in v1:
time: 1260 us; the launch traced here: 1250 us
  Pallas kernels  634 us (50%)
  matrix products  264 us (21%)
  local copies, waits for them, and re-layouts  197 us (16%)
  other arithmetic  138 us (11%)
  starting transfers between devices  15.9 us (1%)
    pallas_call x3, Pallas kernels, scatter(): pl.pallas_call(functools.partial(scatter_kernel, wide, count), out_shape=...  268 us
    pallas_call x2, Pallas kernels, gather(): pl.pallas_call(functools.partial(gather_kernel, wide, count), out_shape=[...  149 us
    pallas_call x1, Pallas kernels, finish(): pl.pallas_call(functools.partial(finish_kernel, wide), out_shape=[jax.Sha...  109 us
    pallas_call x1, Pallas kernels, start(): pl.pallas_call(functools.partial(start_kernel, wide, count), out_shape=[j...  108 us
    dot_general x9, matrix products, project(): return jnp.dot(operand, weights, preferred_element_type=jnp.float32)  81.6 us
    dot_general x10, matrix products, project_rows(): lax.dot_general(operand, gradient, (((0,), (0,)), ((), ())), preferred_el...  71.2 us
    dot_general x8, matrix products, project_back(): lax.dot_general(gradient, weights, (((1,), (1,)), ((), ())), preferred_el...  64.2 us
    unnamed x279, local copies, waits for them, and re-layouts  46.9 us
  transfers between devices with their start and end apart: 7, of which 0 were waited for; matrix products, arithmetic and copies ran while one was open for 15% of the time, Pallas kernels for 30%

profile of v1, /device:TPU:0, one launch (start us, length us, event | category | flops | bytes accessed | tf_op | source)
XLA Modules:
  0.0 1252.8 jit_solution(16572250835435196732)
XLA Ops:
  12.2 107.7 %start.1 = (f32[16,1,648]{2,1,0:T(1,128)}, bf16[16,128,144]{2,1,0:T(8,128)(2,1)}, bf16[128,72]{1,0:T(8,128)(2,1)}, bf16[16,72,3456]{2,1,0:T(8,128)(2,1)}, bf16[16,72,1152]{2,1,0:T(8,128)(2,1)}) custom-call(f32[16,1,648]{2,1,0:T(1,128)} %reshape.560.refs_0_, bf16[16,128,72]{2,1,0:T(8,128)(2,1)} %bitcast.376, bf16[16,72,144]{2,1,0:T(8,128)(2,1)} %bitcast.360, ...), custom_call_target="tpu_custom_call" | custom-call | tf_op jit(solution)/shard_map/start/pallas_call | solution.py:393
  127.1 10.7 convolution_convert_fusion.9
  137.9 16.2 %reshape.656 = bf16[3,208,3,16,72]{4,3,2,1,0:T(8,128)(2,1)} reshape(bf16[624,3456]{1,0:T(8,128)(2,1)} %convolution_convert_fusion.9) | data formatting | bytes 8626176 | tf_op jit(solution)/shard_map/reshape | solution.py:647
  202.4 63.7 %gather_rows.2 = (bf16[16,72,1152]{2,1,0:T(8,128)(2,1)}, bf16[16,72,1152]{2,1,0:T(8,128)(2,1)}, bf16[16,72,3456]{2,1,0:T(8,128)(2,1)}, bf16[16,72,1152]{2,1,0:T(8,128)(2,1)}) custom-call(bf16[72,1152]{1,0:T(8,128)(2,1)} %refs_0_.2, bf16[72,1152]{1,0:T(8,128)(2,1)} %refs_1_.2, bf16[72,3456]{1,0:T(8,128)(2,1)} %refs_2_.1, bf16[72,1152]{1,0:T(8,128)(2,1)} %refs_3_.3), custom_call_target="tpu_custom_call" | custom-call | tf_op jit(solution)/shard_map/gather_rows/pallas_call | solution.py:138
  323.5 85.7 %gather_rows.3 = (bf16[16,72,4608]{2,1,0:T(8,128)(2,1)}, bf16[16,288,1152]{2,1,0:T(8,128)(2,1)}) custom-call(bf16[72,4608]{1,0:T(8,128)(2,1)} %refs_0_.3, bf16[288,1152]{1,0:T(8,128)(2,1)} %refs_1_.3), custom_call_target="tpu_custom_call" | custom-call | tf_op jit(solution)/shard_map/gather_rows/pallas_call | solution.py:138
  409.2 13.3 %fusion.127 = f32[624,4608]{1,0:T(8,128)} fusion(bf16[624,1152]{1,0:T(8,128)(2,1)} %bitcast.386, bf16[4608,1152]{1,0:T(8,128)(2,1)} %bitcast.396), kind=kOutput, calls=%fused_computation.336 | convolution fusion | flops 6624903168 | bytes 23556096 | tf_op jit(solution)/shard_map/dot_general | solution.py:557
  463.6 22.2 %fusion.13 = (bf16[624,4608]{1,0:T(8,128)(2,1)}, f32[624,4608]{1,0:T(8,128)}) fusion(f32[624,4608]{1,0:T(8,128)} %fusion.127, bf16[1152,4608]{1,0:T(8,128)(2,1)} %bitcast.398, f32[624,1152]{1,0:T(8,128)S(1)} %get-tuple-element.103, f32[1152]{0:T(1024)S(1)} %get-tuple-element.82, f32[1152]{0:T(1024)S(1)} %copy-done.109, f32[624]{0:T(1024)S(1)} %fusion.97, ...), kind=kOutput, calls=%fused_computation.32 | convolution fusion | flops 6686005248 | bytes 42260352 | tf_op jit(solution)/shard_map/dot_general | solution.py:553
  485.8 15.7 %multiply_reduce_fusion.4 = (f32[1152]{0:T(1024)}, f32[624]{0:T(1024)S(1)}, f32[1152]{0:T(1024)}, f32[624,1152]{1,0:T(8,128)}) fusion(f32[624,1152]{1,0:T(8,128)S(1)} %get-tuple-element.103, f32[624]{0:T(1024)S(1)} %fusion.97, f32[624]{0:T(1024)S(1)} %broadcast_multiply_fusion, f32[1152]{0:T(1024)S(1)} %copy-done.109, ...), kind=kOutput, calls=%fused_computation.142 | convolution fusion | flops 6630651392 | bytes 22139712 | tf_op jit(solution)/shard_map/dot_general | solution.py:557
  501.5 21.8 %fusion.41 = (f32[1152]{0:T(1024)}, bf16[624,1152]{1,0:T(8,128)(2,1)}, f32[624]{0:T(1024)S(1)}, f32[624,1152]{1,0:T(8,128)S(1)}, bf16[624,1152]{1,0:T(8,128)(2,1)}) fusion(bf16[1,3,208,1152]{3,2,1,0:T(8,128)(2,1)S(1)} %copy-done.50, f32[624,1152]{1,0:T(8,128)} %copy-done.53, f32[1152]{0:T(1024)S(1)} %get-tuple-element.81, ...), kind=kOutput, calls=%fused_computation.139 | convolution fusion | flops 6661562880 | bytes 35081472 | tf_op jit(solution)/shard_map/dot_general | solution.py:553
  523.3 15.6 %convolution_convert_fusion = bf16[4608,1152]{1,0:T(8,128)(2,1)} fusion(bf16[624,1152]{1,0:T(8,128)(2,1)} %get-tuple-element.140, f32[624,4608]{1,0:T(8,128)} %get-tuple-element.172), kind=kOutput, calls=%fused_computation.6 | convolution fusion | flops 6656090112 | bytes 23556096 | tf_op jit(solution)/shard_map/dot_general | solution.py:563
  567.8 8.8 bitcast_multiply_fusion.9
  584.9 19.2 %fusion.117 = (bf16[7,208,2304]{1,2,0:T(8,128)(2,1)S(1)}, f32[7,208,2304]{1,2,0:T(8,128)}) fusion(f32[3,208,1152]{1,2,0:T(8,128)} %get-tuple-element.123, f32[3,208,1152]{1,2,0:T(8,128)} %get-tuple-element.139, f32[3,208,1152]{1,2,0:T(8,128)} %get-tuple-element.124, f32[3,208,1152]{1,2,0:T(8,128)} %get-tuple-element.138, ...), kind=kLoop, calls=%fused_computation.327 | loop fusion | flops 103993344 | bytes 48881664 | tf_op jit(solution)/shard_map/convert.49
  620.4 14.2 %convolution_convert_fusion.1 = bf16[1152,4608]{1,0:T(8,128)(2,1)} fusion(bf16[624,4608]{1,0:T(8,128)(2,1)} %get-tuple-element.171, f32[624,1152]{1,0:T(8,128)} %copy-done.53, f32[1152]{0:T(1024)S(1)} %get-tuple-element.82, f32[1152]{0:T(1024)S(1)} %copy-done.109, f32[624]{0:T(1024)S(1)} %fusion.97, f32[624]{0:T(1024)S(1)} %broadcast_multiply_fusion), kind=kOutput, calls=%fused_computation.7 | convolution fusion | flops 6633805824 | bytes 19257216 | tf_op jit(solution)/shard_map/dot_general | solution.py:563
  634.6 115.7 %scatter_rows.5 = (bf16[72,4608]{1,0:T(8,128)(2,1)}, bf16[288,1152]{1,0:T(8,128)(2,1)}) custom-call(bf16[16,72,4608]{2,1,0:T(8,128)(2,1)} %bitcast.354, bf16[16,288,1152]{2,1,0:T(8,128)(2,1)} %bitcast.353), custom_call_target="tpu_custom_call" | custom-call | tf_op jit(solution)/shard_map/scatter_rows/pallas_call | solution.py:278
  786.6 11.3 multiply_reduce_fusion.6
  797.9 9.5 convolution_convert_fusion.2
  875.5 12.0 multiply_convert_fusion.1
  903.0 10.0 copy.200
  912.9 14.3 %convert_element_type.326 = bf16[624,3456]{0,1:T(8,128)(2,1)} reshape(bf16[3,208,3,16,72]{1,0,4,3,2:T(4,128)(2,1)} %copy.200) | data formatting | bytes 8626176 | tf_op jit(solution)/shard_map/convert_element_type | solution.py:853
  927.4 13.0 %multiply_reduce_fusion.8 = (f32[1152]{0:T(1024)S(1)}, f32[624]{0:T(1024)S(1)}, f32[1152]{0:T(1024)S(1)}, f32[624,1152]{1,0:T(8,128)}) fusion(f32[624]{0:T(1024)S(1)} %copy-done.97, f32[624]{0:T(1024)S(1)} %copy-done.98, bf16[1,3,208,1152]{3,2,1,0:T(8,128)(2,1)S(1)} %copy-done.14, f32[1152]{0:T(1024)S(1)} %copy-done.80, ...), kind=kOutput, calls=%fused_computation.146 | convolution fusion | flops 4976582144 | bytes 18047808 | tf_op jit(solution)/shard_map/dot_general | solution.py:557
  942.4 109.4 %finish.1 = (f32[2,16,1,720]{3,2,1,0:T(1,128)}, bf16[2,16,128,144]{3,2,1,0:T(8,128)(2,1)}, bf16[2,16,128,72]{3,2,1,0:T(8,128)(2,1)}) custom-call(f32[16,1,720]{2,1,0:T(1,128)} %reshape.600.vec_parts, bf16[16,128,144]{2,1,0:T(8,128)(2,1)} %maximum_bitcast_fusion.kv_parts, bf16[16,72,144]{2,1,0:T(8,128)(2,1)} %bitcast.361), custom_call_target="tpu_custom_call" | custom-call | tf_op jit(solution)/shard_map/finish/pallas_call | solution.py:501
  1053.9 11.3 convolution_convert_fusion.3
  1069.2 87.4 %scatter_rows.4 = (bf16[72,1152]{1,0:T(8,128)(2,1)}, bf16[72,1152]{1,0:T(8,128)(2,1)}, bf16[72,3456]{1,0:T(8,128)(2,1)}, bf16[72,1152]{1,0:T(8,128)(2,1)}) custom-call(bf16[16,72,1152]{2,1,0:T(8,128)(2,1)} %bitcast.371, bf16[16,72,1152]{2,1,0:T(8,128)(2,1)} %bitcast.372, bf16[16,72,3456]{2,1,0:T(8,128)(2,1)} %bitcast.355, bf16[16,72,1152]{2,1,0:T(8,128)(2,1)} %bitcast.370), custom_call_target="tpu_custom_call" | custom-call | tf_op jit(solution)/shard_map/scatter_rows/pallas_call | solution.py:278
  1179.0 64.9 %scatter_rows.3 = (bf16[72,3456]{1,0:T(8,128)(2,1)}, bf16[72,1152]{1,0:T(8,128)(2,1)}) custom-call(bf16[16,72,3456]{2,1,0:T(8,128)(2,1)} %bitcast.356, bf16[16,72,1152]{2,1,0:T(8,128)(2,1)} %bitcast.369), custom_call_target="tpu_custom_call" | custom-call | tf_op jit(solution)/shard_map/scatter_rows/pallas_call | solution.py:278
  (457 shorter events, 374.9 us)
Async XLA Ops:
  1.8 420.8 %collective-permute-start.4 = (bf16[72]{0:T(256)(128)(2,1)S(1)}, bf16[72]{0:T(256)(128)(2,1)}, u32[]{:S(2)}, u32[]{:S(2)}) collective-permute-start(bf16[72]{0:T(256)(128)(2,1)S(1)} %fusion.102), channel_id=1, source_target_pairs={{0,16},{16,0},{1,17},{17,1},{2,18},{18,2},{3,19},{19,3},{4,20},{20... | collective-permute-start | bytes 440 | tf_op jit(solution)/shard_map/ppermute | solution.py:611
  5.6 419.0 %collective-permute-start.5 = (bf16[128,256]{1,0:T(8,128)(2,1)S(1)}, bf16[128,256]{1,0:T(8,128)(2,1)S(1)}, u32[]{:S(2)}, u32[]{:S(2)}) collective-permute-start(bf16[128,256]{1,0:T(8,128)(2,1)S(1)} %fusion.177), channel_id=1, source_target_pairs={{0,16},{16,0},{1,17},{17,1},{2,18},{18,2},{3,19},{19,3},{4,20},{20... | collective-permute-start | bytes 196616 | tf_op jit(solution)/shard_map/ppermute | solution.py:611
  8.9 113.3 %copy-start.13 = (bf16[1,3,208,1152]{3,2,1,0:T(8,128)(2,1)S(1)}, bf16[1,3,208,1152]{3,2,1,0:T(8,128)(2,1)}, u32[]{:S(2)}) copy-start(bf16[1,3,208,1152]{3,2,1,0:T(8,128)(2,1)} %param.18) | copy-start | bytes 4313092
  119.9 304.0 %collective-permute-start.6 = (bf16[128,72]{1,0:T(8,128)(2,1)}, bf16[128,72]{1,0:T(8,128)(2,1)S(1)}, u32[]{:S(2)}, u32[]{:S(2)}) collective-permute-start(bf16[128,72]{1,0:T(8,128)(2,1)} %get-tuple-element.48), channel_id=1, source_target_pairs={{0,16},{16,0},{1,17},{17,1},{2,18},{18,2},{3,19},{19,3},{4,20},{20... | collective-permute-start | bytes 55304 | tf_op jit(solution)/shard_map/ppermute | solution.py:611
  122.2 155.1 %copy-start.103 = (pred[128]{0:T(512)(128)(4,1)}, pred[128]{0:T(512)(128)(4,1)S(1)}, u32[]{:S(2)}) copy-start(pred[128]{0:T(512)(128)(4,1)S(1)} %iota_compare_fusion.8) | copy-start | bytes 388
  123.9 67.0 %copy-start.105 = (f32[1152]{0:T(1024)}, f32[1152]{0:T(1024)S(1)}, u32[]{:S(2)}) copy-start(f32[1152]{0:T(1024)S(1)} %get-tuple-element.89) | copy-start | bytes 13828
  123.9 159.0 %copy-start.95 = (f32[1152]{0:T(1024)}, f32[1152]{0:T(1024)S(1)}, u32[]{:S(2)}) copy-start(f32[1152]{0:T(1024)S(1)} %get-tuple-element.85) | copy-start | bytes 13828
  123.9 159.0 %copy-start.107 = (f32[1152]{0:T(1024)}, f32[1152]{0:T(1024)S(1)}, u32[]{:S(2)}) copy-start(f32[1152]{0:T(1024)S(1)} %get-tuple-element.84) | copy-start | bytes 13828
  198.0 68.0 %copy-start.114 = (f32[1152]{0:T(1024)S(1)}, f32[1152]{0:T(1024)}, u32[]{:S(2)}) copy-start(f32[1152]{0:T(1024)} %param.35) | copy-start | bytes 13828
  200.1 70.9 %copy-start.83 = (f32[624]{0:T(1024)}, f32[624]{0:T(1024)S(1)}, u32[]{:S(2)}) copy-start(f32[624]{0:T(1024)S(1)} %broadcast_multiply_fusion.2) | copy-start | bytes 7492
  202.3 63.7 %copy-start.87 = (f32[624]{0:T(1024)}, f32[624]{0:T(1024)S(1)}, u32[]{:S(2)}) copy-start(f32[624]{0:T(1024)S(1)} %multiply_reduce_fusion.15) | copy-start | bytes 7492
  202.3 68.6 %copy-start.99 = (f32[624]{0:T(1024)}, f32[624]{0:T(1024)S(1)}, u32[]{:S(2)}) copy-start(f32[624]{0:T(1024)S(1)} %fusion.95) | copy-start | bytes 7492
  294.6 130.6 %collective-permute-start.1 = (bf16[2,208,2304]{2,1,0:T(8,128)(2,1)}, bf16[2,208,2304]{2,1,0:T(8,128)(2,1)}, u32[]{:S(2)}, u32[]{:S(2)}) collective-permute-start(bf16[2,208,2304]{2,1,0:T(8,128)(2,1)} %get-tuple-element.120), channel_id=1, source_target_pairs={{1,0},{2,1},{3,2},{4,3},{5,4},{6,5},{7,6},{8,7},{9,8},{10,9},{11,1... | collective-permute-start | bytes 5750792 | tf_op jit(solution)/shard_map/ppermute | solution.py:526
  295.9 133.4 %collective-permute-start = (bf16[2,208,2304]{2,1,0:T(8,128)(2,1)}, bf16[2,208,2304]{2,1,0:T(8,128)(2,1)}, u32[]{:S(2)}, u32[]{:S(2)}) collective-permute-start(bf16[2,208,2304]{2,1,0:T(8,128)(2,1)} %get-tuple-element.121), channel_id=1, source_target_pairs={{0,1},{1,2},{2,3},{3,4},{4,5},{5,6},{6,7},{7,8},{8,9},{9,10},{10,1... | collective-permute-start | bytes 5750792 | tf_op jit(solution)/shard_map/ppermute | solution.py:523
  409.2 14.7 %copy-start.94 = (bf16[128,72]{1,0:T(8,128)(2,1)S(1)}, bf16[128,72]{1,0:T(8,128)(2,1)}, u32[]{:S(2)}) copy-start(bf16[128,72]{1,0:T(8,128)(2,1)} %get-tuple-element.48) | copy-start | bytes 55300
  462.8 22.9 %copy-start.53 = (f32[624,1152]{1,0:T(8,128)}, f32[624,1152]{1,0:T(8,128)S(1)}, u32[]{:S(2)}) copy-start(f32[624,1152]{1,0:T(8,128)S(1)} %get-tuple-element.103) | copy-start | bytes 8626180
  485.8 15.8 %copy-start.50 = (bf16[1,3,208,1152]{3,2,1,0:T(8,128)(2,1)S(1)}, bf16[1,3,208,1152]{3,2,1,0:T(8,128)(2,1)}, u32[]{:S(2)}) copy-start(bf16[1,3,208,1152]{3,2,1,0:T(8,128)(2,1)} %param.19) | copy-start | bytes 4313092
  614.8 148.0 %collective-permute-start.3 = (bf16[2,208,2304]{2,1,0:T(8,128)(2,1)}, bf16[2,208,2304]{2,1,0:T(8,128)(2,1)}, u32[]{:S(2)}, u32[]{:S(2)}) collective-permute-start(bf16[2,208,2304]{2,1,0:T(8,128)(2,1)} %copy.189), channel_id=1, source_target_pairs={{1,0},{2,1},{3,2},{4,3},{5,4},{6,5},{7,6},{8,7},{9,8},{10,9},{11,1... | collective-permute-start | bytes 5750792 | tf_op jit(solution)/shard_map/ppermute | solution.py:526
  616.1 150.8 %collective-permute-start.2 = (bf16[2,208,2304]{2,1,0:T(8,128)(2,1)}, bf16[2,208,2304]{2,1,0:T(8,128)(2,1)}, u32[]{:S(2)}, u32[]{:S(2)}) collective-permute-start(bf16[2,208,2304]{2,1,0:T(8,128)(2,1)} %copy.188), channel_id=1, source_target_pairs={{0,1},{1,2},{2,3},{3,4},{4,5},{5,6},{6,7},{7,8},{8,9},{9,10},{10,1... | collective-permute-start | bytes 5750792 | tf_op jit(solution)/shard_map/ppermute | solution.py:523
  912.9 14.3 %copy-start.14 = (bf16[1,3,208,1152]{3,2,1,0:T(8,128)(2,1)S(1)}, bf16[1,3,208,1152]{3,2,1,0:T(8,128)(2,1)}, u32[]{:S(2)}) copy-start(bf16[1,3,208,1152]{3,2,1,0:T(8,128)(2,1)} %param.18) | copy-start | bytes 4313092
  912.9 14.3 %copy-start.80 = (f32[1152]{0:T(1024)S(1)}, f32[1152]{0:T(1024)}, u32[]{:S(2)}) copy-start(f32[1152]{0:T(1024)} %copy-done.79) | copy-start | bytes 13828
  912.9 14.3 %copy-start.97 = (f32[624]{0:T(1024)S(1)}, f32[624]{0:T(1024)}, u32[]{:S(2)}) copy-start(f32[624]{0:T(1024)} %div.122) | copy-start | bytes 7492
  912.9 14.3 %copy-start.98 = (f32[624]{0:T(1024)S(1)}, f32[624]{0:T(1024)}, u32[]{:S(2)}) copy-start(f32[624]{0:T(1024)} %rsqrt.51) | copy-start | bytes 7492
  1179.0 68.7 %copy-start.75 = (bf16[2,128,256]{2,1,0:T(8,128)(2,1)S(1)}, bf16[2,128,256]{2,1,0:T(8,128)(2,1)}, u32[]{:S(2)}) copy-start(bf16[2,128,256]{2,1,0:T(8,128)(2,1)} %maximum_select_fusion) | copy-start | bytes 393220
  (112 other events, 613.3 us)

commit v2 on v0

v2 whole, which is shorter than its diff:
```python
import functools
import math

import jax
import jax.numpy as jnp
from jax import lax
from jax.experimental import pallas as pl
from jax.experimental.pallas import tpu as pltpu
from jax.sharding import PartitionSpec as P

HEADS = 16
LIMIT = 60 * 2**20
MESH = pl.DeviceIdType.MESH
DMA = pltpu.SemaphoreType.DMA
VM = pl.BlockSpec(memory_space=pltpu.VMEM)
ANY = pl.BlockSpec(memory_space=pl.ANY)
f32, bf16 = jnp.float32, jnp.bfloat16
NN, NT, TN = (((1,), (0,)), ((), ())), (((1,), (1,)), ((), ())), (((0,), (0,)), ((), ()))


def dot(a, b, dims=NN):
    return lax.dot_general(a, b, dims, preferred_element_type=jnp.float32)


def row_blocks(count, size, step, carry=0, unroll=1):
    def one(r, value):
        return step(pl.ds(pl.multiple_of(r * size, size), size), value)
    return lax.fori_loop(0, count // size, one, carry, unroll=unroll)


def normal(value):
    centred = value - jnp.mean(value, -1, keepdims=True)
    scale = lax.rsqrt(jnp.mean(centred * centred, -1, keepdims=True) + 1e-06)
    return centred * scale, scale


def windows(width):
    size = width // HEADS
    found = []
    for head in range(HEADS):
        low, high = head * size, (head + 1) * size
        start = low // 128 * 128
        found.append((start, -(-high // 128) * 128 - start))
    return found


def head_mask(heads_ref, head, start, size):
    return heads_ref[head : head + 1, start : start + size]


def softmax_down(scores):
    exps = jnp.exp(scores - jnp.max(scores, 0, keepdims=True))
    return exps * (1.0 / jnp.sum(exps, 0, keepdims=True))


GROUPS = 4


def by_heads(frames, patches, width, step, tick):
    spans = list(enumerate(windows(width)))
    size = HEADS // GROUPS
    for group in range(GROUPS):

        def frame(f, _):
            rows = pl.ds(pl.multiple_of(f * patches, 16), patches)
            for head, (start, lanes_taken) in spans[group * size : (group + 1) * size]:
                step(rows, head, start, lanes_taken)
            tick.inside(f, 0, frames)
            return 0

        lax.fori_loop(0, frames, frame, 0)


def clear(ref):
    ref[...] = jnp.zeros_like(ref)


def spatial_attention(tick, qkv, heads, attn, frames, patches):
    width = attn.shape[-1]
    scale = (width // HEADS) ** -0.5
    clear(attn)

    def step(rows, head, start, size):
        mask = head_mask(heads, head, start, size)
        query = qkv[rows, start : start + size] * mask
        keys = qkv[rows, width + start : width + start + size]
        values = qkv[rows, 2 * width + start : 2 * width + start + size] * mask
        probs = softmax_down(dot(keys, query, NT) * scale).astype(bf16)
        attn[rows, start : start + size] += dot(probs, values, TN).astype(bf16)

    by_heads(frames, patches, width, step, tick)


def spatial_attention_back(tick, qkv, d_attn, heads, d_qkv, frames, patches):
    width = d_attn.shape[-1]
    scale = (width // HEADS) ** -0.5
    clear(d_qkv)

    def step(rows, head, start, size):
        mask = head_mask(heads, head, start, size)
        query = qkv[rows, start : start + size] * mask
        keys = qkv[rows, width + start : width + start + size]
        values = qkv[rows, 2 * width + start : 2 * width + start + size]
        grad = d_attn[rows, start : start + size] * mask
        probs = softmax_down(dot(keys, query, NT) * scale)
        d_probs = dot(values, grad, NT)
        inner = jnp.sum(probs * d_probs, 0, keepdims=True)
        d_scores = (probs * (d_probs - inner)).astype(bf16)
        d_qkv[rows, start : start + size] += (dot(d_scores, keys * mask, TN) * scale).astype(bf16)
        d_qkv[rows, width + start : width + start + size] += (dot(d_scores, query) * scale).astype(bf16)
        d_qkv[rows, 2 * width + start : 2 * width + start + size] += dot(probs.astype(bf16), grad).astype(bf16)

    by_heads(frames, patches, width, step, tick)


def matmul(x, w, out, tick, unit=1152):
    for c in range(0, w.shape[1], unit):
        out[:, c : c + unit] = dot(x[...], w[:, c : c + unit]).astype(out.dtype)
        tick()


def spatial_kernel(frames, patches, tick, x, mod, heads, w_qkv, w_out, normed, qkv, attn, branch, first):
    rows = frames * patches

    def norm(at, _):
        hat, _unused = normal(x[at, :].astype(f32))
        normed[at, :] = (hat * (1.0 + mod[1:2, :]) + mod[0:1, :]).astype(bf16)
        return 0

    row_blocks(rows, 16, norm, unroll=3)
    tick()
    matmul(normed, w_qkv, qkv, tick)
    spatial_attention(tick, qkv, heads, attn, frames, patches)
    product = dot(attn[...], w_out[...])
    branch[...] = product.astype(bf16)
    first[...] = x[...].astype(f32) + mod[2:3, :] * product


def back_norm(rows, hat_of, gain_row, d_normed, add_to, sums, size=16):
    width = d_normed.shape[-1]

    def one(at, carry):
        total, weighted = carry
        hat, scale = normal(hat_of(at))
        grad = d_normed[at, :]
        total += grad.reshape(size // 8, 8, width).sum(0)
        product = grad * hat
        weighted += product.reshape(size // 8, 8, width).sum(0)
        d_hat = grad * gain_row
        d_value = scale * (d_hat - jnp.mean(d_hat, -1, keepdims=True)
                           - hat * jnp.mean(d_hat * hat, -1, keepdims=True))
        add_to(at, d_value)
        return total, weighted

    zero = jnp.zeros((8, width), f32)
    total, weighted = row_blocks(rows, size, one, (zero, zero))
    return jnp.sum(total, 0, keepdims=True), jnp.sum(weighted, 0, keepdims=True)


def gate_back(rows, gradient, branch, gate_row, d_branch, size=16):
    width = gradient.shape[-1]

    def one(at, total):
        grad = gradient[at, :]
        d_branch[at, :] = (gate_row * grad).astype(bf16)
        return total + (grad * branch[at, :].astype(f32)).reshape(size // 8, 8, width).sum(0)

    total = row_blocks(rows, size, one, jnp.zeros((8, width), f32))
    return jnp.sum(total, 0, keepdims=True)


def spatial_back_kernel(frames, patches, tick, gradient, x, mod, heads, w_qkv, w_out, normed, qkv, attn, branch,
                        d_hidden, g_qkv, g_out, d_mod, d_branch, d_attn, d_qkv, d_normed, part, load):
    rows, width = x.shape

    def fetch(n):
        return pltpu.make_async_copy(w_qkv.at[:, pl.ds(n * width, width)], part.at[n % 2], load.at[n % 2])

    fetch(0).start()
    fetch(1).start()
    d_mod[2:3, :] = gate_back(rows, gradient, branch, mod[2:3, :], d_branch)
    tick()
    g_out[...] = dot(attn[...], d_branch[...], TN).astype(bf16)
    tick()
    d_attn[...] = dot(d_branch[...], w_out[...], NT).astype(bf16)
    tick()
    spatial_attention_back(tick, qkv, d_attn, heads, d_qkv, frames, patches)
    for n in range(3):
        cols = slice(n * width, (n + 1) * width)
        g_qkv[:, cols] = dot(normed[...], d_qkv[:, cols], TN).astype(bf16)
        tick()
        fetch(n).wait()
        product = dot(d_qkv[:, cols], part[n % 2], NT)
        if n == 0:
            d_normed[...] = product
            fetch(2).start()
        else:
            d_normed[...] += product
        tick()

    def add_to(at, value):
        d_hidden[at, :] = (gradient[at, :] + value).astype(bf16)

    d_mod[0:1, :], d_mod[1:2, :] = back_norm(
        rows, lambda at: x[at, :].astype(f32), 1.0 + mod[1:2, :], d_normed, add_to, None)


class Halo:
    def __init__(self, place, sems):
        n, me = place.wide, place.index
        self.sems = sems
        self.beyond = ((place.plane, lax.rem(me + 1, n)), (place.plane, lax.rem(me + n - 1, n)))

    def copy(self, way, source, target):
        return remote(source, target, self.sems.at[0, way], self.sems.at[1, way], self.beyond[way])


def cross_kernel(wide, frames, patches, tick, first, gain, mod, heads, valid, text_kv, w_q, w_out, w_tqkv,
                 normed, query, attn, second, normed_t, qkv_t, near, outer, sems):
    rows, width = first.shape
    scale = (width // HEADS) ** -0.5
    halo = Halo(Place(wide), sems)

    def norm(at, _):
        hat, _unused = normal(first[at, :])
        normed[at, :] = (hat * gain[...]).astype(bf16)
        return 0

    row_blocks(rows, 16, norm, unroll=3)
    tick()
    query[...] = dot(normed[...], w_q[...]).astype(bf16)
    clear(attn)
    tick()

    def step(at, head, start, size):
        mask = head_mask(heads, head, start, size)
        q = query[at, start : start + size] * mask
        keys = text_kv[:, start : start + size]
        values = text_kv[:, width + start : width + start + size] * mask
        scores = jnp.where(valid[...] > 0, dot(keys, q, NT) * scale, -1e30)
        attn[at, start : start + size] += dot(softmax_down(scores).astype(bf16), values, TN).astype(bf16)

    by_heads(frames, patches, width, step, tick)
    second[...] = first[...] + dot(attn[...], w_out[...])
    tick()

    def norm_t(at, _):
        hat, _unused = normal(second[at, :])
        normed_t[at, :] = (hat * (1.0 + mod[4:5, :]) + mod[3:4, :]).astype(bf16)
        return 0

    row_blocks(rows, 16, norm_t, unroll=3)
    edge = 2 * patches
    sends = [halo.copy(0, normed_t.at[rows - edge :, :], outer.at[:edge, :]),
             halo.copy(1, normed_t.at[:edge, :], outer.at[edge:, :])]
    for copy in sends:
        copy.start()
    tick()
    matmul(normed_t, w_tqkv, qkv_t, tick)
    for f in range(frames):
        near[2 + f] = qkv_t[f * patches : (f + 1) * patches, width:]
    tick.finish()
    for n, copy in enumerate(sends):
        copy.wait_recv()
        side = outer[n * edge : (n + 1) * edge, :]
        for c in (width, 2 * width):
            found = dot(side, w_tqkv[:, c : c + width]).astype(bf16)
            for f in range(2):
                near[n * (frames + 2) + f, :, c - width : c] = found[f * patches : (f + 1) * patches]
            tick()
    for copy in sends:
        copy.wait_send()


def cross_back_kernel(frames, patches, tick, gradient, first, gain, heads, valid, text_kv, w_q, w_out, normed, query,
                      attn, gradient_out, g_q, g_out, d_gain, d_kv, d_branch, d_attn, d_query, d_normed):
    rows, width = first.shape
    scale = (width // HEADS) ** -0.5
    d_branch[...] = gradient[...].astype(bf16)
    clear(d_query)
    clear(d_kv)
    tick()
    g_out[...] = dot(attn[...], d_branch[...], TN).astype(bf16)
    tick()
    d_attn[...] = dot(d_branch[...], w_out[...], NT).astype(bf16)
    tick()

    def step(at, head, start, size):
        mask = head_mask(heads, head, start, size)
        q = query[at, start : start + size] * mask
        keys = text_kv[:, start : start + size]
        values = text_kv[:, width + start : width + start + size]
        grad = d_attn[at, start : start + size] * mask
        scores = jnp.where(valid[...] > 0, dot(keys, q, NT) * scale, -1e30)
        probs = softmax_down(scores)
        d_probs = dot(values, grad, NT)
        inner = jnp.sum(probs * d_probs, 0, keepdims=True)
        d_scores = (probs * (d_probs - inner)).astype(bf16)
        d_query[at, start : start + size] += (dot(d_scores, keys * mask, TN) * scale).astype(bf16)
        d_kv[:, start : start + size] += dot(d_scores, q) * scale
        d_kv[:, width + start : width + start + size] += dot(probs.astype(bf16), grad)

    by_heads(frames, patches, width, step, tick)
    g_q[...] = dot(normed[...], d_query[...], TN).astype(bf16)
    tick()
    d_normed[...] = dot(d_query[...], w_q[...], NT)
    tick()

    def add_to(at, value):
        gradient_out[at, :] = gradient[at, :] + value

    _unused, d_gain[...] = back_norm(rows, lambda at: first[at, :], gain[...], d_normed, add_to, None)


SLAB = 16


def slab_rows(start):
    return pl.ds(pl.multiple_of(start, SLAB), SLAB)


def slabs(patches, step, tick):
    count = patches // SLAB

    def one(b, _):
        step(pl.multiple_of(b * SLAB, SLAB))
        tick.inside(b, 0, count)
        return 0

    lax.fori_loop(0, count, one, 0)


def head_sums(products, spread):
    high = products.astype(bf16)
    low = (products - high.astype(f32)).astype(bf16)
    return dot(high, spread) + dot(low, spread)


def slab_probs(at, qkv, near, width, allowed, spread, frames, patches):
    scale = (width // HEADS) ** -0.5
    queries = [qkv[slab_rows(f * patches + at), :width].astype(f32) for f in range(frames)]
    products = jnp.concatenate(
        [queries[f] * near[f + o, slab_rows(at), :width].astype(f32) for o in range(5) for f in range(frames)], 0
    )
    every = head_sums(products, spread[...]) * scale
    every = jnp.where(allowed[...] > 0, every, -1e30)
    size = frames * SLAB
    scores = [every[o * size : (o + 1) * size] for o in range(5)]
    top = functools.reduce(jnp.maximum, scores)
    exps = [jnp.exp(s - top) for s in scores]
    share = 1.0 / functools.reduce(jnp.add, exps)
    return queries, [e * share for e in exps]


def slab_part(value, o, f, frames):
    n = (o * frames + f) * SLAB
    return value[n : n + SLAB]


def temporal_kernel(frames, patches, tick, qkv, near, allowed, spread, heads, second, mod, w_out, attn, branch, third):
    rows, width = second.shape

    def step(at):
        _queries, probs = slab_probs(at, qkv, near, width, allowed, spread, frames, patches)
        weights = dot(jnp.concatenate(probs, 0).astype(bf16), heads[...])
        for f in range(frames):
            total = jnp.zeros((SLAB, width), f32)
            for o in range(5):
                total += slab_part(weights, o, f, frames) * near[f + o, slab_rows(at), width:].astype(f32)
            attn[slab_rows(f * patches + at), :] = total.astype(bf16)

    slabs(patches, step, tick)
    product = dot(attn[...], w_out[...])
    branch[...] = product.astype(bf16)
    third[...] = second[...] + mod[5:6, :] * product


def temporal_back_kernel(wide, frames, patches, tick, gradient, qkv, near, allowed, spread, heads, mod, w_out, attn,
                         branch, g_out, d_qkv, d_gate, d_branch, d_attn, edges, arrived, sems):
    rows, width = gradient.shape
    scale = (width // HEADS) ** -0.5
    halo = Halo(Place(wide), sems)
    d_gate[...] = gate_back(rows, gradient, branch, mod[5:6, :], d_branch)
    tick()
    d_attn[...] = dot(d_branch[...], w_out[...], NT).astype(bf16)
    tick()

    def step(at):
        queries, probs = slab_probs(at, qkv, near, width, allowed, spread, frames, patches)
        grads = [d_attn[slab_rows(f * patches + at), :].astype(f32) for f in range(frames)]
        products = jnp.concatenate(
            [grads[f] * near[f + o, slab_rows(at), width:].astype(f32) for o in range(5) for f in range(frames)], 0
        )
        every = head_sums(products, spread[...])
        size = frames * SLAB
        d_probs = [every[o * size : (o + 1) * size] for o in range(5)]
        inner = functools.reduce(jnp.add, [p * d for p, d in zip(probs, d_probs)])
        d_scores = [p * (d - inner) * scale for p, d in zip(probs, d_probs)]
        wide_scores = dot(jnp.concatenate(d_scores, 0).astype(bf16), heads[...])
        wide_probs = dot(jnp.concatenate(probs, 0).astype(bf16), heads[...])
        for f in range(frames):
            total = jnp.zeros((SLAB, width), f32)
            for o in range(5):
                total += slab_part(wide_scores, o, f, frames) * near[f + o, slab_rows(at), :width].astype(f32)
            d_qkv[slab_rows(f * patches + at), :width] = total.astype(bf16)
        for g in range(frames + 4):
            pairs = [(g - f, f) for f in range(frames) if 0 <= g - f < 5]
            d_keys = functools.reduce(jnp.add, [slab_part(wide_scores, o, f, frames) * queries[f] for o, f in pairs])
            d_values = functools.reduce(jnp.add, [slab_part(wide_probs, o, f, frames) * grads[f] for o, f in pairs])
            if 2 <= g < frames + 2:
                here = slab_rows((g - 2) * patches + at)
                d_qkv[here, width : 2 * width] = d_keys.astype(bf16)
                d_qkv[here, 2 * width :] = d_values.astype(bf16)
            else:
                here = slab_rows((g if g < 2 else g - frames) * patches + at)
                edges[here, :width] = d_keys.astype(bf16)
                edges[here, width:] = d_values.astype(bf16)

    slabs(patches, step, tick)
    edge = 2 * patches
    sends = [halo.copy(0, edges.at[edge:, :], arrived.at[:edge, :]), halo.copy(1, edges.at[:edge, :], arrived.at[edge:, :])]
    for copy in sends:
        copy.start()
    tick()
    g_out[...] = dot(attn[...], d_branch[...], TN).astype(bf16)
    tick()
    tick.finish()
    for n, copy in enumerate(sends):
        copy.wait_recv()
        base = 0 if n == 0 else rows - edge

        def add(at, _, n=n, base=base):
            here = slab_rows(base + at.start)
            there = slab_rows(n * edge + at.start)
            d_qkv[here, width:] = (d_qkv[here, width:].astype(f32) + arrived[there, :].astype(f32)).astype(bf16)
            return 0

        row_blocks(edge, 16, add)
        tick()
    for copy in sends:
        copy.wait_send()


def temporal_rows_kernel(tick, gradient, second, mod, d_qkv, normed, w_qkv, gradient_out, g_qkv, d_mod, d_normed):
    rows, width = gradient.shape
    for c in range(0, 3 * width, width):
        g_qkv[:, c : c + width] = dot(normed[...], d_qkv[:, c : c + width], TN).astype(bf16)
        tick()
    d_normed[...] = dot(d_qkv[...], w_qkv[...], NT)
    tick()

    def add_to(at, value):
        gradient_out[at, :] = gradient[at, :] + value

    d_mod[0:1, :], d_mod[1:2, :] = back_norm(
        rows, lambda at: second[at, :], 1.0 + mod[4:5, :], d_normed, add_to, None)


def gelu_both(value):
    c = math.sqrt(2.0 / math.pi)
    square = value * value
    tanh = jnp.tanh(c * (value + 0.044715 * value * square))
    half = 0.5 * (1.0 + tanh)
    slope = half + 0.5 * value * (1.0 - tanh * tanh) * (c * (1.0 + 3 * 0.044715 * square))
    return value * half, slope


def mlp_kernel(tick, third, cotangent, mod, w_up, w_down, block_out, gradient, g_up, g_down, d_mod,
               normed, d_branch, hidden, d_act, act, d_hidden, branch, up, down, gu, gd, load, store):
    rows, width = third.shape
    count = w_up.shape[1] // width

    def loads(j):
        cols = pl.ds(j * width, width)
        return [pltpu.make_async_copy(w_up.at[:, cols], up.at[j % 2], load.at[0, j % 2]),
                pltpu.make_async_copy(w_down.at[cols, :], down.at[j % 2], load.at[1, j % 2])]

    def stores(j):
        cols = pl.ds(j * width, width)
        return (lambda: pltpu.make_async_copy(gu, g_up.at[:, cols], store.at[0]),
                lambda: pltpu.make_async_copy(gd, g_down.at[cols, :], store.at[1]))

    for copy in loads(0):
        copy.start()

    def norm(at, _):
        hat, _unused = normal(third[at, :])
        normed[at, :] = (hat * (1.0 + mod[7:8, :]) + mod[6:7, :]).astype(bf16)
        d_branch[at, :] = (mod[8:9, :] * cotangent[at, :].astype(f32)).astype(bf16)
        return 0

    row_blocks(rows, 16, norm, unroll=3)

    def activate(at, _):
        value, slope = gelu_both(hidden[at, :])
        act[at, :] = value.astype(bf16)
        d_hidden[at, :] = (slope * d_act[at, :]).astype(bf16)
        return 0

    d_normed = gradient
    for j in range(count):
        b = j % 2
        if j + 1 < count:
            for copy in loads(j + 1):
                copy.start()
        for copy in loads(j):
            copy.wait()
        hidden[...] = dot(normed[...], up[b])
        tick()
        d_act[...] = dot(d_branch[...], down[b], NT)
        tick()
        row_blocks(rows, 16, activate, unroll=3)
        if j > 0:
            for copy in stores(j - 1):
                copy().wait()
        gu[...] = dot(normed[...], d_hidden[...], TN).astype(bf16)
        stores(j)[0]().start()
        tick()
        gd[...] = dot(act[...], d_branch[...], TN).astype(bf16)
        stores(j)[1]().start()
        tick()
        if j == 0:
            branch[...] = dot(act[...], down[b])
            tick()
            d_normed[...] = dot(d_hidden[...], up[b], NT)
        else:
            branch[...] += dot(act[...], down[b])
            tick()
            d_normed[...] += dot(d_hidden[...], up[b], NT)
        tick()
    gate_row = mod[8:9, :]

    def last(at, total):
        value = branch[at, :]
        block_out[at, :] = (third[at, :] + gate_row * value).astype(bf16)
        return total + (cotangent[at, :].astype(f32) * value).reshape(2, 8, width).sum(0)

    d_mod[2:3, :] = jnp.sum(row_blocks(rows, 16, last, jnp.zeros((8, width), f32)), 0, keepdims=True)
    tick()

    def add_to(at, value):
        gradient[at, :] = cotangent[at, :].astype(f32) + value

    d_mod[0:1, :], d_mod[1:2, :] = back_norm(rows, lambda at: third[at, :], 1.0 + mod[7:8, :], d_normed, add_to, None)
    for copy in stores(count - 1):
        copy().wait()


class Place:
    def __init__(self, wide):
        self.wide = wide
        self.chips = wide // 2
        self.plane = lax.axis_index("narrow")
        self.index = lax.axis_index("wide")
        self.core = lax.rem(self.index, 2)
        chip = lax.div(self.index, 2)
        odd = lax.rem(chip, 2)
        half = lax.div(chip, 2)
        self.pos = (1 - odd) * half + odd * (self.chips - 1 - half)

    def chip(self, step):
        n = self.chips
        q = lax.rem(self.pos + (step % n), n)
        high = lax.div(q, n // 2)
        return (1 - high) * (2 * q) + high * (2 * (n - q) - 1)

    def member(self, step, core=None):
        return 2 * self.chip(step) + (self.core if core is None else core)

    def near(self):
        return ((self.plane, self.member(1)), (self.plane, self.member(-1)),
                (1 - self.plane, self.index), (self.plane, self.index + 1 - 2 * self.core))

    def beside(self):
        n = self.wide
        return ((self.plane, lax.rem(self.index + 1, n)), (self.plane, lax.rem(self.index + n - 1, n)))

def greet(devices):
    barrier = pltpu.get_barrier_semaphore()
    for device in devices:
        pl.semaphore_signal(barrier, inc=1, device_id=device, device_id_type=MESH)
    pl.semaphore_wait(barrier, len(devices))

def remote(src, dst, send, recv, device):
    return pltpu.make_async_remote_copy(src_ref=src, dst_ref=dst, send_sem=send, recv_sem=recv,
                                        device_id=device, device_id_type=MESH)

def lanes(start, size):
    return pl.ds(pl.multiple_of(start, 128), size)

def gather_scratch(wide, count):
    chips = wide // 2; reach = chips // 2
    return [DMA((count, 2, reach, 2)), DMA((count, 2, reach, 2)), DMA((count, chips - 1)), DMA((count, chips - 1)),
            DMA((count, chips)), DMA((count, chips)), DMA((count,))]

class Sends:
    def __init__(self):
        self.made = []

    def go(self, make, *args):
        make(*args).start()
        self.made.append((make, args))

    def close(self):
        for make, args in self.made:
            make(*args).wait_send()


def pieces_of(arrays):
    found = []
    for n, a in enumerate(arrays):
        rows, width = a.shape[-2:]
        row_step = 96 if rows % 96 == 0 else rows
        col_step = 1152 if width % 1152 == 0 else width
        found += [(n, r, row_step, c, col_step) for r in range(0, rows, row_step) for c in range(0, width, col_step)]
    return found


def gather_steps(place, own, full, sems, pieces):
    ring_s, ring_r, side_s, side_r, twin_s, twin_r, loc = sems
    count = len(pieces)
    chips = place.chips
    reach = chips // 2
    right, left, across, twin = range(4)
    y = place.plane
    sends = Sends()

    def here(i, part=None):
        n, r, rows, c, width = pieces[i]
        a = width // 3
        if part is None:
            return own[n].at[pl.ds(r, rows), pl.ds(c, width)]
        start, size = ((y * (width - a), a), (a, width - 2 * a), ((1 - y) * (width - a), a))[part]
        return own[n].at[pl.ds(r, rows), lanes(c + start, size)]

    def there(i, j, part=None):
        n, r, rows, c, width = pieces[i]
        a = width // 3
        if part is None:
            return full[n].at[j, pl.ds(r, rows), pl.ds(c, width)]
        start, size = ((y * (width - a), a), (a, width - 2 * a), ((1 - y) * (width - a), a))[part]
        return full[n].at[j, pl.ds(r, rows), lanes(c + start, size)]

    def ring(i, d, s, part, step):
        ref = there(i, place.member(step), part)
        return remote(
            here(i, part) if step == 0 else ref, ref, ring_s.at[i, d, s - 1, part], ring_r.at[i, d, s - 1, part],
            place.near()[d],
        )

    def side(i, slot, step, part):
        ref = there(i, place.member(step), part)
        return remote(ref, ref, side_s.at[i, slot], side_r.at[i, slot], place.near()[across])

    def core_copy(i, slot, step, core=None):
        ref = there(i, place.member(step, core))
        return remote(here(i) if step == 0 and core is None else ref, ref, twin_s.at[i, slot], twin_r.at[i, slot],
                      place.near()[twin])

    def local(i):
        return pltpu.make_async_copy(here(i), there(i, place.index), loc.at[i])

    for part in (0, 1):
        for i in range(count):
            for d in (0, 1):
                sends.go(ring, i, d, 1, part, 0)
    for i in range(count):
        local(i).start()
        sends.go(core_copy, i, chips - 1, 0)
    yield

    def shards(s):
        if s == reach:
            return [(2 * s - 2, s)]
        return [(2 * s - 2, -s), (2 * s - 1, s)]

    def finish(s, i):
        for slot, step in shards(s):
            side(i, slot, step, 2).wait_recv()
            sends.go(core_copy, i, slot, step)

    for s in range(1, reach + 1):
        for i in range(count):
            for part in (0, 1):
                for d in (0, 1):
                    if s == reach and part != d:
                        continue
                    step = -s if d == 0 else s
                    ring(i, d, s, part, step).wait_recv()
                    if s + 1 < reach or (s + 1 == reach and part == d):
                        sends.go(ring, i, d, s + 1, part, step)
                    if part == 0:
                        sends.go(side, i, 2 * s - 2 + (0 if s == reach else d), step, 0)
            if s > 1:
                finish(s - 1, i)
            yield
    for i in range(count):
        finish(reach, i)
        yield
    for i in range(count):
        for s in range(1, reach + 1):
            for slot, step in shards(s):
                core_copy(i, slot, step, 1 - place.core).wait_recv()
        core_copy(i, chips - 1, 0, 1 - place.core).wait_recv()
        local(i).wait()
    sends.close()


def scatter_scratch(wide, shapes):
    chips = wide // 2; reach = chips // 2; count = len(shapes)
    bufs = []
    for rows, width in shapes:
        bufs += [pltpu.VMEM((chips, rows, width), bf16),
                 pltpu.VMEM((chips, rows, width), bf16),
                 pltpu.VMEM((chips, rows, 2 * (width // 9)), bf16),
                 pltpu.VMEM((2, reach, rows, width - 2 * (width // 9)), bf16),
                 pltpu.VMEM((rows, width), bf16)]
    sems = [DMA((count, chips)), DMA((count, chips)), DMA((count, chips)), DMA((count, chips)), DMA((count, chips)),
            DMA((count, 2, reach)), DMA((count, 2, reach)), DMA((count,)), DMA((count,))]
    return bufs + sems

def scatter_steps(place, parts, outs, bufs, sems, pieces):
    load, twin_s, twin_r, side_s, side_r, ring_s, ring_r, last_s, last_r = sems
    count = len(pieces)
    chips = place.chips
    reach = chips // 2
    right, left, across, twin = range(4)
    y = place.plane
    other = 1 - place.core
    sends = Sends()
    go = sends.go
    own = [bufs[5*i] for i in range(count)]; tw = [bufs[5*i+1] for i in range(count)]
    sd = [bufs[5*i+2] for i in range(count)]; rg = [bufs[5*i+3] for i in range(count)]; lt = [bufs[5*i+4] for i in range(count)]
    steps = [reach] + [x for s in range(reach - 1, 0, -1) for x in (s, -s)] + [0]
    slot_of = {s: k for k, s in enumerate(steps)}
    slot_of[-reach] = slot_of[reach]
    w = [o.shape[-1] // 9 for o in own]
    def ringcols(i, d, s):
        base = y * 2 * w[i]
        if s > 1: return base, 7 * w[i]
        k = 4 if (d + i) % 2 == 0 else 3
        return (base, 4 * w[i]) if k == 4 else (base + 4 * w[i], 3 * w[i])
    def taken(i, j):
        n, r, rows, col, width = pieces[i]
        return parts[n].at[j, pl.ds(r, rows), pl.ds(col, width)]
    def twin_copy(i, k):
        return remote(taken(i, place.member(steps[k], other)), tw[i].at[k], twin_s.at[i, k], twin_r.at[i, k], place.near()[twin])
    def load_copy(i, k):
        return pltpu.make_async_copy(taken(i, place.member(steps[k])), own[i].at[k], load.at[i, k])
    def side(i, k):
        return remote(own[i].at[k, :, lanes((1 - y) * 7 * w[i], 2 * w[i])], sd[i].at[k], side_s.at[i, k], side_r.at[i, k], place.near()[across])
    def ring(i, d, s):
        start, size = ringcols(i, d, s)
        k = slot_of[(reach + 1 - s) if d == 0 else -(reach + 1 - s)]
        return remote(own[i].at[k, :, lanes(start, size)], rg[i].at[d, s-1, :, lanes(start - y * 2 * w[i], size)],
                      ring_s.at[i, d, s-1], ring_r.at[i, d, s-1], place.near()[d])
    def last(i):
        sl = lanes(y * 2 * w[i], 7 * w[i])
        return remote(own[i].at[slot_of[0], :, sl], lt[i].at[:, sl], last_s.at[i], last_r.at[i], place.near()[across])
    def add(i, dst_k, start, src, src_start, pieces):
        def one(t, _):
            to = lanes(start + t * w[i], w[i])
            value = own[i][dst_k, :, to].astype(f32)
            value += src[:, lanes(src_start + t * w[i], w[i])].astype(f32)
            own[i][dst_k, :, to] = value.astype(bf16)
            return 0
        lax.fori_loop(0, pieces, one, 0)
    for k in range(chips):
        for i in range(count):
            go(twin_copy, i, k); load_copy(i, k).start()
    yield
    def pair(k):
        for i in range(count):
            load_copy(i, k).wait(); twin_copy(i, k).wait_recv()
            add(i, k, 0, tw[i].at[k], 0, 9)
            go(side, i, k)
    def planes(k):
        for i in range(count):
            side(i, k).wait_recv()
            add(i, k, y * 7 * w[i], sd[i].at[k], 0, 2)
    def ring_in(i, d, s):
        ring(i, d, s).wait_recv()
        start, size = ringcols(i, d, s)
        t = reach - s
        add(i, slot_of[t if d == 0 else -t], start, rg[i].at[d, s-1], start - y * 2 * w[i], size // w[i])
    def need(s):
        far = reach + 1 - s
        return [slot_of[far]] if s == 1 or far == 0 else [slot_of[far], slot_of[-far]]
    done = 0
    for s in range(1, reach + 1):
        ready = need(s)
        while done < min(chips, max(ready) + 3):
            pair(done); done += 1
            yield
        for k in ready: planes(k)
        yield
        for i in range(count):
            for d in (0, 1):
                if s > 1: ring_in(i, d, s - 1)
                go(ring, i, d, s)
            yield
    while done < chips:
        pair(done); done += 1
    planes(slot_of[0])
    yield
    for i in range(count):
        for d in (0, 1): ring_in(i, d, reach)
        go(last, i)
        yield
    for i in range(count):
        last(i).wait_recv()
        k = slot_of[0]
        n, r, rows, col, width = pieces[i]
        mine, theirs = y * 7 * w[i], (1 - y) * 7 * w[i]
        for t in range(2):
            a, b = t * w[i] + mine, t * w[i] + theirs
            outs[n][pl.ds(r, rows), lanes(col + a, w[i])] = own[i][k, :, lanes(a, w[i])]
            outs[n][pl.ds(r, rows), lanes(col + b, w[i])] = lt[i][:, lanes(b, w[i])]
        for t in range(2, 7):
            at = pl.ds(t * w[i], w[i])
            outs[n][pl.ds(r, rows), pl.ds(col + t * w[i], w[i])] = (
                own[i][k, :, at].astype(f32) + lt[i][:, at].astype(f32)
            ).astype(bf16)
        yield
    sends.close()


def peers(place):
    n = place.wide
    return [(t, lax.rem(place.index + t, n)) for t in range(1, n)]


class Exchange:
    def __init__(self, place, parts, inbox, every, sems):
        self.place, self.parts, self.inbox, self.every = place, parts, inbox, every
        self.sems = sems
        self.sends = Sends()

    @staticmethod
    def scratch(wide, block, dtype):
        return [pltpu.VMEM((wide,) + block, dtype)] + [DMA((wide,))] * 4

    def device(self, t):
        return lax.rem(self.place.index + t, self.place.wide)

    def out(self, t):
        j = self.device(t)
        return remote(self.parts.at[j], self.inbox.at[t], self.sems[0].at[t], self.sems[1].at[t], (self.place.plane, j))

    def back(self, t, own):
        block = self.place.index if own else self.device(self.place.wide - t)
        ref = self.every.at[block]
        return remote(ref, ref, self.sems[2].at[t], self.sems[3].at[t], (self.place.plane, self.device(t)))

    def send(self):
        for t in range(1, self.place.wide):
            self.sends.go(self.out, t)

    def total(self):
        value = self.parts[self.place.index].astype(f32)
        for t in range(1, self.place.wide):
            self.out(t).wait_recv()
            value += self.inbox[t].astype(f32)
        return value

    def spread(self, value):
        self.every[self.place.index] = value.astype(self.every.dtype)
        for t in range(1, self.place.wide):
            self.sends.go(self.back, t, True)

    def arrive(self):
        for t in range(1, self.place.wide):
            self.back(t, False).wait_recv()

    def close(self):
        self.sends.close()


class Ring:
    def __init__(self, place, parts, every, scratch):
        self.place, self.parts, self.every = place, parts, every
        self.twin, self.inbox, self.outbox = scratch[:3]
        self.sems = scratch[3:]
        self.sends = Sends()

    @staticmethod
    def scratch(wide, block):
        chips = wide // 2
        reach = chips // 2
        return [pltpu.VMEM((chips,) + block, bf16), pltpu.VMEM((2, reach) + block, bf16),
                pltpu.VMEM((2, reach) + block, bf16), DMA((2,)), DMA((2, reach)), DMA((2, reach)),
                DMA((2,)), DMA((2, reach)), DMA((2, reach))]

    def go(self, make, *args):
        self.sends.go(make, *args)

    def reaches(self):
        half = self.place.chips // 2
        return (half, half - 1)

    def value(self, step):
        chip = self.place.chip(step)
        return self.parts[chip, self.place.core].astype(f32) + self.twin[chip].astype(f32)

    def pair(self):
        twin = self.place.near()[3]
        return remote(self.parts.at[:, 1 - self.place.core], self.twin, self.sems[0].at[0], self.sems[0].at[1], twin)

    def hop(self, d, s):
        return remote(self.outbox.at[d, s - 1], self.inbox.at[d, s - 1], self.sems[1].at[d, s - 1],
                      self.sems[2].at[d, s - 1], self.place.near()[d])

    def sum_steps(self):
        self.go(self.pair)
        yield
        self.pair().wait_recv()
        reaches = self.reaches()
        for s in range(1, max(reaches) + 1):
            for d in (0, 1):
                if s > reaches[d]:
                    continue
                step = reaches[d] + 1 - s
                total = self.value(step if d == 0 else -step)
                if s > 1:
                    self.hop(d, s - 1).wait_recv()
                    total += self.inbox[d, s - 2].astype(f32)
                self.outbox[d, s - 1] = total.astype(bf16)
                self.go(self.hop, d, s)
            yield
        self.total = self.value(0)
        for d in (0, 1):
            self.hop(d, reaches[d]).wait_recv()
            self.total += self.inbox[d, reaches[d] - 1].astype(f32)

    def spread(self, d, s, step):
        ref = self.every.at[self.place.chip(step), self.place.core]
        return remote(ref, ref, self.sems[4].at[d, s - 1], self.sems[5].at[d, s - 1], self.place.near()[d])

    def halves(self, own):
        ref = self.every.at[:, self.place.core if own else 1 - self.place.core]
        return remote(ref, ref, self.sems[3].at[0], self.sems[3].at[1], self.place.near()[3])

    def spread_steps(self, value):
        reaches = self.reaches()
        core = self.place.core
        self.every[self.place.chip(0), core] = value.astype(bf16)
        for d in (0, 1):
            self.go(self.spread, d, 1, 0)
        yield
        for s in range(1, max(reaches) + 1):
            for d in (0, 1):
                if s > reaches[d]:
                    continue
                step = -s if d == 0 else s
                self.spread(d, s, step).wait_recv()
                if s < reaches[d]:
                    self.go(self.spread, d, s + 1, step)
            yield
        self.go(self.halves, True)
        yield
        self.halves(False).wait_recv()

    def close(self):
        self.sends.close()


def by_chip(value):
    return value.reshape((value.shape[0] // 2, 2) + value.shape[1:])


def front_steps(modulation, text, prompt):
    modulation.send()
    yield from text.sum_steps()
    prompt[...] = text.total.astype(bf16)
    modulation.spread(modulation.total())
    yield
    modulation.arrive()
    modulation.close()
    text.close()


def text_steps(keys, prompt, kv_cols):
    def block(j, _):
        for core in (0, 1):
            keys.parts[j, core] = dot(kv_cols[j, core], prompt[...]).astype(bf16)
        return 0

    lax.fori_loop(0, keys.place.chips, block, 0)
    yield from keys.sum_steps()
    yield from keys.spread_steps(keys.total)
    keys.close()


def text_back_steps(keys, prompts, kv_rows, sems):
    place = keys.place

    def over(ref, k, own):
        half = ref.at[place.plane if own else 1 - place.plane]
        return remote(half, half, sems.at[k, 0], sems.at[k, 1], place.near()[2])

    yield from keys.sum_steps()
    yield from keys.spread_steps(keys.total)
    over(keys.both, 0, True).start()

    def block(j, total):
        for core in (0, 1):
            total += dot(kv_rows[j, core], keys.every[j, core])
        return total

    rows = lax.fori_loop(0, place.chips, block, jnp.zeros(prompts.every.shape[2:], f32))
    yield from prompts.spread_steps(rows)
    over(prompts.both, 1, True).start()
    yield
    for k, part in ((0, keys), (1, prompts)):
        over(part.both, k, False).wait_recv()
        over(part.both, k, True).wait_send()
        part.close()


def vector_steps(vectors, sems):
    place = vectors.place
    vectors.send()
    yield
    vectors.spread(vectors.total())
    yield
    vectors.arrive()

    def over(own):
        half = vectors.both.at[place.plane if own else 1 - place.plane]
        return remote(half, half, sems.at[0], sems.at[1], place.near()[2])

    over(True).start()
    yield
    over(False).wait_recv()
    over(True).wait_send()
    vectors.close()


def together(generators):
    running = list(generators)
    while running:
        for one in list(running):
            if next(one, running) is running:
                running.remove(one)
        yield


MOST_CHIPS = 8


class Gather:
    direct = False

    def __init__(self, wide, arrays):
        self.inputs = [(a, ANY) for a in arrays]
        self.outputs = [(((wide,) + a.shape, a.dtype), ANY) for a in arrays]
        self.arrays = arrays
        self.pieces = pieces_of(arrays)
        self.scratch = gather_scratch(wide, len(self.pieces))

    def steps(self, place, ins, outs, scratch):
        return gather_steps(place, ins, outs, scratch, self.pieces)

    def plain(self):
        return [lax.all_gather(a, "wide") for a in self.arrays]


class Scatter:
    direct = False

    def __init__(self, wide, arrays):
        self.arrays = arrays
        self.pieces = pieces_of(arrays)
        self.inputs = [(a, ANY) for a in arrays]
        self.outputs = [((a.shape[1:], bf16), VM) for a in arrays]
        self.scratch = scatter_scratch(wide, [(p[2], p[4]) for p in self.pieces])

    def steps(self, place, ins, outs, scratch):
        buffers = 5 * len(self.pieces)
        return scatter_steps(place, ins, outs, scratch[:buffers], scratch[buffers:], self.pieces)

    def plain(self):
        sums = [lax.psum_scatter(a.astype(f32), "wide") for a in self.arrays]
        return [lax.psum(a, "narrow").astype(bf16) for a in sums]


class Front:
    direct = True

    def __init__(self, wide, mod_parts, text_parts):
        self.inputs = [(mod_parts, VM), (by_chip(text_parts), VM)]
        self.outputs = [((mod_parts.shape, f32), VM), ((text_parts.shape[1:], bf16), VM)]
        self.scratch = Exchange.scratch(wide, mod_parts.shape[1:], f32) + Ring.scratch(wide, text_parts.shape[1:])

    def steps(self, place, ins, outs, scratch):
        modulation = Exchange(place, ins[0], scratch[0], outs[0], scratch[1:5])
        return front_steps(modulation, Ring(place, ins[1], None, scratch[5:]), outs[1])

    def plain(self):
        mod_parts, text_parts = (value for value, _ in self.inputs)
        rows = text_parts.reshape((-1,) + text_parts.shape[2:]).astype(f32)
        return [lax.psum(mod_parts, "wide"), lax.psum_scatter(rows, "wide").astype(bf16)]


class Text:
    direct = False

    def __init__(self, wide, prompt, kv_cols):
        block = (kv_cols.shape[1], prompt.shape[1])
        self.inputs = [(prompt, VM), (by_chip(kv_cols), VM)]
        self.outputs = [(((wide // 2, 2) + block, bf16), VM)]
        self.scratch = [pltpu.VMEM((wide // 2, 2) + block, bf16)] + Ring.scratch(wide, block)

    def steps(self, place, ins, outs, scratch):
        return text_steps(Ring(place, scratch[0], outs[0], scratch[1:]), ins[0], ins[1])

    def plain(self):
        prompt, kv_cols = (value for value, _ in self.inputs)
        product = lax.dot_general(kv_cols, prompt, (((3,), (0,)), ((), ())), preferred_element_type=f32)
        return [lax.psum(product, "wide").astype(bf16)]


class TextBack:
    direct = False

    def __init__(self, wide, kv_parts, kv_rows):
        chips = (wide // 2, 2)
        kv_block, block = kv_parts.shape[1:], (kv_rows.shape[1], kv_parts.shape[2])
        self.inputs = [(by_chip(kv_parts), VM), (by_chip(kv_rows), VM)]
        self.outputs = [(((2,) + chips + kv_block, bf16), VM), (((2,) + chips + block, bf16), VM)]
        self.scratch = Ring.scratch(wide, kv_block) + Ring.scratch(wide, block) + [DMA((2, 2))]

    def steps(self, place, ins, outs, scratch):
        keys = Ring(place, ins[0], outs[0].at[place.plane], scratch[:9])
        keys.both = outs[0]
        prompts = Ring(place, None, outs[1].at[place.plane], scratch[9:18])
        prompts.both = outs[1]
        return text_back_steps(keys, prompts, ins[1], scratch[18])

    def plain(self):
        kv_parts, kv_rows = (value for value, _ in self.inputs)
        every = lax.psum(kv_parts.astype(f32), "wide").astype(bf16)
        rows = jnp.einsum("jcrk,jckt->rt", kv_rows, every, preferred_element_type=f32).astype(bf16)
        return [lax.all_gather(every, "narrow"), lax.all_gather(by_chip(lax.all_gather(rows, "wide")), "narrow")]


class Vectors:
    direct = True

    def __init__(self, wide, parts):
        self.inputs = [(parts, VM)]
        self.outputs = [(((2,) + parts.shape, f32), VM)]
        self.scratch = Exchange.scratch(wide, parts.shape[1:], f32) + [DMA((2,))]

    def steps(self, place, ins, outs, scratch):
        vectors = Exchange(place, ins[0], scratch[0], outs[0].at[place.plane], scratch[1:5])
        vectors.both = outs[0]
        return vector_steps(vectors, scratch[5])

    def plain(self):
        return [lax.all_gather(lax.psum(self.inputs[0][0], "wide"), "narrow")]


class Pump:
    def __init__(self, steps, pace):
        self.steps, self.pace = steps, pace
        self.ended = False
        self.calls = self.rounds = 0

    def __call__(self):
        self.calls += 1
        for _ in range(self.pace):
            if not self.ended:
                self.ended = next(self.steps, self) is self
                self.rounds += 1

    def inside(self, index, low, high):
        for n in range(low, high):
            if not self.ended:
                pl.when(index == n)(lambda: self())

    def finish(self):
        while not self.ended:
            self()


def take(refs, *counts):
    found, at = [], 0
    for count in counts:
        found.append(refs[at : at + count])
        at += count
    return found


def fused_kernel(wide, talks, compute, counts, parts, pace, *refs):
    sizes = list(counts) + [n for p in parts for n in (len(p.inputs), len(p.outputs), len(p.scratch))]
    order = [0] + [3 + 3 * i for i in range(len(parts))]
    order += [1] + [4 + 3 * i for i in range(len(parts))]
    order += [2] + [5 + 3 * i for i in range(len(parts))]
    found = dict(zip(order, take(refs, *[sizes[i] for i in order])))
    if talks:
        place = Place(wide)
        greet(all_near(place) if any(p.direct for p in parts) else place.near() + place.beside())
        running = together(
            [p.steps(place, found[3 + 3 * i], found[4 + 3 * i], found[5 + 3 * i]) for i, p in enumerate(parts)]
        )
        pump = Pump(running, pace)
        pump()
    else:
        pump = Pump(iter(()), 1)
    if compute is not None:
        compute(pump, *found[0], *found[1], *found[2])
    pump.finish()


def fused(name, wide, compute, inputs, outputs, scratch, parts=(), pace=1, collective_id=None):
    if wide > 2 * MOST_CHIPS and parts:
        done = [[]] if compute is None else fused(
            name, wide, compute, inputs, outputs, scratch, collective_id=collective_id)
        return done + [part.plain() for part in parts]
    ins = inputs + [x for p in parts for x in p.inputs]
    outs = outputs + [x for p in parts for x in p.outputs]
    talks = collective_id is not None
    options = dict(collective_id=collective_id, has_side_effects=True) if talks else {}
    found = pl.pallas_call(
        functools.partial(fused_kernel, wide, talks, compute, (len(inputs), len(outputs), len(scratch)), parts, pace),
        out_shape=[jax.ShapeDtypeStruct(shape, dtype) for (shape, dtype), _ in outs],
        in_specs=[spec for _, spec in ins],
        out_specs=[spec for _, spec in outs],
        scratch_shapes=scratch + [x for p in parts for x in p.scratch],
        compiler_params=pltpu.CompilerParams(vmem_limit_bytes=LIMIT, **options),
        name=name,
    )(*[value for value, _ in ins])
    return take(found, len(outputs), *[len(p.outputs) for p in parts])


def on_chip(*values):
    return [(value, VM) for value in values]


def all_near(place):
    return [place.near()[2]] + [(place.plane, j) for t, j in peers(place)]


def spatial(wide, frames, patches, x, mod, heads, w_qkv, w_out, **rest):
    rows, width = x.shape
    return fused(
        "spatial", wide, functools.partial(spatial_kernel, frames, patches),
        on_chip(x, mod, heads, w_qkv, w_out),
        on_chip(*[((rows, n * width), d) for n, d in ((1, bf16), (3, bf16), (1, bf16), (1, bf16), (1, f32))]),
        [], **rest,
    )


def spatial_back(wide, frames, patches, gradient, x, mod, heads, w_qkv, w_out, normed, qkv, attn, branch, **rest):
    rows, width = x.shape
    V = pltpu.VMEM
    return fused(
        "spatial_back", wide, functools.partial(spatial_back_kernel, frames, patches),
        on_chip(gradient, x, mod, heads) + [(w_qkv, ANY)] + on_chip(w_out, normed, qkv, attn, branch),
        on_chip(((rows, width), bf16), ((width, 3 * width), bf16), ((width, width), bf16), ((3, width), f32)),
        [V((rows, width), bf16), V((rows, width), bf16), V((rows, 3 * width), bf16),
         V((rows, width), f32), V((2, width, width), bf16), DMA((2,))], **rest,
    )


def cross(wide, frames, patches, first, gain, mod, heads, valid, text_kv, w_q, w_out, w_tqkv, **rest):
    rows, width = first.shape
    return fused(
        "cross", wide, functools.partial(cross_kernel, wide, frames, patches),
        on_chip(first, gain, mod, heads, valid, text_kv, w_q, w_out, w_tqkv),
        on_chip(*[((rows, n * width), d) for n, d in ((1, bf16), (1, bf16), (1, bf16), (1, f32), (1, bf16), (3, bf16))])
        + on_chip(((frames + 4, patches, 2 * width), bf16)),
        [pltpu.VMEM((4 * patches, width), bf16), DMA((2, 2))], **rest,
    )


def cross_back(wide, frames, patches, gradient, first, gain, heads, valid, text_kv, w_q, w_out, normed, query, attn, **rest):
    rows, width = first.shape
    V = pltpu.VMEM
    return fused(
        "cross_back", wide, functools.partial(cross_back_kernel, frames, patches),
        on_chip(gradient, first, gain, heads, valid, text_kv, w_q, w_out, normed, query, attn),
        on_chip(((rows, width), f32), ((width, width), bf16), ((width, width), bf16), ((1, width), f32), (text_kv.shape, f32)),
        [V((rows, width), bf16)] * 3 + [V((rows, width), f32)], **rest,
    )


def temporal(wide, frames, patches, qkv, near, allowed, spread, heads, second, mod, w_out, **rest):
    rows, width = second.shape
    return fused(
        "temporal", wide, functools.partial(temporal_kernel, frames, patches),
        on_chip(qkv, near, allowed, spread, heads, second, mod, w_out),
        on_chip(((rows, width), bf16), ((rows, width), bf16), ((rows, width), f32)), [], **rest,
    )


def temporal_back(wide, frames, patches, gradient, qkv, near, allowed, spread, heads, mod, w_out, attn, branch, **rest):
    rows, width = gradient.shape
    V = pltpu.VMEM
    edges = (4 * patches, 2 * width)
    return fused(
        "temporal_back", wide, functools.partial(temporal_back_kernel, wide, frames, patches),
        on_chip(gradient, qkv, near, allowed, spread, heads, mod, w_out, attn, branch),
        on_chip(((width, width), bf16), ((rows, 3 * width), bf16), ((1, width), f32)),
        [V((rows, width), bf16)] * 2 + [V(edges, bf16)] * 2 + [DMA((2, 2))], **rest,
    )


def temporal_rows(wide, gradient, second, mod, d_qkv, normed, w_qkv, **rest):
    rows, width = gradient.shape
    return fused(
        "temporal_rows", wide, temporal_rows_kernel,
        on_chip(gradient, second, mod, d_qkv, normed, w_qkv),
        on_chip(((rows, width), f32), ((width, 3 * width), bf16), ((2, width), f32)),
        [pltpu.VMEM((rows, width), f32)], **rest,
    )


def mlp(wide, third, cotangent, mod, w_up, w_down, **rest):
    rows, width = third.shape
    V = pltpu.VMEM
    return fused(
        "mlp", wide, mlp_kernel,
        on_chip(third, cotangent, mod) + [(w_up, ANY), (w_down, ANY)],
        on_chip(((rows, width), bf16), ((rows, width), f32)) + [((w_up.shape, bf16), ANY), ((w_down.shape, bf16), ANY)]
        + on_chip(((3, width), f32)),
        [V((rows, width), bf16)] * 2 + [V((rows, width), f32)] * 2 + [V((rows, width), bf16)] * 2
        + [V((rows, width), f32)] + [V((2, width, width), bf16)] * 2 + [V((width, width), bf16)] * 2
        + [DMA((2, 2)), DMA((2,))], **rest,
    )


def time_embed(steps, model_width):
    half_width = model_width // 2
    freqs = jnp.exp(-math.log(10000.0) * jnp.arange(half_width, dtype=jnp.float32) / half_width)
    angles = steps.astype(jnp.float32)[:, None] * freqs[None, :]
    return jnp.concatenate([jnp.cos(angles), jnp.sin(angles)], -1)


def body(
    hidden,
    cotangent,
    text,
    timesteps,
    seg_ids,
    text_len,
    ada_weight,
    text_weight,
    kv_weight,
    qkv_weight,
    out_weight,
    cross_q_weight,
    cross_out_weight,
    temp_qkv_weight,
    temp_out_weight,
    up_weight,
    down_weight,
    cross_gain,
):
    frames, patches, width = hidden.shape[1:]
    rows = frames * patches
    text_count = text.shape[1]
    plane = lax.axis_index("narrow")
    position = lax.axis_index("wide")
    wide = lax.axis_size("wide")
    rows_model, rows_text = ada_weight.shape[0], text_weight.shape[0]
    head_of = jnp.arange(width) // (width // HEADS)
    heads = (head_of[None, :] == jnp.arange(HEADS)[:, None]).astype(bf16)
    spread = (head_of[:, None] == jnp.arange(HEADS)[None, :]).astype(bf16)

    def swap(value):
        return lax.ppermute(value, "narrow", [(0, 1), (1, 0)])

    def by_plane(own, other):
        return jnp.where(plane == 0, jnp.stack([own, other]), jnp.stack([other, own]))

    def whole(value):
        return value.reshape(-1, value.shape[-1])

    def blocks(value):
        return value.reshape(wide, -1, value.shape[-1])

    signal = jax.nn.silu(time_embed(timesteps, width)[0]).astype(bf16)
    signal_rows = lax.dynamic_slice_in_dim(signal, position * rows_model, rows_model)
    mod_part = dot(signal_rows[None, :], ada_weight)
    prompt_rows = lax.dynamic_slice_in_dim(text[0], position * rows_text, rows_text, 1)
    text_part = dot(text_weight, prompt_rows, (((0,), (1,)), ((), ())))
    kv_cols = blocks(kv_weight.T)
    kv_rows = kv_weight.reshape(rows_model, wide, -1).transpose(1, 0, 2)
    front = Front(wide, mod_part.reshape(wide, 1, -1), blocks(text_part.astype(bf16)))
    _none, (modulation, prompt), (full_qkv, full_out) = fused(
        "start", wide, None, [], [], [], parts=[front, Gather(wide, [qkv_weight, out_weight])], collective_id=0
    )
    full_qkv, full_out = whole(full_qkv), whole(full_out)
    mod = modulation.reshape(9, width)

    tokens = hidden[0].reshape(rows, width)
    (normed_a, qkv_a, attn_a, branch_a, first), (kv_all,), gathered = spatial(
        wide, frames, patches, tokens, mod, heads, full_qkv, full_out, collective_id=1, pace=2,
        parts=[
            Text(wide, prompt, kv_cols),
            Gather(wide, [cross_q_weight, cross_out_weight, temp_qkv_weight, temp_out_weight]),
        ],
    )
    full_cross_q, full_cross_out, full_temp_qkv, full_temp_out = map(whole, gathered)
    text_kv = whole(kv_all).T
    valid = (jnp.arange(text_count) < text_len[0]).astype(f32)[:, None]
    gain = cross_gain[None, :]
    (normed_c, query_c, attn_c, second, normed_t, qkv_t, near), (full_down,) = cross(
        wide, frames, patches, first, gain, mod, heads, valid, text_kv, full_cross_q, full_cross_out, full_temp_qkv,
        parts=[Gather(wide, [down_weight])], collective_id=2,
    )
    clip_pad = jnp.pad(seg_ids[0], 2, constant_values=-1)
    clip_local = lax.dynamic_slice_in_dim(clip_pad, position * frames, frames + 4)
    allowed = jnp.stack(
        [clip_local[offset : offset + frames] == clip_local[2 : frames + 2] for offset in range(5)]
    )
    allowed = jnp.broadcast_to(allowed[:, :, None, None], (5, frames, SLAB, HEADS)).reshape(-1, HEADS).astype(f32)
    (attn_t, branch_t, third), (full_up,) = temporal(
        wide, frames, patches, qkv_t, near, allowed, spread, heads, second, mod, full_temp_out,
        parts=[Gather(wide, [up_weight])], collective_id=3, pace=2,
    )

    upstream = cotangent[0].reshape(rows, width)
    ((block_out, gradient, grad_up, grad_down, d_mod_m),) = mlp(
        wide, third, upstream, mod, whole(full_up), whole(full_down)
    )

    (grad_temp_out, d_qkv_t, d_gate_t), (grad_up,) = temporal_back(
        wide, frames, patches, gradient, qkv_t, near, allowed, spread, heads, mod, full_temp_out, attn_t, branch_t,
        parts=[Scatter(wide, [blocks(grad_up)])], collective_id=4, pace=2,
    )
    (gradient, grad_temp_qkv, d_mod_t), (grad_down,) = temporal_rows(
        wide, gradient, second, mod, d_qkv_t, normed_t, full_temp_qkv,
        parts=[Scatter(wide, [blocks(grad_down)])], collective_id=5, pace=6,
    )
    (gradient, grad_cross_q, grad_cross_out, d_gain, d_text_kv), (grad_temp_qkv, grad_temp_out) = cross_back(
        wide, frames, patches, gradient, first, gain, heads, valid, text_kv,
        full_cross_q, full_cross_out, normed_c, query_c, attn_c,
        parts=[Scatter(wide, [blocks(grad_temp_qkv), blocks(grad_temp_out)])], collective_id=6, pace=2,
    )
    found = spatial_back(
        wide, frames, patches, gradient, tokens, mod, heads, full_qkv, full_out, normed_a, qkv_a, attn_a, branch_a,
        parts=[
            TextBack(wide, blocks(d_text_kv.T.astype(bf16)), kv_rows),
            Scatter(wide, [blocks(grad_cross_q), blocks(grad_cross_out)]),
        ],
        collective_id=7,
    )
    (grad_hidden, grad_qkv, grad_out, d_mod_a), (d_kv_both, d_prompt_both), (grad_cross_q, grad_cross_out) = found
    vectors = jnp.concatenate([d_mod_a, d_mod_t, d_gate_t, d_mod_m, d_gain], 0)
    _none, (vec_both,), (grad_qkv, grad_out) = fused(
        "end", wide, None, [], [], [], collective_id=8,
        parts=[Vectors(wide, vectors.reshape(wide, 1, -1)), Scatter(wide, [blocks(grad_qkv), blocks(grad_out)])],
    )
    vec_both = vec_both.reshape(2, 10, width)

    d_modulation = vec_both[:, :9].reshape(2, 9 * width)
    grad_gain = vec_both[0, 9] + vec_both[1, 9]
    both_signal = by_plane(signal_rows, swap(signal_rows)).astype(f32)
    grad_ada = (
        both_signal[0][:, None] * d_modulation[0][None, :] + both_signal[1][:, None] * d_modulation[1][None, :]
    )
    both_prompt = by_plane(prompt, swap(prompt))
    both_rows = by_plane(prompt_rows, swap(prompt_rows)).reshape(2 * text_count, -1)
    pairs = (((0, 2), (0, 2)), ((), ()))
    grad_kv = lax.dot_general(
        both_prompt, d_kv_both.reshape(2, 2 * width, text_count), pairs, preferred_element_type=f32
    )
    d_prompt = d_prompt_both.reshape(2, width, text_count).transpose(0, 2, 1).reshape(2 * text_count, width)
    grad_text = dot(both_rows, d_prompt, TN)
    shape = (1, frames, patches, width)
    return (
        block_out.reshape(shape),
        grad_hidden.reshape(shape),
        grad_ada,
        grad_text,
        grad_kv,
        grad_qkv.astype(f32),
        grad_out.astype(f32),
        grad_cross_q.astype(f32),
        grad_cross_out.astype(f32),
        grad_temp_qkv.astype(f32),
        grad_temp_out.astype(f32),
        grad_up.astype(f32),
        grad_down.astype(f32),
        grad_gain,
    )


def solution(mesh):
    return jax.shard_map(
        body,
        mesh=mesh,
        in_specs=(
            P("narrow", "wide", None, None),
            P("narrow", "wide", None, None),
            P("narrow", None, None),
            P("narrow"),
            P("narrow", None),
            P("narrow"),
            P("wide", None),
            P("wide", None),
            P("wide", None),
            P("wide", None),
            P("wide", None),
            P("wide", None),
            P("wide", None),
            P("wide", None),
            P("wide", None),
            P("wide", None),
            P("wide", None),
            P(),
        ),
        out_specs=(
            P("narrow", "wide", None, None),
            P("narrow", "wide", None, None),
            P("wide", None),
            P("wide", None),
            P("wide", None),
            P("wide", None),
            P("wide", None),
            P("wide", None),
            P("wide", None),
            P("wide", None),
            P("wide", None),
            P("wide", None),
            P("wide", None),
            P(),
        ),
        check_vma=False,
    )
```

time: 2000 us -> 856 us (0.43)
  waiting for transfers between devices: 1040 us -> 0.01 us
  Pallas kernels: 0 us -> 801 us
  matrix products: 298 us -> 4.89 us
  blocking collectives: 280 us -> 0 us
  local copies, waits for them, and re-layouts: 195 us -> 18.6 us
  other arithmetic: 152 us -> 18.2 us
    pallas_call x0 -> x10, Pallas kernels: none -> 801 us  [fused(): pl.pallas_call(functools.partial(fused_kernel, wide, talks, compute, (len...]
    reduce_scatter x2 -> x0, waiting for transfers between devices: 428 us -> none  [grad_rows(): lax.psum_scatter(project_rows(operand, gradient), 'wide', scatter_dimensi...]
    unnamed x23 -> x0, waiting for transfers between devices: 316 us -> none
    dot_general x42 -> x4, matrix products: 298 us -> 4.89 us  [the longest x3 3.54 us: dot(): return lax.dot_general(a, b, dims, preferred_element_type=jnp.float32)]
    psum x4 -> x0, blocking collectives: 262 us -> none  [the longest x2 158 us: body(): modulation, text_sum = lax.psum((mod_part, text_part), 'wide')]
    all_gather x8 -> x0, waiting for transfers between devices: 169 us -> none  [fetch_rows(): lax.all_gather(shortened(shards), 'wide', axis=0, tiled=True)]
    psum x1 -> x0, waiting for transfers between devices: 122 us -> none  [body(): lax.psum(grad_ada_part.astype(jnp.bfloat16), 'narrow').astype(jnp.float32)]
    unnamed x297 -> x39, local copies, waits for them, and re-layouts: 59.6 us -> 1.18 us
  transfers between devices with their start and end apart: 21 -> 3, of which waited for: 8 -> 0; matrix products, arithmetic and copies ran while one was open for 23% -> 5% of each run, Pallas kernels for 0% -> 94%
where the time goes in v2:
time: 856 us; the launch traced here: 850 us
  Pallas kernels  801 us (94%)
  local copies, waits for them, and re-layouts  18.6 us (2%)
  other arithmetic  18.2 us (2%)
    pallas_call x10, Pallas kernels, fused(): pl.pallas_call(functools.partial(fused_kernel, wide, talks, compute, (len...  801 us
  transfers between devices with their start and end apart: 3, of which 0 were waited for; matrix products, arithmetic and copies ran while one was open for 5% of the time, Pallas kernels for 94%

profile of v2, /device:TPU:0, one launch (start us, length us, event | category | flops | bytes accessed | tf_op | source)
XLA Modules:
  0.0 850.1 jit_solution(7549916837927077042)
XLA Ops:
  1.7 3.0 collective-permute-start
  4.7 5.1 reshape.195
  11.3 1.3 fusion
  13.6 59.5 %start.1 = (f32[16,1,648]{2,1,0:T(1,128)}, bf16[72,128]{1,0:T(8,128)(2,1)}, bf16[16,72,3456]{2,1,0:T(8,128)(2,1)}, bf16[16,72,1152]{2,1,0:T(8,128)(2,1)}) custom-call(f32[16,1,648]{2,1,0:T(1,128)} %dot_general.18.refs_0_, bf16[8,2,72,128]{3,2,1,0:T(8,128)(2,1)} %bitcast.113, bf16[72,3456]{1,0:T(8,128)(2,1)} %refs_2_.1, bf16[72,1152]{1,0:T(8,128)(2,1)} %refs_3_.1), custom_call_target="tpu_custom_call" | custom-call | tf_op jit(solution)/shard_map/start/pallas_call | solution.py:1225
  73.1 1.6 collective-permute-start.2
  80.7 91.3 %spatial.1 = (bf16[624,1152]{1,0:T(8,128)(2,1)}, bf16[624,3456]{1,0:T(8,128)(2,1)}, bf16[624,1152]{1,0:T(8,128)(2,1)}, bf16[624,1152]{1,0:T(8,128)(2,1)}, f32[62...) custom-call(bf16[624,1152]{1,0:T(8,128)(2,1)} %bitcast.97, ...), custom_call_target="tpu_custom_call" | custom-call | tf_op jit(solution)/shard_map/spatial/pallas_call | solution.py:1225
  172.0 2.1 copy.41
  176.4 80.9 %cross.1 = (bf16[624,1152]{1,0:T(8,128)(2,1)}, bf16[624,1152]{1,0:T(8,128)(2,1)}, bf16[624,1152]{1,0:T(8,128)(2,1)}, f32[624,1152]{1,0:T(8,128)}, bf16[624,1152]...) custom-call(f32[624,1152]{1,0:T(8,128)} %get-tuple-element.75.refs_0_.r, ...), custom_call_target="tpu_custom_call" | custom-call | tf_op jit(solution)/shard_map/cross/pallas_call | solution.py:1225
  258.0 66.5 %temporal.1 = (bf16[624,1152]{1,0:T(8,128)(2,1)}, bf16[624,1152]{1,0:T(8,128)(2,1)}, f32[624,1152]{1,0:T(8,128)}, bf16[16,72,4608]{2,1,0:T(8,128)(2,1)}) custom-call(bf16[624,3456]{1,0:T(8,128)(2,1)} %get-tuple-element.80.refs_0_.refs_1_, bf16[7,208,2304]{2,1,0:T(8,128)(2,1)} %get-tuple-element.81.refs_1_.refs_2_, ...), custom_call_target="tpu_custom_call" | custom-call | tf_op jit(solution)/shard_map/temporal/pallas_call | solution.py:1225
  324.5 80.5 %mlp.1 = (bf16[624,1152]{1,0:T(8,128)(2,1)}, f32[624,1152]{1,0:T(8,128)}, bf16[1152,4608]{1,0:T(8,128)(2,1)}, bf16[4608,1152]{1,0:T(8,128)(2,1)}, f32[3,1152]{1,0:T(4,128)}) custom-call(f32[624,1152]{1,0:T(8,128)} %get-tuple-element.84.refs_0_, bf16[624,1152]{1,0:T(8,128)(2,1)} %bitcast.110, f32[9,1152]{1,0:T(8,128)} %reshape.196.refs_1_.refs_2_.refs_6_, ...), custom_call_target="tpu_custom_call" | custom-call | tf_op jit(solution)/shard_map/mlp/pallas_call | solution.py:1225
  405.0 90.4 %temporal_back.1 = (bf16[1152,1152]{1,0:T(8,128)(2,1)}, bf16[624,3456]{1,0:T(8,128)(2,1)}, f32[1,1152]{1,0:T(1,128)}, bf16[72,4608]{1,0:T(8,128)(2,1)}) custom-call(f32[624,1152]{1,0:T(8,128)} %get-tuple-element.88.refs_0_, bf16[624,3456]{1,0:T(8,128)(2,1)} %get-tuple-element.80.refs_0_.refs_1_, bf16[7,208,2304]{2,1,0:T(8,128)(2,1)} %get-tuple-element.81.refs_1_.refs_2_, ...), custom_call_target="tpu_custom_call" | custom-call | tf_op jit(solution)/shard_map/temporal_back/pallas_call | solution.py:1225
  495.3 94.0 %temporal_rows.1 = (f32[624,1152]{1,0:T(8,128)}, bf16[1152,3456]{1,0:T(8,128)(2,1)}, f32[2,1152]{1,0:T(2,128)}, bf16[288,1152]{1,0:T(8,128)(2,1)}) custom-call(f32[624,1152]{1,0:T(8,128)} %get-tuple-element.88.refs_0_, f32[624,1152]{1,0:T(8,128)} %get-tuple-element.82.refs_5_.refs_1_, f32[9,1152]{1,0:T(8,128)} %reshape.196.refs_1_.refs_2_.refs_6_, ...), custom_call_target="tpu_custom_call" | custom-call | tf_op jit(solution)/shard_map/temporal_rows/pallas_call | solution.py:1225
  589.3 78.3 %cross_back.1 = (f32[624,1152]{1,0:T(8,128)}, bf16[1152,1152]{1,0:T(8,128)(2,1)}, bf16[1152,1152]{1,0:T(8,128)(2,1)}, f32[1,1152]{1,0:T(1,128)}, f32[128,2304]{1...) custom-call(f32[624,1152]{1,0:T(8,128)} %get-tuple-element.95.refs_0_, ...), custom_call_target="tpu_custom_call" | custom-call | tf_op jit(solution)/shard_map/cross_back/pallas_call | solution.py:1225
  667.7 1.3 convert_bitcast_fusion
  671.1 96.3 %spatial_back.1 = (bf16[624,1152]{1,0:T(8,128)(2,1)}, bf16[1152,3456]{1,0:T(8,128)(2,1)}, bf16[1152,1152]{1,0:T(8,128)(2,1)}, f32[3,1152]{1,0:T(4,128)}, bf16[2,...) custom-call(f32[624,1152]{1,0:T(8,128)} %get-tuple-element.101.refs_, ...), custom_call_target="tpu_custom_call" | custom-call | tf_op jit(solution)/shard_map/spatial_back/pallas_call | solution.py:1225
  769.1 63.1 %end.1 = (f32[2,16,1,720]{3,2,1,0:T(1,128)}, bf16[72,3456]{1,0:T(8,128)(2,1)}, bf16[72,1152]{1,0:T(8,128)(2,1)}) custom-call(f32[16,1,720]{2,1,0:T(1,128)} %reshape.216.refs_0_, bf16[16,72,3456]{2,1,0:T(8,128)(2,1)} %bitcast.95, bf16[16,72,1152]{2,1,0:T(8,128)(2,1)} %bitcast.102), custom_call_target="tpu_custom_call" | custom-call | tf_op jit(solution)/shard_map/end/pallas_call | solution.py:1225
  832.3 1.2 reduce.2
  834.3 2.1 convert_element_type.90
  836.4 1.7 convert_element_type.91
  841.7 1.1 convert_element_type.97
  842.9 1.2 convert_element_type.96
  844.1 2.0 multiply_add_fusion
  846.1 1.3 convolution_bitcast_fusion
  847.5 1.4 convolution_bitcast_fusion.1
  (86 shorter events, 20.2 us)
Async XLA Ops:
  0.6 10.7 %copy-start = (bf16[1,128,4096]{2,1,0:T(8,128)(2,1)S(1)}, bf16[1,128,4096]{2,1,0:T(8,128)(2,1)}, u32[]{:S(2)}) copy-start(bf16[1,128,4096]{2,1,0:T(8,128)(2,1)} %param.20) | copy-start | bytes 3145732
  1.7 842.4 %collective-permute-start = (bf16[72]{0:T(256)(128)(2,1)S(1)}, bf16[72]{0:T(256)(128)(2,1)S(1)}, u32[]{:S(2)}, u32[]{:S(2)}) collective-permute-start(bf16[72]{0:T(256)(128)(2,1)S(1)} %fusion.27), channel_id=1, source_target_pairs={{0,16},{16,0},{1,17},{17,1},{2,18},{18,2},{3,19},{19,3},{4,20},{20... | collective-permute-start | bytes 440 | tf_op jit(solution)/shard_map/ppermute | solution.py:1373
  9.8 68.8 %copy-start.3 = (bf16[72,2304]{1,0:T(8,128)(2,1)S(1)}, bf16[72,2304]{1,0:T(8,128)(2,1)}, u32[]{:S(2)}) copy-start(bf16[72,2304]{1,0:T(8,128)(2,1)} %param.26) | copy-start | bytes 995332
  73.1 773.0 %collective-permute-start.2 = (bf16[72,128]{1,0:T(8,128)(2,1)}, bf16[72,128]{1,0:T(8,128)(2,1)S(1)}, u32[]{:S(2)}, u32[]{:S(2)}) collective-permute-start(bf16[72,128]{1,0:T(8,128)(2,1)} %get-tuple-element.74.refs_5_), channel_id=1, source_target_pairs={{0,16},{16,0},{1,17},{17,1},{2,18},{18,2},{3,19},{19,3},{4,20},{20... | collective-permute-start | bytes 55304 | tf_op jit(solution)/shard_map/ppermute | solution.py:1373
  74.7 772.7 %collective-permute-start.1 = (bf16[128,256]{1,0:T(8,128)(2,1)S(1)}, bf16[128,256]{1,0:T(8,128)(2,1)S(1)}, u32[]{:S(2)}, u32[]{:S(2)}) collective-permute-start(bf16[128,256]{1,0:T(8,128)(2,1)S(1)} %fusion.34), channel_id=1, source_target_pairs={{0,16},{16,0},{1,17},{17,1},{2,18},{18,2},{3,19},{19,3},{4,20},{20... | collective-permute-start | bytes 196616 | tf_op jit(solution)/shard_map/ppermute | solution.py:1373
  80.7 94.7 %copy-start.15 = (f32[1152]{0:T(1024)S(1)}, f32[1152]{0:T(1024)}, u32[]{:S(2)}) copy-start(f32[1152]{0:T(1024)} %param.35) | copy-start | bytes 13828
  80.7 95.3 %copy-start.18 = (s32[1,48]{1,0:T(1,128)S(1)}, s32[1,48]{1,0:T(1,128)}, u32[]{:S(2)}) copy-start(s32[1,48]{1,0:T(1,128)} %param.22) | copy-start | bytes 580
  671.1 96.4 %copy-start.13 = (f32[3,1152]{1,0:T(4,128)S(1)}, f32[3,1152]{1,0:T(4,128)}, u32[]{:S(2)}) copy-start(f32[3,1152]{1,0:T(4,128)} %get-tuple-element.113) | copy-start | bytes 41476
  671.1 96.4 %copy-start.14 = (f32[2,1152]{1,0:T(2,128)S(1)}, f32[2,1152]{1,0:T(2,128)}, u32[]{:S(2)}) copy-start(f32[2,1152]{1,0:T(2,128)} %get-tuple-element.111) | copy-start | bytes 27652
  671.1 96.4 %copy-start.16 = (f32[1,1152]{1,0:T(1,128)S(1)}, f32[1,1152]{1,0:T(1,128)}, u32[]{:S(2)}) copy-start(f32[1,1152]{1,0:T(1,128)} %get-tuple-element.112) | copy-start | bytes 13828
  671.1 96.4 %copy-start.17 = (f32[1,1152]{1,0:T(1,128)S(1)}, f32[1,1152]{1,0:T(1,128)}, u32[]{:S(2)}) copy-start(f32[1,1152]{1,0:T(1,128)} %get-tuple-element.114) | copy-start | bytes 13828
  832.2 5.9 copy-start.7
  832.3 6.2 copy-start.11
  832.3 6.9 copy-start.10
  832.3 7.7 copy-start.8
  834.3 6.7 copy-start.9
  836.4 5.3 copy-start.6
  838.4 4.4 copy-start.5
  842.9 3.2 copy-start.4
  842.9 3.2 copy-start.12
  846.1 2.8 copy-start.2
  846.1 3.9 copy-start.1

commit v3 on v2

--- a/solution.py
+++ b/solution.py
@@ -9,7 +9,7 @@
 from jax.sharding import PartitionSpec as P
 
 HEADS = 16
-LIMIT = 60 * 2**20
+LIMIT = 62 * 2**20
 MESH = pl.DeviceIdType.MESH
 DMA = pltpu.SemaphoreType.DMA
 VM = pl.BlockSpec(memory_space=pltpu.VMEM)
@@ -113,14 +113,30 @@
     by_heads(frames, patches, width, step, tick)
 
 
-def matmul(x, w, out, tick, unit=1152):
-    for c in range(0, w.shape[1], unit):
-        out[:, c : c + unit] = dot(x[...], w[:, c : c + unit]).astype(out.dtype)
+def fetch_columns(source, target, sems):
+    width = source.shape[1] // 3
+
+    def copy(n):
+        cols = pl.ds(n * width, width)
+        return pltpu.make_async_copy(source.at[:, cols], target.at[:, cols], sems.at[n])
+
+    for n in range(3):
+        copy(n).start()
+    return lambda n: copy(n).wait()
+
+
+def matmul(x, w, out, tick, arrive):
+    width = w.shape[1] // 3
+    for n in range(3):
+        arrive(n)
+        cols = slice(n * width, (n + 1) * width)
+        out[:, cols] = dot(x[...], w[:, cols]).astype(out.dtype)
         tick()
 
 
-def spatial_kernel(frames, patches, tick, x, mod, heads, w_qkv, w_out, normed, qkv, attn, branch, first):
+def spatial_kernel(frames, patches, tick, x, mod, heads, w_all, w_out, normed, qkv, attn, branch, first, w_qkv, sems):
     rows = frames * patches
+    arrive = fetch_columns(w_all, w_qkv, sems)
 
     def norm(at, _):
         hat, _unused = normal(x[at, :].astype(f32))
@@ -129,14 +145,14 @@
 
     row_blocks(rows, 16, norm, unroll=3)
     tick()
-    matmul(normed, w_qkv, qkv, tick)
+    matmul(normed, w_qkv, qkv, tick, arrive)
     spatial_attention(tick, qkv, heads, attn, frames, patches)
     product = dot(attn[...], w_out[...])
     branch[...] = product.astype(bf16)
     first[...] = x[...].astype(f32) + mod[2:3, :] * product
 
 
-def back_norm(rows, hat_of, gain_row, d_normed, add_to, sums, size=16):
+def back_norm(tick, rows, hat_of, gain_row, d_normed, add_to, size=16):
     width = d_normed.shape[-1]
 
     def one(at, carry):
@@ -150,6 +166,7 @@
         d_value = scale * (d_hat - jnp.mean(d_hat, -1, keepdims=True)
                            - hat * jnp.mean(d_hat * hat, -1, keepdims=True))
         add_to(at, d_value)
+        tick.along(at.start // size, rows // size, 4)
         return total, weighted
 
     zero = jnp.zeros((8, width), f32)
@@ -169,22 +186,15 @@
     return jnp.sum(total, 0, keepdims=True)
 
 
-def spatial_back_kernel(frames, patches, tick, gradient, x, mod, heads, w_qkv, w_out, normed, qkv, attn, branch,
-                        d_hidden, g_qkv, g_out, d_mod, d_branch, d_attn, d_qkv, d_normed, part, load):
-    rows, width = x.shape
+def rows_back(tick, normed, d_qkv, w_all, g_qkv, d_normed, part, load):
+    width = d_normed.shape[1]
 
     def fetch(n):
-        return pltpu.make_async_copy(w_qkv.at[:, pl.ds(n * width, width)], part.at[n % 2], load.at[n % 2])
+        return pltpu.make_async_copy(w_all.at[:, pl.ds(n * width, width)], part.at[n % 2], load.at[n % 2])
 
     fetch(0).start()
     fetch(1).start()
-    d_mod[2:3, :] = gate_back(rows, gradient, branch, mod[2:3, :], d_branch)
-    tick()
-    g_out[...] = dot(attn[...], d_branch[...], TN).astype(bf16)
-    tick()
-    d_attn[...] = dot(d_branch[...], w_out[...], NT).astype(bf16)
-    tick()
-    spatial_attention_back(tick, qkv, d_attn, heads, d_qkv, frames, patches)
+    yield
     for n in range(3):
         cols = slice(n * width, (n + 1) * width)
         g_qkv[:, cols] = dot(normed[...], d_qkv[:, cols], TN).astype(bf16)
@@ -198,11 +208,26 @@
             d_normed[...] += product
         tick()
 
+
+def spatial_back_kernel(frames, patches, tick, gradient, x, mod, heads, w_qkv, w_out, normed, qkv, attn, branch,
+                        d_hidden, g_qkv, g_out, d_mod, d_branch, d_attn, d_qkv, d_normed, part, load):
+    rows, width = x.shape
+    through = rows_back(tick, normed, d_qkv, w_qkv, g_qkv, d_normed, part, load)
+    next(through)
+    d_mod[2:3, :] = gate_back(rows, gradient, branch, mod[2:3, :], d_branch)
+    tick()
+    g_out[...] = dot(attn[...], d_branch[...], TN).astype(bf16)
+    tick()
+    d_attn[...] = dot(d_branch[...], w_out[...], NT).astype(bf16)
+    tick()
+    spatial_attention_back(tick, qkv, d_attn, heads, d_qkv, frames, patches)
+    for _ in through:
+        pass
+
     def add_to(at, value):
         d_hidden[at, :] = (gradient[at, :] + value).astype(bf16)
 
-    d_mod[0:1, :], d_mod[1:2, :] = back_norm(
-        rows, lambda at: x[at, :].astype(f32), 1.0 + mod[1:2, :], d_normed, add_to, None)
+    d_mod[0:1, :], d_mod[1:2, :] = back_norm(tick, rows, lambda at: x[at, :].astype(f32), 1.0 + mod[1:2, :], d_normed, add_to)
 
 
 class Halo:
@@ -215,9 +240,10 @@
         return remote(source, target, self.sems.at[0, way], self.sems.at[1, way], self.beyond[way])
 
 
-def cross_kernel(wide, frames, patches, tick, first, gain, mod, heads, valid, text_kv, w_q, w_out, w_tqkv,
-                 normed, query, attn, second, normed_t, qkv_t, near, outer, sems):
+def cross_kernel(wide, frames, patches, tick, first, gain, mod, heads, valid, text_kv, w_q, w_out, w_all,
+                 normed, query, attn, second, normed_t, qkv_t, near, outer, sems, w_tqkv, load):
     rows, width = first.shape
+    arrive = fetch_columns(w_all, w_tqkv, load)
     scale = (width // HEADS) ** -0.5
     halo = Halo(Place(wide), sems)
 
@@ -256,7 +282,7 @@
     for copy in sends:
         copy.start()
     tick()
-    matmul(normed_t, w_tqkv, qkv_t, tick)
+    matmul(normed_t, w_tqkv, qkv_t, tick, arrive)
     for f in range(frames):
         near[2 + f] = qkv_t[f * patches : (f + 1) * patches, width:]
     tick.finish()
@@ -309,7 +335,7 @@
     def add_to(at, value):
         gradient_out[at, :] = gradient[at, :] + value
 
-    _unused, d_gain[...] = back_norm(rows, lambda at: first[at, :], gain[...], d_normed, add_to, None)
+    _unused, d_gain[...] = back_norm(tick, rows, lambda at: first[at, :], gain[...], d_normed, add_to)
 
 
 SLAB = 16
@@ -384,6 +410,14 @@
     tick()
     d_attn[...] = dot(d_branch[...], w_out[...], NT).astype(bf16)
     tick()
+
+    ends = [(way, f) for way in (0, 1) for f in (0, 1)]
+
+    def shipped(way, f, at):
+        source = edges.at[slab_rows(((1 - way) * 2 + f) * patches + at), :]
+        target = arrived.at[slab_rows((2 * way + f) * patches + at), :]
+        slab = lax.div(at, SLAB)
+        return remote(source, target, sems.at[0, way, f, slab], sems.at[1, way, f, slab], halo.beyond[way])
 
     def step(at):
         queries, probs = slab_probs(at, qkv, near, width, allowed, spread, frames, patches)
@@ -415,45 +449,43 @@
                 here = slab_rows((g if g < 2 else g - frames) * patches + at)
                 edges[here, :width] = d_keys.astype(bf16)
                 edges[here, width:] = d_values.astype(bf16)
+        for way, f in ends:
+            shipped(way, f, at).start()
 
     slabs(patches, step, tick)
-    edge = 2 * patches
-    sends = [halo.copy(0, edges.at[edge:, :], arrived.at[:edge, :]), halo.copy(1, edges.at[:edge, :], arrived.at[edge:, :])]
-    for copy in sends:
-        copy.start()
     tick()
     g_out[...] = dot(attn[...], d_branch[...], TN).astype(bf16)
-    tick()
     tick.finish()
-    for n, copy in enumerate(sends):
-        copy.wait_recv()
-        base = 0 if n == 0 else rows - edge
-
-        def add(at, _, n=n, base=base):
-            here = slab_rows(base + at.start)
-            there = slab_rows(n * edge + at.start)
+    for way, f in ends:
+        base = f * patches if way == 0 else (frames - 2 + f) * patches
+
+        def add(b, _, way=way, f=f, base=base):
+            at = b * SLAB
+            shipped(way, f, at).wait_recv()
+            here = slab_rows(base + at)
+            there = slab_rows((2 * way + f) * patches + at)
             d_qkv[here, width:] = (d_qkv[here, width:].astype(f32) + arrived[there, :].astype(f32)).astype(bf16)
             return 0
 
-        row_blocks(edge, 16, add)
-        tick()
-    for copy in sends:
-        copy.wait_send()
-
-
-def temporal_rows_kernel(tick, gradient, second, mod, d_qkv, normed, w_qkv, gradient_out, g_qkv, d_mod, d_normed):
+        lax.fori_loop(0, patches // SLAB, add, 0)
+
+    def close(b, _):
+        for way, f in ends:
+            shipped(way, f, b * SLAB).wait_send()
+        return 0
+
+    lax.fori_loop(0, patches // SLAB, close, 0)
+
+
+def temporal_rows_kernel(tick, gradient, second, mod, d_qkv, normed, w_qkv, gradient_out, g_qkv, d_mod, d_normed, part, load):
     rows, width = gradient.shape
-    for c in range(0, 3 * width, width):
-        g_qkv[:, c : c + width] = dot(normed[...], d_qkv[:, c : c + width], TN).astype(bf16)
-        tick()
-    d_normed[...] = dot(d_qkv[...], w_qkv[...], NT)
-    tick()
+    for _ in rows_back(tick, normed, d_qkv, w_qkv, g_qkv, d_normed, part, load):
+        pass
 
     def add_to(at, value):
         gradient_out[at, :] = gradient[at, :] + value
 
-    d_mod[0:1, :], d_mod[1:2, :] = back_norm(
-        rows, lambda at: second[at, :], 1.0 + mod[4:5, :], d_normed, add_to, None)
+    d_mod[0:1, :], d_mod[1:2, :] = back_norm(tick, rows, lambda at: second[at, :], 1.0 + mod[4:5, :], d_normed, add_to)
 
 
 def gelu_both(value):
@@ -511,11 +543,12 @@
         tick()
         row_blocks(rows, 16, activate, unroll=3)
         if j > 0:
-            for copy in stores(j - 1):
-                copy().wait()
+            stores(j - 1)[0]().wait()
         gu[...] = dot(normed[...], d_hidden[...], TN).astype(bf16)
         stores(j)[0]().start()
         tick()
+        if j > 0:
+            stores(j - 1)[1]().wait()
         gd[...] = dot(act[...], d_branch[...], TN).astype(bf16)
         stores(j)[1]().start()
         tick()
@@ -541,7 +574,7 @@
     def add_to(at, value):
         gradient[at, :] = cotangent[at, :].astype(f32) + value
 
-    d_mod[0:1, :], d_mod[1:2, :] = back_norm(rows, lambda at: third[at, :], 1.0 + mod[7:8, :], d_normed, add_to, None)
+    d_mod[0:1, :], d_mod[1:2, :] = back_norm(tick, rows, lambda at: third[at, :], 1.0 + mod[7:8, :], d_normed, add_to)
     for copy in stores(count - 1):
         copy().wait()
 
@@ -557,9 +590,16 @@
         odd = lax.rem(chip, 2)
         half = lax.div(chip, 2)
         self.pos = (1 - odd) * half + odd * (self.chips - 1 - half)
+        self._chips = {}
+        for step in range(self.chips) if self.chips <= 16 else ():
+            self._chips[step] = self.chip(step)
+        self._near = ((self.plane, self.member(1)), (self.plane, self.member(-1)),
+                      (1 - self.plane, self.index), (self.plane, self.index + 1 - 2 * self.core))
 
     def chip(self, step):
         n = self.chips
+        if step % n in self._chips:
+            return self._chips[step % n]
         q = lax.rem(self.pos + (step % n), n)
         high = lax.div(q, n // 2)
         return (1 - high) * (2 * q) + high * (2 * (n - q) - 1)
@@ -568,8 +608,7 @@
         return 2 * self.chip(step) + (self.core if core is None else core)
 
     def near(self):
-        return ((self.plane, self.member(1)), (self.plane, self.member(-1)),
-                (1 - self.plane, self.index), (self.plane, self.index + 1 - 2 * self.core))
+        return self._near
 
     def beside(self):
         n = self.wide
@@ -758,13 +797,8 @@
         sl = lanes(y * 2 * w[i], 7 * w[i])
         return remote(own[i].at[slot_of[0], :, sl], lt[i].at[:, sl], last_s.at[i], last_r.at[i], place.near()[across])
     def add(i, dst_k, start, src, src_start, pieces):
-        def one(t, _):
-            to = lanes(start + t * w[i], w[i])
-            value = own[i][dst_k, :, to].astype(f32)
-            value += src[:, lanes(src_start + t * w[i], w[i])].astype(f32)
-            own[i][dst_k, :, to] = value.astype(bf16)
-            return 0
-        lax.fori_loop(0, pieces, one, 0)
+        to, size = lanes(start, pieces * w[i]), pieces * w[i]
+        own[i][dst_k, :, to] += src[:, lanes(src_start, size)]
     for k in range(chips):
         for i in range(count):
             go(twin_copy, i, k); load_copy(i, k).start()
@@ -791,7 +825,6 @@
         ready = need(s)
         while done < min(chips, max(ready) + 3):
             pair(done); done += 1
-            yield
         for k in ready: planes(k)
         yield
         for i in range(count):
@@ -810,17 +843,14 @@
     for i in range(count):
         last(i).wait_recv()
         k = slot_of[0]
-        n, r, rows, col, width = pieces[i]
         mine, theirs = y * 7 * w[i], (1 - y) * 7 * w[i]
         for t in range(2):
             a, b = t * w[i] + mine, t * w[i] + theirs
-            outs[n][pl.ds(r, rows), lanes(col + a, w[i])] = own[i][k, :, lanes(a, w[i])]
-            outs[n][pl.ds(r, rows), lanes(col + b, w[i])] = lt[i][:, lanes(b, w[i])]
+            outs[i][:, lanes(a, w[i])] = own[i][k, :, lanes(a, w[i])]
+            outs[i][:, lanes(b, w[i])] = lt[i][:, lanes(b, w[i])]
         for t in range(2, 7):
             at = pl.ds(t * w[i], w[i])
-            outs[n][pl.ds(r, rows), pl.ds(col + t * w[i], w[i])] = (
-                own[i][k, :, at].astype(f32) + lt[i][:, at].astype(f32)
-            ).astype(bf16)
+            outs[i][:, at] = own[i][k, :, at] + lt[i][:, at]
         yield
     sends.close()
 
@@ -1001,14 +1031,8 @@
     yield from keys.sum_steps()
     yield from keys.spread_steps(keys.total)
     over(keys.both, 0, True).start()
-
-    def block(j, total):
-        for core in (0, 1):
-            total += dot(kv_rows[j, core], keys.every[j, core])
-        return total
-
-    rows = lax.fori_loop(0, place.chips, block, jnp.zeros(prompts.every.shape[2:], f32))
-    yield from prompts.spread_steps(rows)
+    every = keys.every[...]
+    yield from prompts.spread_steps(dot(kv_rows[...], every.reshape(-1, every.shape[-1])))
     over(prompts.both, 1, True).start()
     yield
     for k, part in ((0, keys), (1, prompts)):
@@ -1036,22 +1060,14 @@
     vectors.close()
 
 
-def together(generators):
-    running = list(generators)
-    while running:
-        for one in list(running):
-            if next(one, running) is running:
-                running.remove(one)
-        yield
-
-
 MOST_CHIPS = 8
 
 
 class Gather:
     direct = False
 
-    def __init__(self, wide, arrays):
+    def __init__(self, wide, arrays, turns=1):
+        self.turns = turns
         self.inputs = [(a, ANY) for a in arrays]
         self.outputs = [(((wide,) + a.shape, a.dtype), ANY) for a in arrays]
         self.arrays = arrays
@@ -1061,30 +1077,45 @@
     def steps(self, place, ins, outs, scratch):
         return gather_steps(place, ins, outs, scratch, self.pieces)
 
-    def plain(self):
+    def plain(self, _outputs):
         return [lax.all_gather(a, "wide") for a in self.arrays]
 
 
 class Scatter:
     direct = False
-
-    def __init__(self, wide, arrays):
-        self.arrays = arrays
-        self.pieces = pieces_of(arrays)
+    turns = 1
+
+    def __init__(self, wide, pieces, turns=1):
+        self.turns = turns
+        arrays = []
+        for piece in pieces:
+            if not any(piece[0] is a for a in arrays):
+                arrays.append(piece[0])
+        self.given = pieces
+        self.pieces = [([piece[0] is a for a in arrays].index(True),) + piece[1:] for piece in pieces]
         self.inputs = [(a, ANY) for a in arrays]
-        self.outputs = [((a.shape[1:], bf16), VM) for a in arrays]
-        self.scratch = scatter_scratch(wide, [(p[2], p[4]) for p in self.pieces])
+        self.outputs = [(((p[2], p[4]), bf16), VM) for p in pieces]
+        self.scratch = scatter_scratch(wide, [(p[2], p[4]) for p in pieces])
 
     def steps(self, place, ins, outs, scratch):
         buffers = 5 * len(self.pieces)
         return scatter_steps(place, ins, outs, scratch[:buffers], scratch[buffers:], self.pieces)
 
-    def plain(self):
-        sums = [lax.psum_scatter(a.astype(f32), "wide") for a in self.arrays]
-        return [lax.psum(a, "narrow").astype(bf16) for a in sums]
+    def plain(self, _outputs):
+        return [plain_scatter(*piece) for piece in self.given]
+
+
+def plain_scatter(array, row, rows, col, cols):
+    part = array[:, row : row + rows, col : col + cols].astype(f32)
+    return lax.psum(lax.psum_scatter(part, "wide"), "narrow").astype(bf16)
+
+
+def pieces_in(array):
+    return [(array,) + p[1:] for p in pieces_of([array])]
 
 
 class Front:
+    turns = 1
     direct = True
 
     def __init__(self, wide, mod_parts, text_parts):
@@ -1096,13 +1127,14 @@
         modulation = Exchange(place, ins[0], scratch[0], outs[0], scratch[1:5])
         return front_steps(modulation, Ring(place, ins[1], None, scratch[5:]), outs[1])
 
-    def plain(self):
+    def plain(self, _outputs):
         mod_parts, text_parts = (value for value, _ in self.inputs)
         rows = text_parts.reshape((-1,) + text_parts.shape[2:]).astype(f32)
         return [lax.psum(mod_parts, "wide"), lax.psum_scatter(rows, "wide").astype(bf16)]
 
 
 class Text:
+    turns = 1
     direct = False
 
     def __init__(self, wide, prompt, kv_cols):
@@ -1114,19 +1146,20 @@
     def steps(self, place, ins, outs, scratch):
         return text_steps(Ring(place, scratch[0], outs[0], scratch[1:]), ins[0], ins[1])
 
-    def plain(self):
+    def plain(self, _outputs):
         prompt, kv_cols = (value for value, _ in self.inputs)
         product = lax.dot_general(kv_cols, prompt, (((3,), (0,)), ((), ())), preferred_element_type=f32)
         return [lax.psum(product, "wide").astype(bf16)]
 
 
 class TextBack:
+    turns = 1
     direct = False
 
     def __init__(self, wide, kv_parts, kv_rows):
         chips = (wide // 2, 2)
-        kv_block, block = kv_parts.shape[1:], (kv_rows.shape[1], kv_parts.shape[2])
-        self.inputs = [(by_chip(kv_parts), VM), (by_chip(kv_rows), VM)]
+        kv_block, block = kv_parts.shape[1:], (kv_rows.shape[0], kv_parts.shape[2])
+        self.inputs = [(by_chip(kv_parts), VM), (kv_rows, VM)]
         self.outputs = [(((2,) + chips + kv_block, bf16), VM), (((2,) + chips + block, bf16), VM)]
         self.scratch = Ring.scratch(wide, kv_block) + Ring.scratch(wide, block) + [DMA((2, 2))]
 
@@ -1137,14 +1170,15 @@
         prompts.both = outs[1]
         return text_back_steps(keys, prompts, ins[1], scratch[18])
 
-    def plain(self):
+    def plain(self, _outputs):
         kv_parts, kv_rows = (value for value, _ in self.inputs)
         every = lax.psum(kv_parts.astype(f32), "wide").astype(bf16)
-        rows = jnp.einsum("jcrk,jckt->rt", kv_rows, every, preferred_element_type=f32).astype(bf16)
+        rows = dot(kv_rows, every.reshape(-1, every.shape[-1])).astype(bf16)
         return [lax.all_gather(every, "narrow"), lax.all_gather(by_chip(lax.all_gather(rows, "wide")), "narrow")]
 
 
 class Vectors:
+    turns = 1
     direct = True
 
     def __init__(self, wide, parts):
@@ -1157,31 +1191,46 @@
         vectors.both = outs[0]
         return vector_steps(vectors, scratch[5])
 
-    def plain(self):
+    def plain(self, _outputs):
         return [lax.all_gather(lax.psum(self.inputs[0][0], "wide"), "narrow")]
 
 
 class Pump:
-    def __init__(self, steps, pace):
-        self.steps, self.pace = steps, pace
-        self.ended = False
-        self.calls = self.rounds = 0
+    def __init__(self, pace=1, every=1):
+        self.running, self.pace, self.every = [], pace, every
+        self.calls = 0
+
+    def due(self):
+        self.calls += 1
+        return self.calls % self.every == 0
 
     def __call__(self):
-        self.calls += 1
+        if self.due():
+            self.move()
+
+    def move(self):
         for _ in range(self.pace):
-            if not self.ended:
-                self.ended = next(self.steps, self) is self
-                self.rounds += 1
+            for steps, turns in list(self.running):
+                for _ in range(turns):
+                    if next(steps, self) is self:
+                        self.running.remove((steps, turns))
+                        break
 
     def inside(self, index, low, high):
         for n in range(low, high):
-            if not self.ended:
-                pl.when(index == n)(lambda: self())
+            if self.due() and self.running:
+                pl.when(index == n)(lambda: self.move())
+
+    def along(self, index, count, calls):
+        if count < 2 * calls:
+            return
+        for n in range(calls):
+            if self.due() and self.running:
+                pl.when(index == (n + 1) * count // (calls + 1))(lambda: self.move())
 
     def finish(self):
-        while not self.ended:
-            self()
+        while self.running:
+            self.move()
 
 
 def take(refs, *counts):
@@ -1192,38 +1241,37 @@
     return found
 
 
-def fused_kernel(wide, talks, compute, counts, parts, pace, *refs):
+def fused_kernel(wide, talks, compute, counts, parts, pace, burst, every, *refs):
     sizes = list(counts) + [n for p in parts for n in (len(p.inputs), len(p.outputs), len(p.scratch))]
     order = [0] + [3 + 3 * i for i in range(len(parts))]
     order += [1] + [4 + 3 * i for i in range(len(parts))]
     order += [2] + [5 + 3 * i for i in range(len(parts))]
     found = dict(zip(order, take(refs, *[sizes[i] for i in order])))
+    pump = Pump(pace, every)
     if talks:
         place = Place(wide)
         greet(all_near(place) if any(p.direct for p in parts) else place.near() + place.beside())
-        running = together(
-            [p.steps(place, found[3 + 3 * i], found[4 + 3 * i], found[5 + 3 * i]) for i, p in enumerate(parts)]
-        )
-        pump = Pump(running, pace)
-        pump()
-    else:
-        pump = Pump(iter(()), 1)
+        for i, p in enumerate(parts):
+            steps = p.steps(place, found[3 + 3 * i], found[4 + 3 * i], found[5 + 3 * i])
+            pump.running.append((steps, p.turns))
+        for _ in range(burst):
+            pump.move()
     if compute is not None:
         compute(pump, *found[0], *found[1], *found[2])
     pump.finish()
 
 
-def fused(name, wide, compute, inputs, outputs, scratch, parts=(), pace=1, collective_id=None):
+def fused(name, wide, compute, inputs, outputs, scratch, parts=(), pace=1, collective_id=None, burst=1, every=1):
     if wide > 2 * MOST_CHIPS and parts:
         done = [[]] if compute is None else fused(
             name, wide, compute, inputs, outputs, scratch, collective_id=collective_id)
-        return done + [part.plain() for part in parts]
+        return done + [part.plain(done[0]) for part in parts]
     ins = inputs + [x for p in parts for x in p.inputs]
     outs = outputs + [x for p in parts for x in p.outputs]
     talks = collective_id is not None
     options = dict(collective_id=collective_id, has_side_effects=True) if talks else {}
     found = pl.pallas_call(
-        functools.partial(fused_kernel, wide, talks, compute, (len(inputs), len(outputs), len(scratch)), parts, pace),
+        functools.partial(fused_kernel, wide, talks, compute, (len(inputs), len(outputs), len(scratch)), parts, pace, burst, every),
         out_shape=[jax.ShapeDtypeStruct(shape, dtype) for (shape, dtype), _ in outs],
         in_specs=[spec for _, spec in ins],
         out_specs=[spec for _, spec in outs],
@@ -1246,9 +1294,9 @@
     rows, width = x.shape
     return fused(
         "spatial", wide, functools.partial(spatial_kernel, frames, patches),
-        on_chip(x, mod, heads, w_qkv, w_out),
+        on_chip(x, mod, heads) + [(w_qkv, ANY)] + on_chip(w_out),
         on_chip(*[((rows, n * width), d) for n, d in ((1, bf16), (3, bf16), (1, bf16), (1, bf16), (1, f32))]),
-        [], **rest,
+        [pltpu.VMEM(w_qkv.shape, bf16), DMA((3,))], **rest,
     )
 
 
@@ -1268,10 +1316,10 @@
     rows, width = first.shape
     return fused(
         "cross", wide, functools.partial(cross_kernel, wide, frames, patches),
-        on_chip(first, gain, mod, heads, valid, text_kv, w_q, w_out, w_tqkv),
+        on_chip(first, gain, mod, heads, valid, text_kv, w_q, w_out) + [(w_tqkv, ANY)],
         on_chip(*[((rows, n * width), d) for n, d in ((1, bf16), (1, bf16), (1, bf16), (1, f32), (1, bf16), (3, bf16))])
         + on_chip(((frames + 4, patches, 2 * width), bf16)),
-        [pltpu.VMEM((4 * patches, width), bf16), DMA((2, 2))], **rest,
+        [pltpu.VMEM((4 * patches, width), bf16), DMA((2, 2)), pltpu.VMEM(w_tqkv.shape, bf16), DMA((3,))], **rest,
     )
 
 
@@ -1303,7 +1351,7 @@
         "temporal_back", wide, functools.partial(temporal_back_kernel, wide, frames, patches),
         on_chip(gradient, qkv, near, allowed, spread, heads, mod, w_out, attn, branch),
         on_chip(((width, width), bf16), ((rows, 3 * width), bf16), ((1, width), f32)),
-        [V((rows, width), bf16)] * 2 + [V(edges, bf16)] * 2 + [DMA((2, 2))], **rest,
+        [V((rows, width), bf16)] * 2 + [V(edges, bf16)] * 2 + [DMA((2, 2, 2, patches // SLAB))], **rest,
     )
 
 
@@ -1311,9 +1359,9 @@
     rows, width = gradient.shape
     return fused(
         "temporal_rows", wide, temporal_rows_kernel,
-        on_chip(gradient, second, mod, d_qkv, normed, w_qkv),
+        on_chip(gradient, second, mod, d_qkv, normed) + [(w_qkv, ANY)],
         on_chip(((rows, width), f32), ((width, 3 * width), bf16), ((2, width), f32)),
-        [pltpu.VMEM((rows, width), f32)], **rest,
+        [pltpu.VMEM((rows, width), f32), pltpu.VMEM((2, width, width), bf16), DMA((2,))], **rest,
     )
 
 
@@ -1378,6 +1426,9 @@
     def whole(value):
         return value.reshape(-1, value.shape[-1])
 
+    def joined(parts, axis):
+        return jnp.concatenate([part.astype(f32) for part in parts], axis)
+
     def blocks(value):
         return value.reshape(wide, -1, value.shape[-1])
 
@@ -1387,20 +1438,19 @@
     prompt_rows = lax.dynamic_slice_in_dim(text[0], position * rows_text, rows_text, 1)
     text_part = dot(text_weight, prompt_rows, (((0,), (1,)), ((), ())))
     kv_cols = blocks(kv_weight.T)
-    kv_rows = kv_weight.reshape(rows_model, wide, -1).transpose(1, 0, 2)
     front = Front(wide, mod_part.reshape(wide, 1, -1), blocks(text_part.astype(bf16)))
     _none, (modulation, prompt), (full_qkv, full_out) = fused(
-        "start", wide, None, [], [], [], parts=[front, Gather(wide, [qkv_weight, out_weight])], collective_id=0
+        "start", wide, None, [], [], [], parts=[front, Gather(wide, [qkv_weight, out_weight], turns=3)], collective_id=0
     )
     full_qkv, full_out = whole(full_qkv), whole(full_out)
     mod = modulation.reshape(9, width)
 
     tokens = hidden[0].reshape(rows, width)
     (normed_a, qkv_a, attn_a, branch_a, first), (kv_all,), gathered = spatial(
-        wide, frames, patches, tokens, mod, heads, full_qkv, full_out, collective_id=1, pace=2,
+        wide, frames, patches, tokens, mod, heads, full_qkv, full_out, collective_id=1,
         parts=[
             Text(wide, prompt, kv_cols),
-            Gather(wide, [cross_q_weight, cross_out_weight, temp_qkv_weight, temp_out_weight]),
+            Gather(wide, [cross_q_weight, cross_out_weight, temp_qkv_weight, temp_out_weight], turns=3),
         ],
     )
     full_cross_q, full_cross_out, full_temp_qkv, full_temp_out = map(whole, gathered)
@@ -1409,7 +1459,7 @@
     gain = cross_gain[None, :]
     (normed_c, query_c, attn_c, second, normed_t, qkv_t, near), (full_down,) = cross(
         wide, frames, patches, first, gain, mod, heads, valid, text_kv, full_cross_q, full_cross_out, full_temp_qkv,
-        parts=[Gather(wide, [down_weight])], collective_id=2,
+        parts=[Gather(wide, [down_weight])], collective_id=2, every=2,
     )
     clip_pad = jnp.pad(seg_ids[0], 2, constant_values=-1)
     clip_local = lax.dynamic_slice_in_dim(clip_pad, position * frames, frames + 4)
@@ -1419,40 +1469,44 @@
     allowed = jnp.broadcast_to(allowed[:, :, None, None], (5, frames, SLAB, HEADS)).reshape(-1, HEADS).astype(f32)
     (attn_t, branch_t, third), (full_up,) = temporal(
         wide, frames, patches, qkv_t, near, allowed, spread, heads, second, mod, full_temp_out,
-        parts=[Gather(wide, [up_weight])], collective_id=3, pace=2,
+        parts=[Gather(wide, [up_weight])], collective_id=3,
     )
 
     upstream = cotangent[0].reshape(rows, width)
     ((block_out, gradient, grad_up, grad_down, d_mod_m),) = mlp(
         wide, third, upstream, mod, whole(full_up), whole(full_down)
     )
-
-    (grad_temp_out, d_qkv_t, d_gate_t), (grad_up,) = temporal_back(
+    grad_up = grad_up.reshape(wide, rows_model, -1)
+
+    (grad_temp_out, d_qkv_t, d_gate_t), up_parts = temporal_back(
         wide, frames, patches, gradient, qkv_t, near, allowed, spread, heads, mod, full_temp_out, attn_t, branch_t,
-        parts=[Scatter(wide, [blocks(grad_up)])], collective_id=4, pace=2,
-    )
-    (gradient, grad_temp_qkv, d_mod_t), (grad_down,) = temporal_rows(
+        parts=[Scatter(wide, pieces_in(grad_up))], collective_id=4,
+    )
+    (gradient, grad_temp_qkv, d_mod_t), down_parts = temporal_rows(
         wide, gradient, second, mod, d_qkv_t, normed_t, full_temp_qkv,
-        parts=[Scatter(wide, [blocks(grad_down)])], collective_id=5, pace=6,
-    )
-    (gradient, grad_cross_q, grad_cross_out, d_gain, d_text_kv), (grad_temp_qkv, grad_temp_out) = cross_back(
+        parts=[Scatter(wide, pieces_in(blocks(grad_down)))], collective_id=5, pace=2, burst=3,
+    )
+    (gradient, grad_cross_q, grad_cross_out, d_gain, d_text_kv), (*temp_qkv_parts, grad_temp_out) = cross_back(
         wide, frames, patches, gradient, first, gain, heads, valid, text_kv,
         full_cross_q, full_cross_out, normed_c, query_c, attn_c,
-        parts=[Scatter(wide, [blocks(grad_temp_qkv), blocks(grad_temp_out)])], collective_id=6, pace=2,
+        parts=[Scatter(wide, pieces_in(blocks(grad_temp_qkv)) + pieces_in(blocks(grad_temp_out)))], collective_id=6, burst=4,
     )
     found = spatial_back(
         wide, frames, patches, gradient, tokens, mod, heads, full_qkv, full_out, normed_a, qkv_a, attn_a, branch_a,
         parts=[
-            TextBack(wide, blocks(d_text_kv.T.astype(bf16)), kv_rows),
-            Scatter(wide, [blocks(grad_cross_q), blocks(grad_cross_out)]),
+            TextBack(wide, blocks(d_text_kv.T.astype(bf16)), kv_weight),
+            Scatter(wide, [p for g in (grad_cross_q, grad_cross_out) for p in pieces_in(blocks(g))]),
         ],
         collective_id=7,
     )
     (grad_hidden, grad_qkv, grad_out, d_mod_a), (d_kv_both, d_prompt_both), (grad_cross_q, grad_cross_out) = found
     vectors = jnp.concatenate([d_mod_a, d_mod_t, d_gate_t, d_mod_m, d_gain], 0)
-    _none, (vec_both,), (grad_qkv, grad_out) = fused(
+    _none, (vec_both,), (*qkv_parts, grad_out) = fused(
         "end", wide, None, [], [], [], collective_id=8,
-        parts=[Vectors(wide, vectors.reshape(wide, 1, -1)), Scatter(wide, [blocks(grad_qkv), blocks(grad_out)])],
+        parts=[
+            Vectors(wide, vectors.reshape(wide, 1, -1)),
+            Scatter(wide, pieces_in(blocks(grad_qkv)) + pieces_in(blocks(grad_out)), turns=2),
+        ],
     )
     vec_both = vec_both.reshape(2, 10, width)
 
@@ -1477,14 +1531,14 @@
         grad_ada,
         grad_text,
         grad_kv,
-        grad_qkv.astype(f32),
+        joined(qkv_parts, 1),
         grad_out.astype(f32),
         grad_cross_q.astype(f32),
         grad_cross_out.astype(f32),
-        grad_temp_qkv.astype(f32),
+        joined(temp_qkv_parts, 1),
         grad_temp_out.astype(f32),
-        grad_up.astype(f32),
-        grad_down.astype(f32),
+        joined(up_parts, 1),
+        joined(down_parts, 0),
         grad_gain,
     )
 

time: 856 us -> 818 us (0.956)
  Pallas kernels: 801 us -> 767 us
    pallas_call x10, Pallas kernels: 801 us -> 767 us  [fused(): pl.pallas_call(functools.partial(fused_kernel, wide, talks, compute, (len...]
  transfers between devices with their start and end apart: 3 -> 3, of which waited for: 0 -> 0; matrix products, arithmetic and copies ran while one was open for 5% -> 4% of each run, Pallas kernels for 94% -> 94%
where the time goes in v3:
time: 818 us; the launch traced here: 813 us
  Pallas kernels  767 us (94%)
  other arithmetic  17 us (2%)
  local copies, waits for them, and re-layouts  16.9 us (2%)
    pallas_call x10, Pallas kernels, fused(): pl.pallas_call(functools.partial(fused_kernel, wide, talks, compute, (len...  767 us
  transfers between devices with their start and end apart: 3, of which 0 were waited for; matrix products, arithmetic and copies ran while one was open for 4% of the time, Pallas kernels for 94%

profile of v3, /device:TPU:0, one launch (start us, length us, event | category | flops | bytes accessed | tf_op | source)
XLA Modules:
  0.0 812.7 jit_solution(15494521560409881376)
XLA Ops:
  1.7 3.0 collective-permute-start
  4.7 5.1 reshape.189
  12.5 51.4 %start.1 = (f32[16,1,648]{2,1,0:T(1,128)}, bf16[72,128]{1,0:T(8,128)(2,1)}, bf16[16,72,3456]{2,1,0:T(8,128)(2,1)}, bf16[16,72,1152]{2,1,0:T(8,128)(2,1)}) custom-call(f32[16,1,648]{2,1,0:T(1,128)} %dot_general.18.refs_0_, bf16[8,2,72,128]{3,2,1,0:T(8,128)(2,1)} %bitcast.109, bf16[72,3456]{1,0:T(8,128)(2,1)} %refs_2_.1, bf16[72,1152]{1,0:T(8,128)(2,1)} %refs_3_.1), custom_call_target="tpu_custom_call" | custom-call | tf_op jit(solution)/shard_map/start/pallas_call | solution.py:1273
  63.9 1.6 collective-permute-start.2
  70.5 86.9 %spatial.1 = (bf16[624,1152]{1,0:T(8,128)(2,1)}, bf16[624,3456]{1,0:T(8,128)(2,1)}, bf16[624,1152]{1,0:T(8,128)(2,1)}, bf16[624,1152]{1,0:T(8,128)(2,1)}, f32[62...) custom-call(bf16[624,1152]{1,0:T(8,128)(2,1)} %bitcast.94, ...), custom_call_target="tpu_custom_call" | custom-call | tf_op jit(solution)/shard_map/spatial/pallas_call | solution.py:1273
  157.4 2.1 copy.40
  161.8 81.0 %cross.1 = (bf16[624,1152]{1,0:T(8,128)(2,1)}, bf16[624,1152]{1,0:T(8,128)(2,1)}, bf16[624,1152]{1,0:T(8,128)(2,1)}, f32[624,1152]{1,0:T(8,128)}, bf16[624,1152]...) custom-call(f32[624,1152]{1,0:T(8,128)} %get-tuple-element.84.refs_0_.r, ...), custom_call_target="tpu_custom_call" | custom-call | tf_op jit(solution)/shard_map/cross/pallas_call | solution.py:1273
  243.5 54.4 %temporal.1 = (bf16[624,1152]{1,0:T(8,128)(2,1)}, bf16[624,1152]{1,0:T(8,128)(2,1)}, f32[624,1152]{1,0:T(8,128)}, bf16[16,72,4608]{2,1,0:T(8,128)(2,1)}) custom-call(bf16[624,3456]{1,0:T(8,128)(2,1)} %get-tuple-element.89.refs_0_.refs_1_, bf16[7,208,2304]{2,1,0:T(8,128)(2,1)} %get-tuple-element.90.refs_1_.refs_2_, ...), custom_call_target="tpu_custom_call" | custom-call | tf_op jit(solution)/shard_map/temporal/pallas_call | solution.py:1273
  298.0 82.5 %mlp.1 = (bf16[624,1152]{1,0:T(8,128)(2,1)}, f32[624,1152]{1,0:T(8,128)}, bf16[1152,4608]{1,0:T(8,128)(2,1)}, bf16[4608,1152]{1,0:T(8,128)(2,1)}, f32[3,1152]{1,0:T(4,128)}) custom-call(f32[624,1152]{1,0:T(8,128)} %get-tuple-element.93.refs_0_, bf16[624,1152]{1,0:T(8,128)(2,1)} %bitcast.106, f32[9,1152]{1,0:T(8,128)} %reshape.190.refs_1_.refs_2_.refs_6_, ...), custom_call_target="tpu_custom_call" | custom-call | tf_op jit(solution)/shard_map/mlp/pallas_call | solution.py:1273
  380.4 111.3 %temporal_back.1 = (bf16[1152,1152]{1,0:T(8,128)(2,1)}, bf16[624,3456]{1,0:T(8,128)(2,1)}, f32[1,1152]{1,0:T(1,128)}, bf16[72,1152]{1,0:T(8,128)(2,1)}, bf16[72,...) custom-call(f32[624,1152]{1,0:T(8,128)} %get-tuple-element.97.refs_0_, ...), custom_call_target="tpu_custom_call" | custom-call | tf_op jit(solution)/shard_map/temporal_back/pallas_call | solution.py:1273
  491.7 75.6 %temporal_rows.1 = (f32[624,1152]{1,0:T(8,128)}, bf16[1152,3456]{1,0:T(8,128)(2,1)}, f32[2,1152]{1,0:T(2,128)}, bf16[96,1152]{1,0:T(8,128)(2,1)}, bf16[96,1152]{1,0:T(8,128)(2,1)}, /*index=5*/bf16[96,1152]{1,0:T(8,128)(2,1)}) custom-call(f32[624,1152]{1,0:T(8,128)} %get-tuple-element.97.refs_0_, f32[624,1152]{1,0:T(8,128)} %get-tuple-element.91.refs_5_.refs_1_, ...), custom_call_target="tpu_custom_call" | custom-call | tf_op jit(solution)/shard_map/temporal_rows/pallas_call | solution.py:1273
  567.3 69.1 %cross_back.1 = (f32[624,1152]{1,0:T(8,128)}, bf16[1152,1152]{1,0:T(8,128)(2,1)}, bf16[1152,1152]{1,0:T(8,128)(2,1)}, f32[1,1152]{1,0:T(1,128)}, f32[128,2304]{1...) custom-call(f32[624,1152]{1,0:T(8,128)} %get-tuple-element.104.refs_, ...), custom_call_target="tpu_custom_call" | custom-call | tf_op jit(solution)/shard_map/cross_back/pallas_call | solution.py:1273
  636.5 1.3 convert_bitcast_fusion
  638.9 93.7 %spatial_back.1 = (bf16[624,1152]{1,0:T(8,128)(2,1)}, bf16[1152,3456]{1,0:T(8,128)(2,1)}, bf16[1152,1152]{1,0:T(8,128)(2,1)}, f32[3,1152]{1,0:T(4,128)}, bf16[2,...) custom-call(f32[624,1152]{1,0:T(8,128)} %get-tuple-element.110.refs_, ...), custom_call_target="tpu_custom_call" | custom-call | tf_op jit(solution)/shard_map/spatial_back/pallas_call | solution.py:1273
  732.6 1.1 concatenate.31
  734.5 61.3 %end.1 = (f32[2,16,1,720]{3,2,1,0:T(1,128)}, bf16[72,1152]{1,0:T(8,128)(2,1)}, bf16[72,1152]{1,0:T(8,128)(2,1)}, bf16[72,1152]{1,0:T(8,128)(2,1)}, bf16[72,1152]{1,0:T(8,128)(2,1)}) custom-call(f32[16,1,720]{2,1,0:T(1,128)} %reshape.208.refs_0_, bf16[16,72,3456]{2,1,0:T(8,128)(2,1)} %bitcast.93, bf16[16,72,1152]{2,1,0:T(8,128)(2,1)} %bitcast.101), custom_call_target="tpu_custom_call" | custom-call | tf_op jit(solution)/shard_map/end/pallas_call | solution.py:1273
  795.8 1.2 reduce.2
  797.8 1.7 convert_element_type.91
  801.3 1.1 maximum_convert_fusion.1
  804.6 1.2 maximum_convert_fusion
  806.6 2.0 multiply_add_fusion
  808.6 1.4 convolution_bitcast_fusion
  809.9 1.4 convolution_bitcast_fusion.1
  811.3 1.1 copy.54
  (110 shorter events, 17.5 us)
Async XLA Ops:
  0.6 10.7 %copy-start = (bf16[1,128,4096]{2,1,0:T(8,128)(2,1)S(1)}, bf16[1,128,4096]{2,1,0:T(8,128)(2,1)}, u32[]{:S(2)}) copy-start(bf16[1,128,4096]{2,1,0:T(8,128)(2,1)} %param.20) | copy-start | bytes 3145732
  1.7 804.8 %collective-permute-start = (bf16[72]{0:T(256)(128)(2,1)S(1)}, bf16[72]{0:T(256)(128)(2,1)S(1)}, u32[]{:S(2)}, u32[]{:S(2)}) collective-permute-start(bf16[72]{0:T(256)(128)(2,1)S(1)} %fusion.27), channel_id=1, source_target_pairs={{0,16},{16,0},{1,17},{17,1},{2,18},{18,2},{3,19},{19,3},{4,20},{20... | collective-permute-start | bytes 440 | tf_op jit(solution)/shard_map/ppermute | solution.py:1421
  10.6 58.8 %copy-start.3 = (bf16[72,2304]{1,0:T(8,128)(2,1)S(1)}, bf16[72,2304]{1,0:T(8,128)(2,1)}, u32[]{:S(2)}) copy-start(bf16[72,2304]{1,0:T(8,128)(2,1)} %refs_11_.1) | copy-start | bytes 995332
  63.9 744.6 %collective-permute-start.2 = (bf16[72,128]{1,0:T(8,128)(2,1)}, bf16[72,128]{1,0:T(8,128)(2,1)S(1)}, u32[]{:S(2)}, u32[]{:S(2)}) collective-permute-start(bf16[72,128]{1,0:T(8,128)(2,1)} %get-tuple-element.83.refs_5_), channel_id=1, source_target_pairs={{0,16},{16,0},{1,17},{17,1},{2,18},{18,2},{3,19},{19,3},{4,20},{20... | collective-permute-start | bytes 55304 | tf_op jit(solution)/shard_map/ppermute | solution.py:1421
  65.5 744.4 %collective-permute-start.1 = (bf16[128,256]{1,0:T(8,128)(2,1)S(1)}, bf16[128,256]{1,0:T(8,128)(2,1)S(1)}, u32[]{:S(2)}, u32[]{:S(2)}) collective-permute-start(bf16[128,256]{1,0:T(8,128)(2,1)S(1)} %fusion.34), channel_id=1, source_target_pairs={{0,16},{16,0},{1,17},{17,1},{2,18},{18,2},{3,19},{19,3},{4,20},{20... | collective-permute-start | bytes 196616 | tf_op jit(solution)/shard_map/ppermute | solution.py:1421
  70.5 90.3 %copy-start.28 = (f32[1152]{0:T(1024)S(1)}, f32[1152]{0:T(1024)}, u32[]{:S(2)}) copy-start(f32[1152]{0:T(1024)} %param.35) | copy-start | bytes 13828
  70.5 90.9 %copy-start.31 = (s32[1,48]{1,0:T(1,128)S(1)}, s32[1,48]{1,0:T(1,128)}, u32[]{:S(2)}) copy-start(s32[1,48]{1,0:T(1,128)} %param.22) | copy-start | bytes 580
  638.8 93.7 %copy-start.26 = (f32[3,1152]{1,0:T(4,128)S(1)}, f32[3,1152]{1,0:T(4,128)}, u32[]{:S(2)}) copy-start(f32[3,1152]{1,0:T(4,128)} %get-tuple-element.122) | copy-start | bytes 41476
  638.9 93.7 %copy-start.27 = (f32[2,1152]{1,0:T(2,128)S(1)}, f32[2,1152]{1,0:T(2,128)}, u32[]{:S(2)}) copy-start(f32[2,1152]{1,0:T(2,128)} %get-tuple-element.120) | copy-start | bytes 27652
  638.9 93.7 %copy-start.29 = (f32[1,1152]{1,0:T(1,128)S(1)}, f32[1,1152]{1,0:T(1,128)}, u32[]{:S(2)}) copy-start(f32[1,1152]{1,0:T(1,128)} %get-tuple-element.121) | copy-start | bytes 13828
  638.9 93.7 %copy-start.30 = (f32[1,1152]{1,0:T(1,128)S(1)}, f32[1,1152]{1,0:T(1,128)}, u32[]{:S(2)}) copy-start(f32[1,1152]{1,0:T(1,128)} %get-tuple-element.123) | copy-start | bytes 13828
  795.7 3.7 copy-start.5
  795.8 4.0 copy-start.20
  795.8 4.8 copy-start.19
  797.0 4.3 copy-start.9
  797.0 4.3 copy-start.10
  797.0 4.3 copy-start.11
  799.8 2.7 copy-start.12
  799.8 2.7 copy-start.13
  799.8 2.7 copy-start.14
  805.8 2.8 copy-start.4
  805.8 2.8 copy-start.25
  806.5 3.4 copy-start.8
  808.6 2.8 copy-start.2
  (11 other events, 22.5 us)

commit v4 on v3

--- a/solution.py
+++ b/solution.py
@@ -234,6 +234,8 @@
     def __init__(self, place, sems):
         n, me = place.wide, place.index
         self.sems = sems
+        self.leaves = (me < n - 1, me > 0)
+        self.comes = (me > 0, me < n - 1)
         self.beyond = ((place.plane, lax.rem(me + 1, n)), (place.plane, lax.rem(me + n - 1, n)))
 
     def copy(self, way, source, target):
@@ -279,23 +281,28 @@
     edge = 2 * patches
     sends = [halo.copy(0, normed_t.at[rows - edge :, :], outer.at[:edge, :]),
              halo.copy(1, normed_t.at[:edge, :], outer.at[edge:, :])]
-    for copy in sends:
-        copy.start()
+    for n, copy in enumerate(sends):
+        pl.when(halo.leaves[n])(copy.start)
     tick()
     matmul(normed_t, w_tqkv, qkv_t, tick, arrive)
     for f in range(frames):
         near[2 + f] = qkv_t[f * patches : (f + 1) * patches, width:]
     tick.finish()
     for n, copy in enumerate(sends):
-        copy.wait_recv()
+        pl.when(halo.comes[n])(copy.wait_recv)
+
+        @pl.when(jnp.logical_not(halo.comes[n]))
+        def _(n=n):
+            outer[n * edge : (n + 1) * edge, :] = jnp.zeros((edge, width), bf16)
+
         side = outer[n * edge : (n + 1) * edge, :]
         for c in (width, 2 * width):
             found = dot(side, w_tqkv[:, c : c + width]).astype(bf16)
             for f in range(2):
                 near[n * (frames + 2) + f, :, c - width : c] = found[f * patches : (f + 1) * patches]
             tick()
-    for copy in sends:
-        copy.wait_send()
+    for n, copy in enumerate(sends):
+        pl.when(halo.leaves[n])(copy.wait_send)
 
 
 def cross_back_kernel(frames, patches, tick, gradient, first, gain, heads, valid, text_kv, w_q, w_out, normed, query,
@@ -410,8 +417,6 @@
     tick()
     d_attn[...] = dot(d_branch[...], w_out[...], NT).astype(bf16)
     tick()
-
-    ends = [(way, f) for way in (0, 1) for f in (0, 1)]
 
     def shipped(way, f, at):
         source = edges.at[slab_rows(((1 - way) * 2 + f) * patches + at), :]
@@ -449,32 +454,47 @@
                 here = slab_rows((g if g < 2 else g - frames) * patches + at)
                 edges[here, :width] = d_keys.astype(bf16)
                 edges[here, width:] = d_values.astype(bf16)
-        for way, f in ends:
-            shipped(way, f, at).start()
+        for way in (0, 1):
+
+            @pl.when(halo.leaves[way])
+            def _(way=way):
+                for f in (0, 1):
+                    shipped(way, f, at).start()
 
     slabs(patches, step, tick)
     tick()
     g_out[...] = dot(attn[...], d_branch[...], TN).astype(bf16)
     tick.finish()
-    for way, f in ends:
-        base = f * patches if way == 0 else (frames - 2 + f) * patches
-
-        def add(b, _, way=way, f=f, base=base):
-            at = b * SLAB
-            shipped(way, f, at).wait_recv()
-            here = slab_rows(base + at)
-            there = slab_rows((2 * way + f) * patches + at)
-            d_qkv[here, width:] = (d_qkv[here, width:].astype(f32) + arrived[there, :].astype(f32)).astype(bf16)
-            return 0
-
-        lax.fori_loop(0, patches // SLAB, add, 0)
-
-    def close(b, _):
-        for way, f in ends:
-            shipped(way, f, b * SLAB).wait_send()
-        return 0
-
-    lax.fori_loop(0, patches // SLAB, close, 0)
+    slab_count = patches // SLAB
+    for way in (0, 1):
+
+        @pl.when(halo.comes[way])
+        def _(way=way):
+            for f in (0, 1):
+                base = f * patches if way == 0 else (frames - 2 + f) * patches
+
+                def add(b, _, way=way, f=f, base=base):
+                    at = b * SLAB
+                    shipped(way, f, at).wait_recv()
+                    here = slab_rows(base + at)
+                    there = slab_rows((2 * way + f) * patches + at)
+                    d_qkv[here, width:] = (
+                        d_qkv[here, width:].astype(f32) + arrived[there, :].astype(f32)
+                    ).astype(bf16)
+                    return 0
+
+                lax.fori_loop(0, slab_count, add, 0)
+
+    for way in (0, 1):
+
+        @pl.when(halo.leaves[way])
+        def _(way=way):
+            def close(b, _):
+                for f in (0, 1):
+                    shipped(way, f, b * SLAB).wait_send()
+                return 0
+
+            lax.fori_loop(0, slab_count, close, 0)
 
 
 def temporal_rows_kernel(tick, gradient, second, mod, d_qkv, normed, w_qkv, gradient_out, g_qkv, d_mod, d_normed, part, load):
@@ -1480,11 +1500,11 @@
 
     (grad_temp_out, d_qkv_t, d_gate_t), up_parts = temporal_back(
         wide, frames, patches, gradient, qkv_t, near, allowed, spread, heads, mod, full_temp_out, attn_t, branch_t,
-        parts=[Scatter(wide, pieces_in(grad_up))], collective_id=4,
+        parts=[Scatter(wide, pieces_in(grad_up))], collective_id=4, burst=4,
     )
     (gradient, grad_temp_qkv, d_mod_t), down_parts = temporal_rows(
         wide, gradient, second, mod, d_qkv_t, normed_t, full_temp_qkv,
-        parts=[Scatter(wide, pieces_in(blocks(grad_down)))], collective_id=5, pace=2, burst=3,
+        parts=[Scatter(wide, pieces_in(blocks(grad_down)))], collective_id=5, pace=2, burst=4,
     )
     (gradient, grad_cross_q, grad_cross_out, d_gain, d_text_kv), (*temp_qkv_parts, grad_temp_out) = cross_back(
         wide, frames, patches, gradient, first, gain, heads, valid, text_kv,

time: 818 us -> 813 us (level)
  no operation moved by 1% of the time
where the time goes in v4:
time: 813 us; the launch traced here: 808 us
  Pallas kernels  762 us (94%)
  other arithmetic  17 us (2%)
  local copies, waits for them, and re-layouts  16.9 us (2%)
    pallas_call x10, Pallas kernels, fused(): pl.pallas_call(functools.partial(fused_kernel, wide, talks, compute, (len...  762 us
  transfers between devices with their start and end apart: 3, of which 0 were waited for; matrix products, arithmetic and copies ran while one was open for 4% of the time, Pallas kernels for 94%

profile of v4, /device:TPU:0, one launch (start us, length us, event | category | flops | bytes accessed | tf_op | source)
XLA Modules:
  0.0 807.6 jit_solution(5327749611487232089)
XLA Ops:
  1.7 3.0 collective-permute-start
  4.7 5.1 reshape.189
  12.5 51.4 %start.1 = (f32[16,1,648]{2,1,0:T(1,128)}, bf16[72,128]{1,0:T(8,128)(2,1)}, bf16[16,72,3456]{2,1,0:T(8,128)(2,1)}, bf16[16,72,1152]{2,1,0:T(8,128)(2,1)}) custom-call(f32[16,1,648]{2,1,0:T(1,128)} %dot_general.18.refs_0_, bf16[8,2,72,128]{3,2,1,0:T(8,128)(2,1)} %bitcast.109, bf16[72,3456]{1,0:T(8,128)(2,1)} %refs_2_.1, bf16[72,1152]{1,0:T(8,128)(2,1)} %refs_3_.1), custom_call_target="tpu_custom_call" | custom-call | tf_op jit(solution)/shard_map/start/pallas_call | solution.py:1293
  63.9 1.6 collective-permute-start.2
  70.5 86.7 %spatial.1 = (bf16[624,1152]{1,0:T(8,128)(2,1)}, bf16[624,3456]{1,0:T(8,128)(2,1)}, bf16[624,1152]{1,0:T(8,128)(2,1)}, bf16[624,1152]{1,0:T(8,128)(2,1)}, f32[62...) custom-call(bf16[624,1152]{1,0:T(8,128)(2,1)} %bitcast.94, ...), custom_call_target="tpu_custom_call" | custom-call | tf_op jit(solution)/shard_map/spatial/pallas_call | solution.py:1293
  157.2 2.1 copy.40
  161.6 71.0 %cross.1 = (bf16[624,1152]{1,0:T(8,128)(2,1)}, bf16[624,1152]{1,0:T(8,128)(2,1)}, bf16[624,1152]{1,0:T(8,128)(2,1)}, f32[624,1152]{1,0:T(8,128)}, bf16[624,1152]...) custom-call(f32[624,1152]{1,0:T(8,128)} %get-tuple-element.84.refs_0_.r, ...), custom_call_target="tpu_custom_call" | custom-call | tf_op jit(solution)/shard_map/cross/pallas_call | solution.py:1293
  233.4 61.5 %temporal.1 = (bf16[624,1152]{1,0:T(8,128)(2,1)}, bf16[624,1152]{1,0:T(8,128)(2,1)}, f32[624,1152]{1,0:T(8,128)}, bf16[16,72,4608]{2,1,0:T(8,128)(2,1)}) custom-call(bf16[624,3456]{1,0:T(8,128)(2,1)} %get-tuple-element.89.refs_0_.refs_1_, bf16[7,208,2304]{2,1,0:T(8,128)(2,1)} %get-tuple-element.90.refs_1_.refs_2_, ...), custom_call_target="tpu_custom_call" | custom-call | tf_op jit(solution)/shard_map/temporal/pallas_call | solution.py:1293
  294.8 82.6 %mlp.1 = (bf16[624,1152]{1,0:T(8,128)(2,1)}, f32[624,1152]{1,0:T(8,128)}, bf16[1152,4608]{1,0:T(8,128)(2,1)}, bf16[4608,1152]{1,0:T(8,128)(2,1)}, f32[3,1152]{1,0:T(4,128)}) custom-call(f32[624,1152]{1,0:T(8,128)} %get-tuple-element.93.refs_0_, bf16[624,1152]{1,0:T(8,128)(2,1)} %bitcast.106, f32[9,1152]{1,0:T(8,128)} %reshape.190.refs_1_.refs_2_.refs_6_, ...), custom_call_target="tpu_custom_call" | custom-call | tf_op jit(solution)/shard_map/mlp/pallas_call | solution.py:1293
  377.5 89.9 %temporal_back.1 = (bf16[1152,1152]{1,0:T(8,128)(2,1)}, bf16[624,3456]{1,0:T(8,128)(2,1)}, f32[1,1152]{1,0:T(1,128)}, bf16[72,1152]{1,0:T(8,128)(2,1)}, bf16[72,...) custom-call(f32[624,1152]{1,0:T(8,128)} %get-tuple-element.97.refs_0_, ...), custom_call_target="tpu_custom_call" | custom-call | tf_op jit(solution)/shard_map/temporal_back/pallas_call | solution.py:1293
  467.4 94.4 %temporal_rows.1 = (f32[624,1152]{1,0:T(8,128)}, bf16[1152,3456]{1,0:T(8,128)(2,1)}, f32[2,1152]{1,0:T(2,128)}, bf16[96,1152]{1,0:T(8,128)(2,1)}, bf16[96,1152]{1,0:T(8,128)(2,1)}, /*index=5*/bf16[96,1152]{1,0:T(8,128)(2,1)}) custom-call(f32[624,1152]{1,0:T(8,128)} %get-tuple-element.97.refs_0_, f32[624,1152]{1,0:T(8,128)} %get-tuple-element.91.refs_5_.refs_1_, ...), custom_call_target="tpu_custom_call" | custom-call | tf_op jit(solution)/shard_map/temporal_rows/pallas_call | solution.py:1293
  561.9 69.8 %cross_back.1 = (f32[624,1152]{1,0:T(8,128)}, bf16[1152,1152]{1,0:T(8,128)(2,1)}, bf16[1152,1152]{1,0:T(8,128)(2,1)}, f32[1,1152]{1,0:T(1,128)}, f32[128,2304]{1...) custom-call(f32[624,1152]{1,0:T(8,128)} %get-tuple-element.104.refs_, ...), custom_call_target="tpu_custom_call" | custom-call | tf_op jit(solution)/shard_map/cross_back/pallas_call | solution.py:1293
  631.7 1.3 convert_bitcast_fusion
  634.1 93.9 %spatial_back.1 = (bf16[624,1152]{1,0:T(8,128)(2,1)}, bf16[1152,3456]{1,0:T(8,128)(2,1)}, bf16[1152,1152]{1,0:T(8,128)(2,1)}, f32[3,1152]{1,0:T(4,128)}, bf16[2,...) custom-call(f32[624,1152]{1,0:T(8,128)} %get-tuple-element.110.refs_, ...), custom_call_target="tpu_custom_call" | custom-call | tf_op jit(solution)/shard_map/spatial_back/pallas_call | solution.py:1293
  728.1 1.1 concatenate.31
  729.9 60.8 %end.1 = (f32[2,16,1,720]{3,2,1,0:T(1,128)}, bf16[72,1152]{1,0:T(8,128)(2,1)}, bf16[72,1152]{1,0:T(8,128)(2,1)}, bf16[72,1152]{1,0:T(8,128)(2,1)}, bf16[72,1152]{1,0:T(8,128)(2,1)}) custom-call(f32[16,1,720]{2,1,0:T(1,128)} %reshape.208.refs_0_, bf16[16,72,3456]{2,1,0:T(8,128)(2,1)} %bitcast.93, bf16[16,72,1152]{2,1,0:T(8,128)(2,1)} %bitcast.101), custom_call_target="tpu_custom_call" | custom-call | tf_op jit(solution)/shard_map/end/pallas_call | solution.py:1293
  790.8 1.2 reduce.2
  792.8 1.7 convert_element_type.91
  796.3 1.1 maximum_convert_fusion.1
  799.6 1.2 maximum_convert_fusion
  801.5 2.0 multiply_add_fusion
  803.5 1.4 convolution_bitcast_fusion
  804.9 1.4 convolution_bitcast_fusion.1
  806.3 1.1 copy.54
  (110 shorter events, 17.5 us)
Async XLA Ops:
  0.6 10.7 %copy-start = (bf16[1,128,4096]{2,1,0:T(8,128)(2,1)S(1)}, bf16[1,128,4096]{2,1,0:T(8,128)(2,1)}, u32[]{:S(2)}) copy-start(bf16[1,128,4096]{2,1,0:T(8,128)(2,1)} %param.20) | copy-start | bytes 3145732
  1.7 799.8 %collective-permute-start = (bf16[72]{0:T(256)(128)(2,1)S(1)}, bf16[72]{0:T(256)(128)(2,1)S(1)}, u32[]{:S(2)}, u32[]{:S(2)}) collective-permute-start(bf16[72]{0:T(256)(128)(2,1)S(1)} %fusion.27), channel_id=1, source_target_pairs={{0,16},{16,0},{1,17},{17,1},{2,18},{18,2},{3,19},{19,3},{4,20},{20... | collective-permute-start | bytes 440 | tf_op jit(solution)/shard_map/ppermute | solution.py:1441
  10.6 58.8 %copy-start.3 = (bf16[72,2304]{1,0:T(8,128)(2,1)S(1)}, bf16[72,2304]{1,0:T(8,128)(2,1)}, u32[]{:S(2)}) copy-start(bf16[72,2304]{1,0:T(8,128)(2,1)} %refs_11_.1) | copy-start | bytes 995332
  63.9 739.6 %collective-permute-start.2 = (bf16[72,128]{1,0:T(8,128)(2,1)}, bf16[72,128]{1,0:T(8,128)(2,1)S(1)}, u32[]{:S(2)}, u32[]{:S(2)}) collective-permute-start(bf16[72,128]{1,0:T(8,128)(2,1)} %get-tuple-element.83.refs_5_), channel_id=1, source_target_pairs={{0,16},{16,0},{1,17},{17,1},{2,18},{18,2},{3,19},{19,3},{4,20},{20... | collective-permute-start | bytes 55304 | tf_op jit(solution)/shard_map/ppermute | solution.py:1441
  65.5 739.4 %collective-permute-start.1 = (bf16[128,256]{1,0:T(8,128)(2,1)S(1)}, bf16[128,256]{1,0:T(8,128)(2,1)S(1)}, u32[]{:S(2)}, u32[]{:S(2)}) collective-permute-start(bf16[128,256]{1,0:T(8,128)(2,1)S(1)} %fusion.34), channel_id=1, source_target_pairs={{0,16},{16,0},{1,17},{17,1},{2,18},{18,2},{3,19},{19,3},{4,20},{20... | collective-permute-start | bytes 196616 | tf_op jit(solution)/shard_map/ppermute | solution.py:1441
  70.5 90.2 %copy-start.28 = (f32[1152]{0:T(1024)S(1)}, f32[1152]{0:T(1024)}, u32[]{:S(2)}) copy-start(f32[1152]{0:T(1024)} %param.35) | copy-start | bytes 13828
  70.5 90.8 %copy-start.31 = (s32[1,48]{1,0:T(1,128)S(1)}, s32[1,48]{1,0:T(1,128)}, u32[]{:S(2)}) copy-start(s32[1,48]{1,0:T(1,128)} %param.22) | copy-start | bytes 580
  634.1 94.0 %copy-start.26 = (f32[3,1152]{1,0:T(4,128)S(1)}, f32[3,1152]{1,0:T(4,128)}, u32[]{:S(2)}) copy-start(f32[3,1152]{1,0:T(4,128)} %get-tuple-element.122) | copy-start | bytes 41476
  634.1 94.0 %copy-start.27 = (f32[2,1152]{1,0:T(2,128)S(1)}, f32[2,1152]{1,0:T(2,128)}, u32[]{:S(2)}) copy-start(f32[2,1152]{1,0:T(2,128)} %get-tuple-element.120) | copy-start | bytes 27652
  634.1 94.0 %copy-start.29 = (f32[1,1152]{1,0:T(1,128)S(1)}, f32[1,1152]{1,0:T(1,128)}, u32[]{:S(2)}) copy-start(f32[1,1152]{1,0:T(1,128)} %get-tuple-element.121) | copy-start | bytes 13828
  634.1 94.0 %copy-start.30 = (f32[1,1152]{1,0:T(1,128)S(1)}, f32[1,1152]{1,0:T(1,128)}, u32[]{:S(2)}) copy-start(f32[1,1152]{1,0:T(1,128)} %get-tuple-element.123) | copy-start | bytes 13828
  790.7 3.7 copy-start.5
  790.7 4.0 copy-start.20
  790.7 4.8 copy-start.19
  792.0 4.3 copy-start.9
  792.0 4.3 copy-start.10
  792.0 4.3 copy-start.11
  794.7 2.7 copy-start.12
  794.8 2.7 copy-start.13
  794.8 2.7 copy-start.14
  800.7 2.8 copy-start.4
  800.7 2.8 copy-start.25
  801.5 3.4 copy-start.8
  803.5 2.8 copy-start.2
  (11 other events, 22.5 us)
